TPU v7x, 1024 devices: a whole 4x8x16 slice. The times are simulated.
1024 devices in a mesh: seq: 64 (over z, x), mp: 16 (over y, core).
Axes of the slice: x: 4, y: 8, z: 16, core: 2. Of those that a mesh axis runs over, the one named last changes fastest.
Arguments:
- hidden_state: bfloat16 [32768, 4096], P('seq', 'mp'), may hold values from -16 to 16
- router_weight: float32 [32768], P('seq'), may hold values from 0.2 to 1
- norm_gain: float32 [4096], replicated, may hold values from 0.5 to 1.5
- query_weight: bfloat16 [4096, 4096], P(None, 'mp'), may hold values from -1 to 1
- kv_weight: bfloat16 [4096, 2048], P(None, 'mp'), may hold values from -1 to 1
- out_weight: bfloat16 [4096, 4096], P('mp'), may hold values from -0.09375 to 0.09375
- sel_rows: int32 [8192], P('seq'), may hold values from -1 to 511, as said below
- dest_shard: int32 [8192], P('seq'), may hold values from -1 to 63, as said below
- dest_slot: int32 [8192], P('seq'), may hold values from -1 to 63, as said below
Outputs:
- mixed: bfloat16 [32768, 4096], P('seq', 'mp')
Inputs may be any that keep to these rules, and one draw needn't show every extreme that they name: `sel_rows`: within a shard the used entries come first, -1 after them; used rows are distinct and ascending. `dest_shard`: A shard's used entries take consecutive ranks in order, shards in order; the token of rank q goes to shard q mod 64; -1 on unused entries. Some shard uses all 128 entries, so 2 tokens go from it to one shard, and every shard receives exactly 64. `dest_slot`: the slot of the token of rank q is q // 64; -1 on unused entries.
All inputs are finite; a program needn't handle non-finite values.
Results may differ from a plain program's by a relative error of at most 0.0045.
Values may be sent and summed in bfloat16 or wider, within the bound.
No kernel may reach another device: no remote copies, remote signals or barrier semaphores. Data moves between devices by JAX's collectives and lax.ppermute only.
A program may use at most 32 MiB of HBM per device.

v0:
```python
import math

import jax
import jax.numpy as jnp
from jax import lax
from jax.sharding import PartitionSpec as P

HEADS = 32
KV_HEADS = 8
HEAD_DIM = 128
SEL_DEV = 64


rope_base = 500000.0


def rotate(head_vals, positions):
    half_dim = head_vals.shape[-1] // 2
    freqs = rope_base ** (-(jnp.arange(half_dim, dtype=jnp.float32) * 2.0 / head_vals.shape[-1]))
    angles = positions.astype(jnp.float32)[:, None] * freqs[None, :]
    cosine = jnp.cos(angles)[:, None, :]
    sine = jnp.sin(angles)[:, None, :]
    first_half = head_vals[..., :half_dim]
    second_half = head_vals[..., half_dim:]
    return jnp.concatenate(
        [first_half * cosine - second_half * sine, second_half * cosine + first_half * sine],
        axis=-1,
    )


def local(
    hidden_state,
    router_weight,
    norm_gain,
    query_weight,
    kv_weight,
    out_weight,
    sel_rows,
    dest_shard,
    dest_slot,
):
    seq_count = lax.axis_size("seq")
    seq_index = lax.axis_index("seq")
    model_index = lax.axis_index("mp")
    tok_count, local_width = hidden_state.shape
    slot_count = sel_rows.shape[0]
    pair_slots = slot_count // seq_count
    sel_count = SEL_DEV
    head_dim = HEAD_DIM
    local_heads = query_weight.shape[1] // head_dim
    group_size = HEADS // KV_HEADS
    kv_local = max(1, local_heads // group_size)
    per_group = local_heads // kv_local
    usable = sel_rows >= 0
    entry_index = jnp.arange(slot_count, dtype=jnp.int32)
    pair_index = entry_index // seq_count
    target = jnp.where(usable, dest_shard, seq_count)
    safe_rows = jnp.where(usable, sel_rows, 0)
    picked = hidden_state[safe_rows]
    send_rows = (
        jnp.zeros((seq_count, pair_slots, local_width), jnp.bfloat16)
        .at[target, pair_index]
        .set(picked, mode="drop")
    )
    send_slot = (
        jnp.full((seq_count, pair_slots), -1, jnp.int32)
        .at[target, pair_index]
        .set(dest_slot, mode="drop")
    )
    send_pos = (
        jnp.zeros((seq_count, pair_slots), jnp.int32)
        .at[target, pair_index]
        .set(seq_index * tok_count + safe_rows, mode="drop")
    )
    got_rows, got_slot, got_pos = (
        lax.all_to_all(send_rows, "seq", split_axis=0, concat_axis=0, tiled=True),
        lax.all_to_all(send_slot, "seq", split_axis=0, concat_axis=0, tiled=True),
        lax.all_to_all(send_pos, "seq", split_axis=0, concat_axis=0, tiled=True),
    )
    flat_slot = got_slot.reshape(-1)
    landing = jnp.where(flat_slot >= 0, flat_slot, sel_count)
    local_rows = (
        jnp.zeros((sel_count, local_width), jnp.bfloat16)
        .at[landing]
        .set(got_rows.reshape(-1, local_width), mode="drop")
    )
    positions = jnp.zeros((sel_count,), jnp.int32).at[landing].set(got_pos.reshape(-1), mode="drop")
    full_rows = lax.all_gather(local_rows, "mp", axis=1, tiled=True)
    row_float = full_rows.astype(jnp.float32)
    inverse = lax.rsqrt(jnp.mean(row_float * row_float, axis=1, keepdims=True) + 1e-05)
    normed = (row_float * inverse * norm_gain[None, :]).astype(jnp.bfloat16)
    queries = jnp.dot(normed, query_weight, preferred_element_type=jnp.float32).reshape(
        sel_count, local_heads, head_dim
    )
    queries = rotate(queries, positions).astype(jnp.bfloat16)
    kv_part = jnp.dot(normed, kv_weight, preferred_element_type=jnp.float32)
    part_heads = kv_part.shape[1] // head_dim
    kv_split = kv_part.reshape(sel_count, part_heads, head_dim)
    head_ids = model_index * part_heads + jnp.arange(part_heads, dtype=jnp.int32)
    turned = rotate(kv_split, positions)
    kv_split = jnp.where((head_ids < KV_HEADS)[None, :, None], turned, kv_split)
    kv_columns_here = kv_split.astype(jnp.bfloat16).reshape(sel_count, part_heads * head_dim)
    kv_all = lax.all_gather(kv_columns_here, "mp", axis=1, tiled=True)
    first_head = model_index * local_heads // group_size
    key_block = lax.dynamic_slice_in_dim(kv_all, first_head * head_dim, kv_local * head_dim, 1)
    value_block = lax.dynamic_slice_in_dim(
        kv_all, (KV_HEADS + first_head) * head_dim, kv_local * head_dim, 1
    )
    grouped = queries.transpose(1, 0, 2).reshape(kv_local, per_group * sel_count, head_dim)
    query_rank = jnp.tile(jnp.arange(sel_count, dtype=jnp.int32) * seq_count + seq_index, per_group)
    score_scale = 1.0 / math.sqrt(head_dim)
    max_now = jnp.full((kv_local, per_group * sel_count), -1e30, jnp.float32)
    key_piece = lax.all_gather(key_block, "seq", axis=0, tiled=True)
    value_piece = lax.all_gather(value_block, "seq", axis=0, tiled=True)
    piece_rows = key_piece.shape[0]
    key_heads = key_piece.reshape(piece_rows, kv_local, head_dim)
    value_heads = value_piece.reshape(piece_rows, kv_local, head_dim)
    whole_row = jnp.arange(piece_rows, dtype=jnp.int32)
    key_rank = whole_row % sel_count * seq_count + whole_row // sel_count
    allowed = (key_rank[None, :] <= query_rank[:, None])[None]
    scores = (
        jnp.einsum("gqd,ngd->gqn", grouped, key_heads, preferred_element_type=jnp.float32)
        * score_scale
    )
    masked = jnp.where(allowed, scores, -1e30)
    new_max = jnp.maximum(max_now, jnp.max(masked, axis=2))
    weights = jnp.where(allowed, jnp.exp(masked - new_max[..., None]), 0.0)
    acc_next = jnp.einsum(
        "gqn,ngd->gqd",
        weights.astype(jnp.bfloat16),
        value_heads,
        preferred_element_type=jnp.float32,
    )
    total_next = jnp.sum(weights, axis=2)
    attended = (acc_next / total_next[..., None]).reshape(local_heads, sel_count, head_dim)
    attended = (
        attended.transpose(1, 0, 2).reshape(sel_count, local_heads * head_dim).astype(jnp.bfloat16)
    )
    clip_target = jnp.minimum(target, seq_count - 1)
    slot_used = (got_slot >= 0)[..., None]
    slot_safe = jnp.maximum(got_slot, 0)
    back_heads = jnp.where(slot_used, attended[slot_safe], jnp.zeros((), jnp.bfloat16))
    returned = lax.all_to_all(back_heads, "seq", split_axis=0, concat_axis=0, tiled=True)
    own_heads = returned[clip_target, pair_index]
    summed = lax.psum_scatter(
        lax.dot_general(
            out_weight, own_heads, (((0,), (1,)), ((), ())), preferred_element_type=jnp.float32
        ).astype(jnp.bfloat16),
        "mp",
        scatter_dimension=0,
        tiled=True,
    ).astype(jnp.float32)
    own_update = summed.T.astype(jnp.bfloat16)
    fresh = (
        picked.astype(jnp.float32)
        + router_weight[safe_rows][:, None] * own_update.astype(jnp.float32)
    ).astype(jnp.bfloat16)
    write_at = jnp.where(usable, sel_rows, tok_count)
    return hidden_state.at[write_at].set(fresh, mode="drop")


def solution(mesh):
    in_specs = (
        P("seq", "mp"),
        P("seq"),
        P(),
        P(None, "mp"),
        P(None, "mp"),
        P("mp", None),
        P("seq"),
        P("seq"),
        P("seq"),
    )
    out_specs = P("seq", "mp")
    return jax.shard_map(local, mesh=mesh, in_specs=in_specs, out_specs=out_specs, check_vma=False)
```

profile of v0, /device:TPU:1, one launch (start us, length us, event | category | flops | bytes accessed | tf_op | source)
XLA Modules:
  0.0 524.0 jit_solution(16168404478402191450)
XLA Ops:
  6.5 1.1 copy.50
  7.6 0.7 fusion.48
  8.4 11.0 %scatter_fusion = s32[64,2]{0,1:T(2,128)S(1)} fusion(s32[64,2]{0,1:T(2,128)S(1)} %broadcast_in_dim.93, s32[128]{0:T(128)S(1)} %get-tuple-element.16, s32[128]{0:T(128)} %param.17), kind=kCustom, calls=%fused_computation.4 | custom fusion | bytes 2560 | tf_op jit(solution)/shard_map/scatter | solution.py:68
  19.4 0.7 copy.29
  20.0 22.8 %all-to-all-start = ((s32[64,1,2]{2,1,0:T(1,128)}), s32[64,1,2]{2,1,0:T(1,128)S(1)}, u32[]{:S(2)}, u32[]{:S(2)}) async-start(s32[64,1,2]{2,1,0:T(1,128)} %copy.29), calls=%async_computation | async-start | bytes 65536 | tf_op jit(solution)/shard_map/all_to_all | solution.py:77
  43.6 6.5 %scatter_fusion.2 = s32[64,2]{0,1:T(2,128)S(1)} fusion(s32[64,2]{0,1:T(2,128)S(1)} %broadcast.295, s32[128]{0:T(128)S(1)} %get-tuple-element.16, s32[128]{0:T(128)S(1)} %get-tuple-element.19), kind=kCustom, calls=%fused_computation.7 | custom fusion | bytes 2560 | tf_op jit(solution)/shard_map/scatter | solution.py:73
  50.0 0.7 copy.33
  50.7 5.7 %all-to-all-done = s32[64,1,2]{2,1,0:T(1,128)S(1)} async-done(((s32[64,1,2]{2,1,0:T(1,128)}), s32[64,1,2]{2,1,0:T(1,128)S(1)}, u32[]{:S(2)}, u32[]{:S(2)}) %all-to-all-start) | async-done | bytes 544 | tf_op jit(solution)/shard_map/all_to_all | solution.py:77
  56.4 8.8 %all-to-all-start.2 = ((s32[64,1,2]{2,1,0:T(1,128)}), s32[64,1,2]{2,1,0:T(1,128)S(1)}, u32[]{:S(2)}, u32[]{:S(2)}) async-start(s32[64,1,2]{2,1,0:T(1,128)} %copy.33), calls=%async_computation.2 | async-start | bytes 65536 | tf_op jit(solution)/shard_map/all_to_all | solution.py:78
  65.3 0.8 gather_fusion
  66.8 14.2 %scatter_fusion.1 = bf16[64,2,256]{2,1,0:T(2,128)(2,1)} fusion(bf16[64,2,256]{2,1,0:T(2,128)(2,1)} %broadcast_in_dim.99, s32[128]{0:T(128)S(1)} %get-tuple-element.16, bf16[128,256]{1,0:T(8,128)(2,1)S(1)} %gather_fusion), kind=kCustom, calls=%fused_computation.5 | custom fusion | bytes 197632 | tf_op jit(solution)/shard_map/scatter | solution.py:63
  81.1 14.5 %all-to-all-start.1 = ((bf16[64,2,256]{2,1,0:T(2,128)(2,1)}), bf16[64,2,256]{2,1,0:T(2,128)(2,1)S(1)}, u32[]{:S(2)}, u32[]{:S(2)}) async-start(bf16[64,2,256]{2,1,0:T(2,128)(2,1)} %scatter_fusion.1), calls=%async_computation.1 | async-start | bytes 131072 | tf_op jit(solution)/shard_map/all_to_all | solution.py:76
  96.1 0.8 maximum_reduce_fusion
  97.9 1.0 scatter_custom_fusion.4
  98.9 10.7 %all-to-all-done.1 = bf16[64,2,256]{2,1,0:T(2,128)(2,1)S(1)} async-done(((bf16[64,2,256]{2,1,0:T(2,128)(2,1)}), bf16[64,2,256]{2,1,0:T(2,128)(2,1)S(1)}, u32[]{:S(2)}, u32[]{:S(2)}) %all-to-all-start.1) | async-done | bytes 65568 | tf_op jit(solution)/shard_map/all_to_all | solution.py:76
  109.6 1.0 scatter_custom_fusion.2
  110.7 22.2 %all_gather.12 = bf16[64,4096]{1,0:T(8,128)(2,1)S(1)} all-gather(bf16[64,256]{1,0:T(8,128)(2,1)S(1)} %scatter_custom_fusion.2), channel_id=1, replica_groups=mesh['seq'=64,'mp'=16] {'mp'}, dimensions={1}, use_global_device_ids=true | all-gather | bytes 557056 | tf_op jit(solution)/shard_map/all_gather | solution.py:88
  133.1 1.6 fusion.13
  135.0 15.6 %all_gather.13 = bf16[64,2048]{1,0:T(8,128)(2,1)S(1)} all-gather(bf16[64,128]{1,0:T(8,128)(2,1)S(1)} %fusion.29), channel_id=1, replica_groups=mesh['seq'=64,'mp'=16] {'mp'}, dimensions={1}, use_global_device_ids=true | all-gather | bytes 278528 | tf_op jit(solution)/shard_map/all_gather | solution.py:103
  152.7 2.1 fusion.15
  155.1 119.2 %all-gather.3.cloned.1.call-done = bf16[4096,128]{1,0:T(8,128)(2,1)} async-done(((bf16[64,128]{1,0:T(8,128)(2,1)}), bf16[4096,128]{1,0:T(8,128)(2,1)}) %all-gather.3.cloned.1.call-update) | async-done | bytes 1048592 | tf_op jit(solution)/shard_map/all_gather | solution.py:113
  274.3 1.8 fusion.54
  276.1 1.3 copy-done.2
  278.0 141.8 %all-gather.5.cloned.1.call-done = bf16[4096,128]{1,0:T(8,128)(2,1)} async-done(((bf16[64,128]{1,0:T(8,128)(2,1)}), bf16[4096,128]{1,0:T(8,128)(2,1)}) %all-gather.5.cloned.1.call-update) | async-done | bytes 1048592 | tf_op jit(solution)/shard_map/all_gather | solution.py:114
  419.8 2.4 fusion.4
  422.2 0.8 gather_fusion.2
  423.2 22.9 %all_to_all.28 = bf16[64,2,256]{2,1,0:T(2,128)(2,1)S(1)} all-to-all(bf16[64,2,256]{2,1,0:T(2,128)(2,1)S(1)} %broadcast_select_fusion), channel_id=1, replica_groups=mesh['seq'=64,'mp'=16] {'seq'}, dimensions={0} | all-to-all | bytes 131072 | tf_op jit(solution)/shard_map/all_to_all | solution.py:143
  446.1 1.1 gather_fusion.3
  447.2 1.4 fusion.1
  448.7 1.3 gather_fusion.1
  450.0 64.5 %reduce-scatter.2.cloned.1.call-done = bf16[256,128]{0,1:T(8,128)(2,1)} async-done(((bf16[4096,128]{0,1:T(8,128)(2,1)}), bf16[256,128]{0,1:T(8,128)(2,1)}) %reduce-scatter.2.cloned.1.call-update) | async-done | bytes 65552 | tf_op jit(solution)/shard_map/reduce_scatter | solution.py:145
  514.4 3.1 scatter_custom_fusion.5
  (53 shorter events, 6.5 us)
Async XLA Ops:
  6.5 440.7 %copy-start = (bf16[256,4096]{1,0:T(8,128)(2,1)S(1)}, bf16[256,4096]{1,0:T(8,128)(2,1)}, u32[]{:S(2)}) copy-start(bf16[256,4096]{1,0:T(8,128)(2,1)} %param.14) | copy-start | bytes 6291460
  7.6 73.4 %copy-start.3 = (bf16[512,256]{1,0:T(8,128)(2,1)}, bf16[512,256]{1,0:T(8,128)(2,1)S(1)}, u32[]{:S(2)}) copy-start(bf16[512,256]{1,0:T(8,128)(2,1)S(1)} %copy.50) | copy-start | bytes 786436
  20.0 36.4 %all-to-all-start = ((s32[64,1,2]{2,1,0:T(1,128)}), s32[64,1,2]{2,1,0:T(1,128)S(1)}, u32[]{:S(2)}, u32[]{:S(2)}) async-start(s32[64,1,2]{2,1,0:T(1,128)} %copy.29), calls=%async_computation | async-start | bytes 65536 | tf_op jit(solution)/shard_map/all_to_all | solution.py:77
  43.5 89.5 %copy-start.4 = (f32[4096]{0:T(1024)S(1)}, f32[4096]{0:T(1024)}, u32[]{:S(2)}) copy-start(f32[4096]{0:T(1024)} %param.11) | copy-start | bytes 49156
  56.4 24.6 %all-to-all-start.2 = ((s32[64,1,2]{2,1,0:T(1,128)}), s32[64,1,2]{2,1,0:T(1,128)S(1)}, u32[]{:S(2)}, u32[]{:S(2)}) async-start(s32[64,1,2]{2,1,0:T(1,128)} %copy.33), calls=%async_computation.2 | async-start | bytes 65536 | tf_op jit(solution)/shard_map/all_to_all | solution.py:78
  81.1 28.6 %all-to-all-start.1 = ((bf16[64,2,256]{2,1,0:T(2,128)(2,1)}), bf16[64,2,256]{2,1,0:T(2,128)(2,1)S(1)}, u32[]{:S(2)}, u32[]{:S(2)}) async-start(bf16[64,2,256]{2,1,0:T(2,128)(2,1)} %scatter_fusion.1), calls=%async_computation.1 | async-start | bytes 131072 | tf_op jit(solution)/shard_map/all_to_all | solution.py:76
  95.5 178.7 %all-gather.3.cloned.1.call-start = ((), (), s32[]{:S(2)}) async-start(), calls=%async_computation.5 | async-start | bytes 1064960 | tf_op jit(solution)/shard_map/all_gather | solution.py:113
  151.2 268.5 %all-gather.5.cloned.1.call-start = ((), (), s32[]{:S(2)}) async-start(), calls=%async_computation.6 | async-start | bytes 1064960 | tf_op jit(solution)/shard_map/all_gather | solution.py:114
  152.0 362.4 %reduce-scatter.2.cloned.1.call-start = ((), (), s32[]{:S(2)}) async-start(), calls=%async_computation.7 | async-start | bytes 1114112 | tf_op jit(solution)/shard_map/reduce_scatter | solution.py:145
  276.0 1.4 copy-start.2
  447.2 1.5 copy-start.1
Sparse Core Ops, SparseCore 0:
  151.3 122.8 all-gather.2
  278.4 141.3 all-gather.4
  448.8 65.5 reduce-scatter.1
where the time goes:
time: 525 us; the launch traced here: 524 us
  waiting for transfers between devices  343 us (65%)
  blocking collectives  60.6 us (12%)
  starting transfers between devices  46.2 us (9%)
  local copies, waits for them, and re-layouts  44.3 us (8%)
  between operations  13.5 us (3%)
  matrix products  9.33 us (2%)
  other arithmetic  7.52 us (1%)
    all_gather x1, waiting for transfers between devices, local(): value_piece = lax.all_gather(value_block, 'seq', axis=0, tiled=True)  142 us
    all_gather x1, waiting for transfers between devices, local(): key_piece = lax.all_gather(key_block, 'seq', axis=0, tiled=True)  119 us
    reduce_scatter x1, waiting for transfers between devices, local(): lax.psum_scatter(lax.dot_general(out_weight, own_heads, (((0,), (1,)), ((...  64.5 us
    all_to_all x1, blocking collectives, local(): lax.all_to_all(back_heads, 'seq', split_axis=0, concat_axis=0, tiled=True)  22.9 us
    all_to_all x1, starting transfers between devices, local(): lax.all_to_all(send_slot, 'seq', split_axis=0, concat_axis=0, tiled=True)  22.8 us
    all_gather x1, blocking collectives, local(): full_rows = lax.all_gather(local_rows, 'mp', axis=1, tiled=True)  22.2 us
    all_gather x1, blocking collectives, local(): kv_all = lax.all_gather(kv_columns_here, 'mp', axis=1, tiled=True)  15.6 us
    all_to_all x1, starting transfers between devices, local(): lax.all_to_all(send_rows, 'seq', split_axis=0, concat_axis=0, tiled=True)  14.5 us
  transfers between devices with their start and end apart: 6, of which 5 were waited for; matrix products, arithmetic and copies ran while one was open for 6% of the time, Pallas kernels for 0%

commit v1 on v0

v1 whole, which is shorter than its diff:
```python
import functools
import math

import jax
import jax.numpy as jnp
from jax import lax
from jax.experimental import pallas as pl
from jax.experimental.pallas import tpu as pltpu
from jax.sharding import Mesh
from jax.sharding import PartitionSpec as P

KV_HEADS = 8
HEAD_DIM = 128
ROPE_BASE = 500000.0
EPS = 1e-05

Z, X, Y, C = 16, 4, 8, 2
SEQ, MP = ("z", "x"), ("y", "c")
N_MP = Y * C
CAP = 128
TOK = 512
WIDTH = 256
EARLY = 112
LATE = CAP - EARLY
STATS = 16
UNUSED = 1e30
LOW, LOWER = -1e30, -2e30
VMEM = 48 * 1024 * 1024

params = pltpu.CompilerParams(vmem_limit_bytes=VMEM)
in_vmem = pl.BlockSpec(memory_space=pltpu.VMEM)
in_smem = pl.BlockSpec(memory_space=pltpu.SMEM)


def shape(dims, dtype=jnp.bfloat16):
    return jax.ShapeDtypeStruct(dims, dtype)


def dot(a, b, contract):
    return lax.dot_general(a, b, (contract, ((), ())), preferred_element_type=jnp.float32)


def one_hot(sel_row):
    rows = lax.broadcasted_iota(jnp.int32, (TOK, CAP), 0)
    return jnp.where(rows == sel_row, 1.0, 0.0)


def pick_kernel(sel_ref, hidden_ref, early_ref, late_ref):
    hot = one_hot(sel_ref[...]).astype(jnp.bfloat16)
    picked = dot(hot, hidden_ref[...], ((0,), (0,))).astype(jnp.bfloat16)
    early_ref[...] = picked[:EARLY]
    for m in range(N_MP):
        late_ref[m] = picked[EARLY:]


def norm_kv_kernel(
    early_ref, late_ref, gain_ref, weight_ref, cos_ref, sin_ref, mark_ref, normed_ref, kv_ref
):
    parts = ((early_ref, 0, EARLY), (late_ref, EARLY, LATE))
    for ref, first, count in parts:
        square = jnp.zeros((count, WIDTH), jnp.float32)
        for m in range(N_MP):
            vals = ref[m].astype(jnp.float32)
            square += vals * vals
        mean = jnp.sum(square, axis=1, keepdims=True) / (N_MP * WIDTH)
        inverse = lax.rsqrt(mean + EPS)
        for m in range(N_MP):
            vals = ref[m].astype(jnp.float32) * inverse * gain_ref[m : m + 1, :]
            normed_ref[m, first : first + count, :] = vals.astype(jnp.bfloat16)
    total = jnp.zeros((CAP, HEAD_DIM), jnp.float32)
    for m in range(N_MP):
        total += dot(normed_ref[m], weight_ref[m * WIDTH : (m + 1) * WIDTH, :], ((1,), (0,)))
    turned = total * cos_ref[...] + pltpu.roll(total, HEAD_DIM // 2, 1) * sin_ref[...]
    kv_ref[...] = (turned + mark_ref[...]).astype(jnp.bfloat16)


def query_kernel(normed_ref, weight_ref, cos_ref, sin_ref, out_ref):
    total = jnp.zeros((CAP, WIDTH), jnp.float32)
    for m in range(N_MP):
        total += dot(normed_ref[m], weight_ref[m * WIDTH : (m + 1) * WIDTH, :], ((1,), (0,)))
    for h in range(WIDTH // HEAD_DIM):
        head = total[:, h * HEAD_DIM : (h + 1) * HEAD_DIM]
        turned = head * cos_ref[...] + pltpu.roll(head, HEAD_DIM // 2, 1) * sin_ref[...]
        turned = turned.astype(jnp.bfloat16)
        for t in range(X):
            out_ref[t, :, h * HEAD_DIM : (h + 1) * HEAD_DIM] = turned


def attend_kernel(place_ref, query_ref, own_ref, other_ref, out_ref, high_ref, sum_ref, acc_ref):
    z, x, c = place_ref[0], place_ref[1], place_ref[2]
    heads = WIDTH // HEAD_DIM
    queries = X * CAP
    scale = math.log2(math.e) / math.sqrt(HEAD_DIM)
    high_ref[...] = jnp.full(high_ref.shape, LOW, jnp.float32)
    sum_ref[...] = jnp.zeros(sum_ref.shape, jnp.float32)
    acc_ref[...] = jnp.zeros(acc_ref.shape, jnp.float32)
    query_order = z * (X * CAP) + lax.broadcasted_iota(jnp.int32, (1, queries), 1)

    def step(pair, carry):
        own = own_ref[pl.ds(2 * pair, 2)].reshape(2 * CAP, HEAD_DIM)
        other = other_ref[pl.ds(2 * pair, 2)].reshape(2 * CAP, HEAD_DIM)
        keys = jnp.where(c == 0, own, other)
        values = jnp.where(c == 0, other, own)
        values_t = values.T
        row = lax.broadcasted_iota(jnp.int32, (2 * CAP, 1), 0)
        shard = (2 * pair + row // CAP) * X + x
        key_order = shard * CAP + row % CAP
        unused = keys[:, 0:1].astype(jnp.float32) > 0.1 * UNUSED
        key_order = jnp.where(unused, 1 << 30, key_order)
        allowed = key_order <= query_order
        for h in range(heads):
            query = query_ref[:, :, h * HEAD_DIM : (h + 1) * HEAD_DIM].reshape(queries, HEAD_DIM)
            scores = dot(keys, query, ((1,), (1,))) * scale
            scores = jnp.where(allowed, scores, LOWER)
            before = high_ref[h]
            high = jnp.maximum(before, jnp.max(scores, axis=0, keepdims=True))
            weights = jnp.exp2(scores - high)
            fade = jnp.exp2(before - high)
            high_ref[h] = high
            sum_ref[h] = sum_ref[h] * fade + jnp.sum(weights, axis=0, keepdims=True)
            acc_ref[h] = acc_ref[h] * fade + dot(
                values_t, weights.astype(jnp.bfloat16), ((1,), (0,))
            )
        return carry

    lax.fori_loop(0, z // 2 + 1, step, 0)
    stat_row = lax.broadcasted_iota(jnp.int32, (STATS, queries), 0)
    stats = jnp.zeros((STATS, queries), jnp.float32)
    for h in range(heads):
        total = sum_ref[h]
        safe = jnp.maximum(total, 1e-30)
        attended = (acc_ref[h] / safe).astype(jnp.bfloat16)
        for t in range(X):
            out_ref[t, h * HEAD_DIM : (h + 1) * HEAD_DIM, :] = attended[:, t * CAP : (t + 1) * CAP]
        left = jnp.where(total > 0.0, high_ref[h] + jnp.log2(safe), LOW)
        for k in range(3):
            piece = left.astype(jnp.bfloat16).astype(jnp.float32)
            stats = jnp.where(stat_row == heads * k + h, piece, stats)
            left = left - piece
    stats = stats.astype(jnp.bfloat16)
    for t in range(X):
        out_ref[t, heads * HEAD_DIM :, :] = stats[:, t * CAP : (t + 1) * CAP]


def project_kernel(parts_ref, weight_ref, out_ref):
    heads = WIDTH // HEAD_DIM
    stats = [parts_ref[t, heads * HEAD_DIM :, :].astype(jnp.float32) for t in range(X)]
    columns = []
    for h in range(heads):
        logs = [s[h : h + 1] + s[heads + h : heads + h + 1] + s[2 * heads + h : 2 * heads + h + 1] for s in stats]
        high = functools.reduce(jnp.maximum, logs)
        shares = [jnp.exp2(v - high) for v in logs]
        total = functools.reduce(jnp.add, shares)
        mixed = jnp.zeros((HEAD_DIM, CAP), jnp.float32)
        for t in range(X):
            part = parts_ref[t, h * HEAD_DIM : (h + 1) * HEAD_DIM, :].astype(jnp.float32)
            mixed += part * shares[t]
        columns.append((mixed / total).T.astype(jnp.bfloat16))
    attended = jnp.concatenate(columns, axis=1)
    for m in range(N_MP):
        block = dot(attended, weight_ref[:, m * WIDTH : (m + 1) * WIDTH], ((1,), (0,)))
        out_ref[m] = block.astype(jnp.bfloat16)


def mix_kernel(sel_ref, router_ref, hidden_ref, parts_ref, out_ref):
    update = jnp.zeros((CAP, WIDTH), jnp.float32)
    for m in range(N_MP):
        update += parts_ref[m].astype(jnp.float32)
    hot = one_hot(sel_ref[...])
    spread = dot(hot.astype(jnp.bfloat16), update.astype(jnp.bfloat16), ((1,), (0,)))
    taken = jnp.max(hot, axis=1, keepdims=True) > 0.0
    eye = lax.broadcasted_iota(jnp.int32, (CAP, CAP), 0) == lax.broadcasted_iota(
        jnp.int32, (CAP, CAP), 1
    )
    for b in range(TOK // CAP):
        rows = slice(b * CAP, (b + 1) * CAP)
        router = jnp.sum(
            jnp.where(eye, router_ref[:, rows], 0.0), axis=1, keepdims=True
        )
        before = hidden_ref[rows, :]
        fresh = before.astype(jnp.float32) + router * spread[rows]
        out_ref[rows, :] = jnp.where(taken[rows], fresh, before.astype(jnp.float32)).astype(
            jnp.bfloat16
        )


def call(kernel, out_shape, count, scratch=(), smem_first=False, flops=0, nbytes=0):
    specs = [in_vmem] * count
    if smem_first:
        specs[0] = in_smem
    many = isinstance(out_shape, (tuple, list))
    return pl.pallas_call(
        kernel,
        out_shape=out_shape,
        in_specs=specs,
        out_specs=[in_vmem] * len(out_shape) if many else in_vmem,
        scratch_shapes=list(scratch),
        compiler_params=params,
        cost_estimate=pl.CostEstimate(flops=flops, bytes_accessed=nbytes, transcendentals=0),
    )


def local(
    hidden_state,
    router_weight,
    norm_gain,
    query_weight,
    kv_weight,
    out_weight,
    sel_rows,
    dest_shard,
    dest_slot,
):
    z, x = lax.axis_index("z"), lax.axis_index("x")
    core = lax.axis_index("c")
    model = lax.axis_index("y") * C + core
    place = jnp.stack([z, x, core]).astype(jnp.int32)
    sel = sel_rows.reshape(1, CAP)

    with jax.named_scope("pick"):
        early, late = call(
            pick_kernel, [shape((EARLY, WIDTH)), shape((N_MP, LATE, WIDTH))], 2
        )(sel, hidden_state)
    with jax.named_scope("gather_features"):
        late_all = lax.all_to_all(late, MP, 0, 0, tiled=True)
        early_all = lax.all_gather(early, MP, axis=0, tiled=False)

    with jax.named_scope("rotation"):
        half = HEAD_DIM // 2
        positions = (z * X + x) * TOK + jnp.maximum(sel_rows, 0)
        freqs = ROPE_BASE ** (-(jnp.arange(half, dtype=jnp.float32) * 2.0 / HEAD_DIM))
        angles = positions.astype(jnp.float32)[:, None] * freqs[None, :]
        cosine, sine = jnp.cos(angles), jnp.sin(angles)
        cos_q = jnp.concatenate([cosine, cosine], axis=1)
        sin_q = jnp.concatenate([-sine, sine], axis=1)
        is_key = model < KV_HEADS
        cos_kv = jnp.where(is_key, cos_q, 1.0)
        sin_kv = jnp.where(is_key, sin_q, 0.0)
        lane = jnp.arange(HEAD_DIM, dtype=jnp.int32)[None, :]
        mark = jnp.where(is_key & (sel_rows < 0)[:, None] & (lane == 0), UNUSED, 0.0)

    with jax.named_scope("keys_values"):
        normed, kv = call(
            norm_kv_kernel,
            [shape((N_MP, CAP, WIDTH)), shape((CAP, HEAD_DIM))],
            7,
            flops=2 * CAP * 4096 * HEAD_DIM,
            nbytes=4 << 20,
        )(early_all, late_all, norm_gain.reshape(N_MP, WIDTH), kv_weight, cos_kv, sin_kv, mark)
        to_heads = [(m, 2 * m if m < KV_HEADS else 2 * (m - KV_HEADS) + 1) for m in range(N_MP)]
        kv = lax.ppermute(kv, MP, to_heads)
    with jax.named_scope("queries"):
        queries = call(
            query_kernel,
            shape((X, CAP, WIDTH)),
            4,
            flops=2 * CAP * 4096 * WIDTH,
            nbytes=4 << 20,
        )(normed, query_weight, cos_q, sin_q)
        queries = lax.all_to_all(queries, "x", 0, 0, tiled=True)
    with jax.named_scope("spread_keys_values"):
        own = lax.all_to_all(jnp.broadcast_to(kv[None], (Z, CAP, HEAD_DIM)), "z", 0, 0, tiled=True)
        other = lax.ppermute(own, "c", [(0, 1), (1, 0)])
    with jax.named_scope("attend"):
        heads = WIDTH // HEAD_DIM
        parts = call(
            attend_kernel,
            shape((X, WIDTH + STATS, CAP)),
            4,
            scratch=(
                pltpu.VMEM((heads, 1, X * CAP), jnp.float32),
                pltpu.VMEM((heads, 1, X * CAP), jnp.float32),
                pltpu.VMEM((heads, HEAD_DIM, X * CAP), jnp.float32),
            ),
            smem_first=True,
            flops=4 * X * CAP * WIDTH * Z * CAP,
            nbytes=2 << 20,
        )(place, queries, own, other)
        parts = lax.all_to_all(parts, "x", 0, 0, tiled=True)
    with jax.named_scope("project"):
        partial = call(
            project_kernel,
            shape((N_MP, CAP, WIDTH)),
            2,
            flops=2 * CAP * WIDTH * 4096,
            nbytes=3 << 20,
        )(parts, out_weight)
        partial = lax.all_to_all(partial, MP, 0, 0, tiled=True)
    with jax.named_scope("mix"):
        return call(mix_kernel, shape((TOK, WIDTH)), 4, nbytes=2 << 20)(
            sel, router_weight.reshape(1, TOK), hidden_state, partial
        )


def solution(mesh):
    fine = Mesh(mesh.devices.reshape(Z, X, Y, C), ("z", "x", "y", "c"))
    in_specs = (
        P(SEQ, MP),
        P(SEQ),
        P(),
        P(None, MP),
        P(None, MP),
        P(MP, None),
        P(SEQ),
        P(SEQ),
        P(SEQ),
    )
    return jax.shard_map(
        local, mesh=fine, in_specs=in_specs, out_specs=P(SEQ, MP), check_vma=False
    )
```

time: 525 us -> 151 us (0.29)
  waiting for transfers between devices: 343 us -> 13 us
  local copies, waits for them, and re-layouts: 44.3 us -> 3.08 us
  blocking collectives: 60.6 us -> 99.7 us
  starting transfers between devices: 46.2 us -> 25.5 us
  between operations: 13.5 us -> 0.14 us
  matrix products: 9.33 us -> 0 us
  Pallas kernels: 0 us -> 6.47 us
    all_gather x2 -> x0, waiting for transfers between devices: 261 us -> none  [the longest x1 142 us: local(): value_piece = lax.all_gather(value_block, 'seq', axis=0, tiled=True)]
    reduce_scatter x1 -> x0, waiting for transfers between devices: 64.5 us -> none  [local(): lax.psum_scatter(lax.dot_general(out_weight, own_heads, (((0,), (1,)), ((...]
    all_to_all x1 -> x3, blocking collectives: 22.9 us -> 80 us  [the longest x1 41.8 us: local(): partial = lax.all_to_all(partial, MP, 0, 0, tiled=True)]
    scatter x5 -> x0, local copies, waits for them, and re-layouts: 33.7 us -> none  [the longest x1 14.2 us: local(): send_rows = jnp.zeros((seq_count, pair_slots, local_width), jnp.bfloat16)...]
    all_to_all x3 -> x2, starting transfers between devices: 46.1 us -> 21.5 us  [the longest x1 17.5 us: local(): late_all = lax.all_to_all(late, MP, 0, 0, tiled=True)]
    all_gather x2 -> x1, blocking collectives: 37.8 us -> 19.8 us  [local(): early_all = lax.all_gather(early, MP, axis=0, tiled=False)]
    all_to_all x3 -> x2, waiting for transfers between devices: 16.4 us -> 5.59 us  [the longest x1 5.58 us: local(): queries = lax.all_to_all(queries, 'x', 0, 0, tiled=True)]
    dot_general x5 -> x0, matrix products: 9.33 us -> none  [the longest x1 2.41 us: local(): jnp.einsum('gqn,ngd->gqd', weights.astype(jnp.bfloat16), value_heads, pre...]
  transfers between devices with their start and end apart: 6 -> 4, of which waited for: 5 -> 2; matrix products, arithmetic and copies ran while one was open for 6% -> 2% of each run, Pallas kernels for 0% -> 1%
where the time goes in v1:
time: 151 us; the launch traced here: 150 us
  blocking collectives  99.7 us (66%)
  starting transfers between devices  25.5 us (17%)
  waiting for transfers between devices  13 us (9%)
  Pallas kernels  6.47 us (4%)
  local copies, waits for them, and re-layouts  3.08 us (2%)
  other arithmetic  2.56 us (2%)
    all_to_all x1, blocking collectives, local(): partial = lax.all_to_all(partial, MP, 0, 0, tiled=True)  41.8 us
    all_to_all x1, blocking collectives, local(): lax.all_to_all(jnp.broadcast_to(kv[None], (Z, CAP, HEAD_DIM)), 'z', 0, 0,...  30.2 us
    all_gather x1, blocking collectives, local(): early_all = lax.all_gather(early, MP, axis=0, tiled=False)  19.8 us
    all_to_all x1, starting transfers between devices, local(): late_all = lax.all_to_all(late, MP, 0, 0, tiled=True)  17.5 us
    all_to_all x1, blocking collectives, local(): parts = lax.all_to_all(parts, 'x', 0, 0, tiled=True)  7.97 us
    ppermute x1, waiting for transfers between devices, local(): kv = lax.ppermute(kv, MP, to_heads)  7.4 us
    all_to_all x1, waiting for transfers between devices, local(): queries = lax.all_to_all(queries, 'x', 0, 0, tiled=True)  5.58 us
    all_to_all x1, starting transfers between devices, local(): queries = lax.all_to_all(queries, 'x', 0, 0, tiled=True)  4.02 us
  transfers between devices with their start and end apart: 4, of which 2 were waited for; matrix products, arithmetic and copies ran while one was open for 2% of the time, Pallas kernels for 1%

profile of v1, /device:TPU:1, one launch (start us, length us, event | category | flops | bytes accessed | tf_op | source)
XLA Modules:
  0.0 150.4 jit_solution(1922246449693905900)
XLA Ops:
  0.0 0.9 copy-done.3
  1.0 0.7 copy-done.7
  1.6 0.9 pick.1
  2.5 17.5 %all-to-all-start = ((bf16[16,16,256]{2,1,0:T(8,128)(2,1)}), bf16[16,16,256]{2,1,0:T(8,128)(2,1)S(1)}, u32[]{:S(2)}, u32[]{:S(2)}) async-start(bf16[16,16,256]{2,1,0:T(8,128)(2,1)} %get-tuple-element.10), calls=%async_computation | async-start | bytes 262144 | tf_op jit(solution)/shard_map/gather_features/all_to_all | solution.py:225
  20.0 0.7 add_convert_fusion
  20.6 0.7 compare_and_fusion
  21.3 19.8 %all-gather = bf16[1792,256]{1,0:T(8,128)(2,1)S(1)} all-gather(bf16[112,256]{1,0:T(8,128)(2,1)S(1)} %get-tuple-element.9), channel_id=2, replica_groups=mesh['z'=16,'x'=4,'y'=8,'c'=2] {'y','c'}, dimensions={0}, use_global_device_ids=true | all-gather | bytes 974848 | tf_op jit(solution)/shard_map/gather_features/all_gather | solution.py:226
  41.1 0.3 fusion
  41.4 0.8 pad_maximum_fusion
  42.2 0.0 copy-done.10
  42.2 0.1 and_select_fusion.mark_ref
  42.3 0.0 all-to-all-done.late_ref
  42.3 0.0 copy-start.2
  42.3 1.3 copy-done.2
  43.6 0.7 keys_values.1
  44.4 2.1 %collective-permute-start = (bf16[128,128]{1,0:T(8,128)(2,1)S(1)}, bf16[128,128]{1,0:T(8,128)(2,1)S(1)}, u32[]{:S(2)}, u32[]{:S(2)}) collective-permute-start(bf16[128,128]{1,0:T(8,128)(2,1)S(1)} %get-tuple-element.12), channel_id=1, source_target_pairs={{0,0},{1,2},{2,4},{3,6},{4,8},{5,10},{6,12},{7,14},{8,1},{9,3},{10... | collective-permute-start | bytes 98312 | tf_op jit(solution)/shard_map/keys_values/ppermute | solution.py:251
  46.5 7.4 %collective-permute-done = bf16[128,128]{1,0:T(8,128)(2,1)S(1)} collective-permute-done((bf16[128,128]{1,0:T(8,128)(2,1)S(1)}, bf16[128,128]{1,0:T(8,128)(2,1)S(1)}, u32[]{:S(2)}, u32[]{:S(2)}) %collective-permute-start) | collective-permute-done | bytes 32800 | tf_op jit(solution)/shard_map/keys_values/ppermute | solution.py:251
  53.9 0.1 broadcast_in_dim.26
  54.0 30.2 %all_to_all.25.own_ref = bf16[16,128,128]{2,1,0:T(8,128)(2,1)S(1)} all-to-all(bf16[16,128,128]{2,1,0:T(8,128)(2,1)S(1)} %broadcast_in_dim.26), channel_id=1, replica_groups=mesh['z'=16,'x'=4,'y'=8,'c'=2] {'z'}, dimensions={0} | all-to-all | bytes 1048576 | tf_op jit(solution)/shard_map/spread_keys_values/all_to_all | solution.py:262
  84.1 1.9 %collective-permute-start.1 = (bf16[16,128,128]{2,1,0:T(8,128)(2,1)S(1)}, bf16[16,128,128]{2,1,0:T(8,128)(2,1)}, u32[]{:S(2)}, u32[]{:S(2)}) collective-permute-start(bf16[16,128,128]{2,1,0:T(8,128)(2,1)S(1)} %all_to_all.25.own_ref), channel_id=1, source_target_pairs={{0,1},{1,0},{2,3},{3,2},{4,5},{5,4},{6,7},{7,6},{8,9},{9,8},{10,11... | collective-permute-start | bytes 1572872 | tf_op jit(solution)/shard_map/spread_keys_values/ppermute | solution.py:263
  86.0 0.0 copy-done
  86.1 1.2 queries.1
  87.3 4.0 %all-to-all-start.1 = ((bf16[4,128,256]{2,1,0:T(8,128)(2,1)}), bf16[4,128,256]{2,1,0:T(8,128)(2,1)S(1)}, u32[]{:S(2)}, u32[]{:S(2)}) async-start(bf16[4,128,256]{2,1,0:T(8,128)(2,1)} %queries.1), calls=%async_computation.1 | async-start | bytes 524288 | tf_op jit(solution)/shard_map/queries/all_to_all | solution.py:260
  91.3 0.1 pad_add_fusion.place_ref
  91.4 5.6 %all-to-all-done.1.query_ref = bf16[4,128,256]{2,1,0:T(8,128)(2,1)S(1)} async-done(((bf16[4,128,256]{2,1,0:T(8,128)(2,1)}), bf16[4,128,256]{2,1,0:T(8,128)(2,1)S(1)}, u32[]{:S(2)}, u32[]{:S(2)}) %all-to-all-start.1) | async-done | bytes 262176 | tf_op jit(solution)/shard_map/queries/all_to_all | solution.py:260
  97.0 0.0 collective-permute-done.1.other_ref
  97.0 2.0 %attend.1 = bf16[4,272,128]{2,1,0:T(8,128)(2,1)S(1)} custom-call(s32[3]{0:T(128)S(1)} %pad_add_fusion.place_ref, bf16[4,128,256]{2,1,0:T(8,128)(2,1)S(1)} %all-to-all-done.1.query_ref, bf16[16,128,128]{2,1,0:T(8,128)(2,1)S(1)} %all_to_all.25.own_ref, bf16[16,128,128]{2,1,0:T(8,128)(2,1)} %collective-permute-done.1.other_ref), custom_call_target="tpu_custom_call" | custom-call | flops 1073741824 | bytes 2097152 | tf_op jit(solution)/shard_map/attend/pallas_call | solution.py:266
  99.0 8.0 %all_to_all.26.parts_ref = bf16[4,272,128]{2,1,0:T(8,128)(2,1)S(1)} all-to-all(bf16[4,272,128]{2,1,0:T(8,128)(2,1)S(1)} %attend.1), channel_id=1, replica_groups=mesh['z'=16,'x'=4,'y'=8,'c'=2] {'x'}, dimensions={0} | all-to-all | bytes 557056 | tf_op jit(solution)/shard_map/attend/all_to_all | solution.py:279
  106.9 0.5 project.1
  107.5 41.8 %all_to_all.27.parts_ref = bf16[16,128,256]{2,1,0:T(8,128)(2,1)S(1)} all-to-all(bf16[16,128,256]{2,1,0:T(8,128)(2,1)S(1)} %project.1), channel_id=1, replica_groups=mesh['z'=16,'x'=4,'y'=8,'c'=2] {'y','c'}, dimensions={0} | all-to-all | bytes 2097152 | tf_op jit(solution)/shard_map/project/all_to_all | solution.py:288
  149.3 0.0 copy-done.9
  149.3 1.1 mix.1
  (17 shorter events, 0.0 us)
Async XLA Ops:
  0.0 0.9 copy-start.3
  1.0 0.7 copy-start.7
  1.6 40.6 %copy-start.10 = (f32[4096]{0:T(1024)S(1)}, f32[4096]{0:T(1024)}, u32[]{:S(2)}) copy-start(f32[4096]{0:T(1024)} %param.11) | copy-start | bytes 49156
  2.5 39.8 %all-to-all-start = ((bf16[16,16,256]{2,1,0:T(8,128)(2,1)}), bf16[16,16,256]{2,1,0:T(8,128)(2,1)S(1)}, u32[]{:S(2)}, u32[]{:S(2)}) async-start(bf16[16,16,256]{2,1,0:T(8,128)(2,1)} %get-tuple-element.10), calls=%async_computation | async-start | bytes 262144 | tf_op jit(solution)/shard_map/gather_features/all_to_all | solution.py:225
  42.2 43.9 %copy-start = (bf16[4096,256]{1,0:T(8,128)(2,1)S(1)}, bf16[4096,256]{1,0:T(8,128)(2,1)}, u32[]{:S(2)}) copy-start(bf16[4096,256]{1,0:T(8,128)(2,1)} %weight_ref.4) | copy-start | bytes 6291460
  42.3 1.4 copy-start.2
  43.6 42.4 %copy-start.5 = (f32[128,128]{1,0:T(8,128)S(1)}, f32[128,128]{1,0:T(8,128)}, u32[]{:S(2)}) copy-start(f32[128,128]{1,0:T(8,128)} %get-tuple-element.15.cos_ref) | copy-start | bytes 196612
  43.6 42.4 %copy-start.6 = (f32[128,128]{1,0:T(8,128)S(1)}, f32[128,128]{1,0:T(8,128)}, u32[]{:S(2)}) copy-start(f32[128,128]{1,0:T(8,128)} %get-tuple-element.21.sin_ref) | copy-start | bytes 196612
  44.4 9.5 %collective-permute-start = (bf16[128,128]{1,0:T(8,128)(2,1)S(1)}, bf16[128,128]{1,0:T(8,128)(2,1)S(1)}, u32[]{:S(2)}, u32[]{:S(2)}) collective-permute-start(bf16[128,128]{1,0:T(8,128)(2,1)S(1)} %get-tuple-element.12), channel_id=1, source_target_pairs={{0,0},{1,2},{2,4},{3,6},{4,8},{5,10},{6,12},{7,14},{8,1},{9,3},{10... | collective-permute-start | bytes 98312 | tf_op jit(solution)/shard_map/keys_values/ppermute | solution.py:251
  84.1 12.9 %collective-permute-start.1 = (bf16[16,128,128]{2,1,0:T(8,128)(2,1)S(1)}, bf16[16,128,128]{2,1,0:T(8,128)(2,1)}, u32[]{:S(2)}, u32[]{:S(2)}) collective-permute-start(bf16[16,128,128]{2,1,0:T(8,128)(2,1)S(1)} %all_to_all.25.own_ref), channel_id=1, source_target_pairs={{0,1},{1,0},{2,3},{3,2},{4,5},{5,4},{6,7},{7,6},{8,9},{9,8},{10,11... | collective-permute-start | bytes 1572872 | tf_op jit(solution)/shard_map/spread_keys_values/ppermute | solution.py:263
  87.3 9.7 %all-to-all-start.1 = ((bf16[4,128,256]{2,1,0:T(8,128)(2,1)}), bf16[4,128,256]{2,1,0:T(8,128)(2,1)S(1)}, u32[]{:S(2)}, u32[]{:S(2)}) async-start(bf16[4,128,256]{2,1,0:T(8,128)(2,1)} %queries.1), calls=%async_computation.1 | async-start | bytes 524288 | tf_op jit(solution)/shard_map/queries/all_to_all | solution.py:260
  91.4 15.6 %copy-start.1 = (bf16[256,4096]{1,0:T(8,128)(2,1)S(1)}, bf16[256,4096]{1,0:T(8,128)(2,1)}, u32[]{:S(2)}) copy-start(bf16[256,4096]{1,0:T(8,128)(2,1)} %weight_ref.5) | copy-start | bytes 6291460
  106.9 42.4 %copy-start.4 = (bf16[512,256]{1,0:T(8,128)(2,1)S(1)}, bf16[512,256]{1,0:T(8,128)(2,1)}, u32[]{:S(2)}) copy-start(bf16[512,256]{1,0:T(8,128)(2,1)} %hidden_ref.3) | copy-start | bytes 786436
  106.9 42.4 %copy-start.8 = (s32[128]{0:T(128)S(1)}, s32[128]{0:T(128)}, u32[]{:S(2)}) copy-start(s32[128]{0:T(128)} %param.15) | copy-start | bytes 1540
  106.9 42.4 %copy-start.9 = (f32[512]{0:T(512)S(1)}, f32[512]{0:T(512)}, u32[]{:S(2)}) copy-start(f32[512]{0:T(512)} %param.10) | copy-start | bytes 6148

commit v2 on v1

v2 whole, which is shorter than its diff:
```python
import functools
import math

import jax
import jax.numpy as jnp
from jax import lax
from jax.experimental import pallas as pl
from jax.experimental.pallas import tpu as pltpu
from jax.sharding import Mesh
from jax.sharding import PartitionSpec as P

HEAD_DIM = 128
HALF_DIM = HEAD_DIM // 2
ROPE_BASE = 500000.0
EPS = 1e-05

Z, X, Y, C = 16, 4, 8, 2
AXES = ("z", "x", "y", "c")
SEQ, MP = ("z", "x"), ("y", "c")
N_MP = Y * C
CAP = 128
HALF = CAP // C
TOK = 512
WIDTH = 256
HEADS = WIDTH // HEAD_DIM
ROWS = C * HEADS * HALF
STATS = 16
UNUSED = 1e30
CHAINS = 2
LOW, LOWER = -1e30, -2e30
VMEM = 48 * 1024 * 1024
WHOLE = 62 * 1024 * 1024

in_vmem = pl.BlockSpec(memory_space=pltpu.VMEM)
in_smem = pl.BlockSpec(memory_space=pltpu.SMEM)
in_hbm = pl.BlockSpec(memory_space=pltpu.HBM)


def shape(dims, dtype=jnp.bfloat16):
    return jax.ShapeDtypeStruct(dims, dtype)


def dot(a, b, contract):
    return lax.dot_general(a, b, (contract, ((), ())), preferred_element_type=jnp.float32)


def one_hot(sel_row):
    rows = lax.broadcasted_iota(jnp.int32, (TOK, CAP), 0)
    return jnp.where(rows == sel_row, 1.0, 0.0)


def turn(head, cosine, sine):
    return head * cosine + pltpu.roll(head, HALF_DIM, 1) * sine


def pick_kernel(sel_ref, hidden_ref, out_ref):
    hot = one_hot(sel_ref[...]).astype(jnp.bfloat16)
    picked = dot(hot, hidden_ref[...], ((0,), (0,))).astype(jnp.bfloat16)
    for m in range(N_MP):
        half = m % C
        out_ref[m] = picked[half * HALF : (half + 1) * HALF]


def touch_kernel(weight_ref, after_ref, out_ref):
    del after_ref
    out_ref[...] = weight_ref[:16, :]


def norm_kv_kernel(
    core_ref,
    own_ref,
    other_ref,
    gain_ref,
    cos_ref,
    sin_ref,
    mark_ref,
    weight_ref,
    after_ref,
    normed_ref,
    kv_ref,
):
    del after_ref
    core = core_ref[0]
    for ref, half in ((own_ref, core), (other_ref, 1 - core)):
        square = jnp.zeros((HALF, WIDTH), jnp.float32)
        for m in range(N_MP):
            vals = ref[m].astype(jnp.float32)
            square += vals * vals
        mean = jnp.sum(square, axis=1, keepdims=True) / (N_MP * WIDTH)
        inverse = lax.rsqrt(mean + EPS)
        first = pl.multiple_of(half * HALF, HALF)
        for m in range(N_MP):
            vals = ref[m].astype(jnp.float32) * inverse * gain_ref[m : m + 1, :]
            normed_ref[pl.ds(first, HALF), m * WIDTH : (m + 1) * WIDTH] = vals.astype(jnp.bfloat16)
    total = dot(normed_ref[...], weight_ref[...], ((1,), (0,)))
    kv_ref[...] = (turn(total, cos_ref[...], sin_ref[...]) + mark_ref[...]).astype(jnp.bfloat16)


def query_kernel(core_ref, normed_ref, cos_ref, sin_ref, weight_ref, mine_ref, theirs_ref):
    core = core_ref[0]
    total = dot(normed_ref[...], weight_ref[...], ((1,), (0,)))
    for h in range(HEADS):
        head = total[:, h * HEAD_DIM : (h + 1) * HEAD_DIM]
        turned = turn(head, cos_ref[...], sin_ref[...]).astype(jnp.bfloat16)
        lower, upper = turned[:HALF], turned[HALF:]
        rows = slice(h * HALF, (h + 1) * HALF)
        mine_ref[rows, :] = jnp.where(core == 0, lower, upper)
        theirs_ref[rows, :] = jnp.where(core == 0, upper, lower)


def attend_kernel(place_ref, query_ref, own_ref, other_ref, out_ref, high_ref, sum_ref, acc_ref):
    z, x, c = place_ref[0], place_ref[1], place_ref[2]
    columns = X * ROWS
    scale = math.log2(math.e) / math.sqrt(HEAD_DIM)
    high_ref[...] = jnp.full(high_ref.shape, LOW, jnp.float32)
    sum_ref[...] = jnp.zeros(sum_ref.shape, jnp.float32)
    acc_ref[...] = jnp.zeros(acc_ref.shape, jnp.float32)
    column = lax.broadcasted_iota(jnp.int32, (1, columns), 1)
    query_shard = z * X + column // ROWS
    query_order = query_shard * CAP + c * HALF + column % HALF

    def step(pair, carry):
        own = own_ref[pl.ds(2 * pair, 2)].reshape(2 * CAP, HEAD_DIM)
        other = other_ref[pl.ds(2 * pair, 2)].reshape(2 * CAP, HEAD_DIM)
        keys = jnp.where(c == 0, own, other)
        values_t = jnp.where(c == 0, other, own).T
        row = lax.broadcasted_iota(jnp.int32, (2 * CAP, 1), 0)
        shard = (2 * pair + row // CAP) * X + x
        key_order = shard * CAP + row % CAP
        unused = keys[:, 0:1].astype(jnp.float32) > 0.1 * UNUSED
        key_order = jnp.where(unused, 1 << 30, key_order)
        for part in range(CHAINS):
            span = slice(part * columns // CHAINS, (part + 1) * columns // CHAINS)
            scores = dot(keys, query_ref[span, :], ((1,), (1,))) * scale
            scores = jnp.where(key_order <= query_order[:, span], scores, LOWER)
            before = high_ref[:, span]
            high = jnp.maximum(before, jnp.max(scores, axis=0, keepdims=True))
            weights = jnp.exp2(scores - high)
            fade = jnp.exp2(before - high)
            high_ref[:, span] = high
            sum_ref[:, span] = sum_ref[:, span] * fade + jnp.sum(weights, axis=0, keepdims=True)
            acc_ref[:, span] = acc_ref[:, span] * fade + dot(
                values_t, weights.astype(jnp.bfloat16), ((1,), (0,))
            )
        return carry

    lax.fori_loop(0, z // 2 + 1, step, 0)
    total = sum_ref[...]
    safe = jnp.maximum(total, 1e-30)
    attended = (acc_ref[...] / safe).astype(jnp.bfloat16)
    stat_row = lax.broadcasted_iota(jnp.int32, (STATS, columns), 0)
    stats = jnp.zeros((STATS, columns), jnp.float32)
    left = jnp.where(total > 0.0, high_ref[...] + jnp.log2(safe), LOW)
    for k in range(3):
        piece = left.astype(jnp.bfloat16).astype(jnp.float32)
        stats = jnp.where(stat_row == k, piece, stats)
        left = left - piece
    stats = stats.astype(jnp.bfloat16)
    for home in range(X):
        span = slice(home * ROWS, (home + 1) * ROWS)
        out_ref[home, :HEAD_DIM, :] = attended[:, span]
        out_ref[home, HEAD_DIM:, :] = stats[:, span]


def project_kernel(parts_ref, other_ref, own_ref, out_ref, own_buf, arrived):
    copy = pltpu.make_async_copy(own_ref, own_buf, arrived)
    copy.start()
    logs = []
    for t in range(X):
        stats = parts_ref[t, HEAD_DIM:, :].astype(jnp.float32)
        logs.append(stats[0:1] + stats[1:2] + stats[2:3])
    high = functools.reduce(jnp.maximum, logs)
    shares = [jnp.exp2(v - high) for v in logs]
    total = functools.reduce(jnp.add, shares)
    merged = jnp.zeros((HEAD_DIM, ROWS), jnp.float32)
    for t in range(X):
        part = parts_ref[t, :HEAD_DIM, :].astype(jnp.float32)
        merged += part * (shares[t] / total)
    merged = merged.T.astype(jnp.bfloat16)
    attended = jnp.concatenate(
        [merged[j * HALF : (j + 1) * HALF] for j in range(C * HEADS)], axis=1
    )
    copy.wait()
    for m in range(N_MP):
        columns = slice(m * WIDTH, (m + 1) * WIDTH)
        block = dot(attended[:, :WIDTH], own_buf[:, columns], ((1,), (0,)))
        block += dot(attended[:, WIDTH:], other_ref[:, columns], ((1,), (0,)))
        out_ref[m] = block.astype(jnp.bfloat16)


def mix_kernel(sel_ref, router_ref, hidden_ref, parts_ref, out_ref):
    halves = []
    for half in range(C):
        update = jnp.zeros((HALF, WIDTH), jnp.float32)
        for y in range(Y):
            update += parts_ref[y * C + half].astype(jnp.float32)
        halves.append(update.astype(jnp.bfloat16))
    hot = one_hot(sel_ref[...])
    spread = dot(hot.astype(jnp.bfloat16), jnp.concatenate(halves, axis=0), ((1,), (0,)))
    taken = jnp.max(hot, axis=1, keepdims=True) > 0.0
    eye = lax.broadcasted_iota(jnp.int32, (CAP, CAP), 0) == lax.broadcasted_iota(
        jnp.int32, (CAP, CAP), 1
    )
    for b in range(TOK // CAP):
        rows = slice(b * CAP, (b + 1) * CAP)
        router = jnp.sum(jnp.where(eye, router_ref[:, rows], 0.0), axis=1, keepdims=True)
        before = hidden_ref[rows, :].astype(jnp.float32)
        fresh = before + router * spread[rows]
        out_ref[rows, :] = jnp.where(taken[rows], fresh, before).astype(jnp.bfloat16)


def call(kernel, out_shape, count, scratch=(), smem_first=False, loose=0, flops=0, nbytes=0, vmem=VMEM):
    specs = [in_vmem] * (count - loose) + [in_hbm] * loose
    if smem_first:
        specs[0] = in_smem
    many = isinstance(out_shape, (tuple, list))
    return pl.pallas_call(
        kernel,
        out_shape=out_shape,
        in_specs=specs,
        out_specs=[in_vmem] * len(out_shape) if many else in_vmem,
        scratch_shapes=list(scratch),
        compiler_params=pltpu.CompilerParams(vmem_limit_bytes=vmem),
        cost_estimate=pl.CostEstimate(flops=flops, bytes_accessed=nbytes, transcendentals=0),
    )


def local(
    hidden_state,
    router_weight,
    norm_gain,
    query_weight,
    kv_weight,
    out_weight,
    sel_rows,
    dest_shard,
    dest_slot,
):
    z, x = lax.axis_index("z"), lax.axis_index("x")
    y, core = lax.axis_index("y"), lax.axis_index("c")
    is_key = y < Y // 2
    place = jnp.stack([z, x, core]).astype(jnp.int32)
    core_at = core.astype(jnp.int32)[None]
    sel = sel_rows.reshape(1, CAP)
    swap = [(0, 1), (1, 0)]

    with jax.named_scope("pick"):
        picked = call(pick_kernel, shape((N_MP, HALF, WIDTH)), 2, vmem=WHOLE)(sel, hidden_state)
    with jax.named_scope("gather_features"):
        own_rows = lax.all_to_all(picked, MP, 0, 0, tiled=True)
        other_rows = lax.ppermute(own_rows, "c", swap)

    with jax.named_scope("rotation"):
        positions = (z * X + x) * TOK + jnp.maximum(sel_rows, 0)
        freqs = ROPE_BASE ** (-(jnp.arange(HALF_DIM, dtype=jnp.float32) * 2.0 / HEAD_DIM))
        angles = positions.astype(jnp.float32)[:, None] * freqs[None, :]
        cosine, sine = jnp.cos(angles), jnp.sin(angles)
        cos_q = jnp.concatenate([cosine, cosine], axis=1)
        sin_q = jnp.concatenate([-sine, sine], axis=1)
        cos_kv = jnp.where(is_key, cos_q, 1.0)
        sin_kv = jnp.where(is_key, sin_q, 0.0)
        lane = jnp.arange(HEAD_DIM, dtype=jnp.int32)[None, :]
        mark = jnp.where(is_key & (sel_rows < 0)[:, None] & (lane == 0), UNUSED, 0.0)

    with jax.named_scope("keys_values"):
        touched = call(touch_kernel, shape((16, HEAD_DIM)), 2, loose=1)(kv_weight, picked)
        normed, kv = call(
            norm_kv_kernel,
            [shape((CAP, N_MP * WIDTH)), shape((CAP, HEAD_DIM))],
            9,
            smem_first=True,
            flops=2 * CAP * N_MP * WIDTH * HEAD_DIM,
            nbytes=3 << 20,
        )(
            core_at,
            own_rows,
            other_rows,
            norm_gain.reshape(N_MP, WIDTH),
            cos_kv,
            sin_kv,
            mark,
            kv_weight,
            touched,
        )
        to_heads = [(m, 2 * m if m < Y else 2 * (m - Y) + 1) for m in range(N_MP)]
        kv = lax.ppermute(kv, MP, to_heads)
    with jax.named_scope("queries"):
        mine, theirs = call(
            query_kernel,
            [shape((HEADS * HALF, HEAD_DIM)), shape((HEADS * HALF, HEAD_DIM))],
            5,
            smem_first=True,
            flops=2 * CAP * N_MP * WIDTH * WIDTH,
            nbytes=3 << 20,
        )(core_at, normed, cos_q, sin_q, query_weight)
        kv, mine = lax.optimization_barrier((kv, mine))
    with jax.named_scope("spread_keys_values"):
        kv = jnp.broadcast_to(kv[None], (Z, CAP, HEAD_DIM))
        kv, theirs = lax.optimization_barrier((kv, theirs))
        own = lax.all_to_all(kv, "z", 0, 0, tiled=True)
    with jax.named_scope("share_queries"):
        queries = jnp.concatenate([mine, lax.ppermute(theirs, "c", swap)], axis=0)
        queries = lax.all_gather(queries, "x", axis=0, tiled=True)
        own, queries = lax.optimization_barrier((own, queries))
        other = lax.ppermute(own, "c", swap)
    out_other = lax.ppermute(out_weight, "c", swap)
    with jax.named_scope("attend"):
        columns = X * ROWS
        parts = call(
            attend_kernel,
            shape((X, HEAD_DIM + STATS, ROWS)),
            4,
            scratch=(
                pltpu.VMEM((1, columns), jnp.float32),
                pltpu.VMEM((1, columns), jnp.float32),
                pltpu.VMEM((HEAD_DIM, columns), jnp.float32),
            ),
            smem_first=True,
            flops=4 * columns * HEAD_DIM * Z * CAP,
            nbytes=2 << 20,
        )(place, queries, own, other)
        parts = lax.all_to_all(parts, "x", 0, 0, tiled=True)
    with jax.named_scope("project"):
        partial = call(
            project_kernel,
            shape((N_MP, HALF, WIDTH)),
            3,
            loose=1,
            scratch=(
                pltpu.VMEM((WIDTH, N_MP * WIDTH), jnp.bfloat16),
                pltpu.SemaphoreType.DMA,
            ),
            flops=2 * CAP * WIDTH * N_MP * WIDTH,
            nbytes=5 << 20,
        )(parts, out_other, out_weight)
        partial = lax.all_to_all(partial, MP, 0, 0, tiled=True)
    with jax.named_scope("mix"):
        return call(mix_kernel, shape((TOK, WIDTH)), 4, nbytes=2 << 20)(
            sel, router_weight.reshape(1, TOK), hidden_state, partial
        )


def solution(mesh):
    fine = Mesh(mesh.devices.reshape(Z, X, Y, C), AXES)
    in_specs = (
        P(SEQ, MP),
        P(SEQ),
        P(),
        P(None, MP),
        P(None, MP),
        P(MP, None),
        P(SEQ),
        P(SEQ),
        P(SEQ),
    )
    return jax.shard_map(
        local, mesh=fine, in_specs=in_specs, out_specs=P(SEQ, MP), check_vma=False
    )
```

time: 151 us -> 130 us (0.86)
  blocking collectives: 99.7 us -> 36.1 us
  waiting for transfers between devices: 13 us -> 38.9 us
  starting transfers between devices: 25.5 us -> 41.4 us
  Pallas kernels: 6.47 us -> 9.45 us
  other arithmetic: 2.56 us -> 0.6 us
    all_to_all x2 -> x0, blocking collectives: 38.1 us -> none  [the longest x1 30.2 us: local(): lax.all_to_all(jnp.broadcast_to(kv[None], (Z, CAP, HEAD_DIM)), 'z', 0, 0,...]
    all_to_all x2 -> x3, waiting for transfers between devices: 5.59 us -> 26.9 us  [the longest x1 15.2 us: local(): own_rows = lax.all_to_all(picked, MP, 0, 0, tiled=True)]
    all_to_all x1, blocking collectives: 41.8 us -> 26.1 us  [local(): partial = lax.all_to_all(partial, MP, 0, 0, tiled=True)]
    all_gather x1, blocking collectives: 19.8 us -> 10 us  [local(): queries = lax.all_gather(queries, 'x', axis=0, tiled=True)]
    all_to_all x2 -> x3, starting transfers between devices: 21.5 us -> 31.2 us  [the longest x1 17.5 us: local(): own_rows = lax.all_to_all(picked, MP, 0, 0, tiled=True)]
    ppermute x1 -> x4, starting transfers between devices: 1.91 us -> 8.28 us  [the longest x1 2.41 us: local(): queries = jnp.concatenate([mine, lax.ppermute(theirs, 'c', swap)], axis=0)]
    ppermute x1 -> x4, waiting for transfers between devices: 0.01 us -> 5.22 us  [the longest x1 1.8 us: local(): other = lax.ppermute(own, 'c', swap)]
    pallas_call x5 -> x6, Pallas kernels: 5.36 us -> 8.41 us  [the longest x1 2.73 us: local(): call(project_kernel, shape((N_MP, HALF, WIDTH)), 3, loose=1, scratch=(plt...]
  transfers between devices with their start and end apart: 4 -> 8, of which waited for: 2 -> 7; matrix products, arithmetic and copies ran while one was open for 2% -> 1% of each run, Pallas kernels for 1% -> 2%
where the time goes in v2:
time: 130 us; the launch traced here: 129 us
  starting transfers between devices  41.4 us (32%)
  waiting for transfers between devices  38.9 us (30%)
  blocking collectives  36.1 us (28%)
  Pallas kernels  9.45 us (7%)
  local copies, waits for them, and re-layouts  2.67 us (2%)
    all_to_all x1, blocking collectives, local(): partial = lax.all_to_all(partial, MP, 0, 0, tiled=True)  26.1 us
    all_to_all x1, starting transfers between devices, local(): own_rows = lax.all_to_all(picked, MP, 0, 0, tiled=True)  17.5 us
    all_to_all x1, waiting for transfers between devices, local(): own_rows = lax.all_to_all(picked, MP, 0, 0, tiled=True)  15.2 us
    all_gather x1, blocking collectives, local(): queries = lax.all_gather(queries, 'x', axis=0, tiled=True)  10 us
    all_to_all x1, starting transfers between devices, local(): own = lax.all_to_all(kv, 'z', 0, 0, tiled=True)  9.67 us
    ppermute x1, waiting for transfers between devices, local(): kv = lax.ppermute(kv, MP, to_heads)  6.81 us
    all_to_all x1, waiting for transfers between devices, local(): parts = lax.all_to_all(parts, 'x', 0, 0, tiled=True)  6.4 us
    all_to_all x1, waiting for transfers between devices, local(): own = lax.all_to_all(kv, 'z', 0, 0, tiled=True)  5.28 us
  transfers between devices with their start and end apart: 8, of which 7 were waited for; matrix products, arithmetic and copies ran while one was open for 1% of the time, Pallas kernels for 2%

profile of v2, /device:TPU:1, one launch (start us, length us, event | category | flops | bytes accessed | tf_op | source)
XLA Modules:
  0.0 129.3 jit_solution(13624460332277486567)
XLA Ops:
  0.0 2.1 %pick.1.after_ref = bf16[16,64,256]{2,1,0:T(8,128)(2,1)} custom-call(s32[1,128]{1,0:T(1,128)} %bitcast.5, bf16[512,256]{1,0:T(8,128)(2,1)} %hidden_ref.3), custom_call_target="tpu_custom_call" | custom-call | tf_op jit(solution)/shard_map/pick/pallas_call | solution.py:248
  2.1 17.5 %all-to-all-start = ((bf16[16,64,256]{2,1,0:T(8,128)(2,1)}), bf16[16,64,256]{2,1,0:T(8,128)(2,1)S(1)}, u32[]{:S(2)}, u32[]{:S(2)}) async-start(bf16[16,64,256]{2,1,0:T(8,128)(2,1)} %pick.1.after_ref), calls=%async_computation | async-start | bytes 1048576 | tf_op jit(solution)/shard_map/gather_features/all_to_all | solution.py:250
  19.6 0.7 reshape.26.gain_ref
  20.3 1.0 copy-done
  21.4 0.3 fusion
  21.7 15.2 %all-to-all-done.own_ref = bf16[16,64,256]{2,1,0:T(8,128)(2,1)S(1)} async-done(((bf16[16,64,256]{2,1,0:T(8,128)(2,1)}), bf16[16,64,256]{2,1,0:T(8,128)(2,1)S(1)}, u32[]{:S(2)}, u32[]{:S(2)}) %all-to-all-start) | async-done | bytes 524320 | tf_op jit(solution)/shard_map/gather_features/all_to_all | solution.py:250
  37.0 2.0 %collective-permute-start = (bf16[16,64,256]{2,1,0:T(8,128)(2,1)S(1)}, bf16[16,64,256]{2,1,0:T(8,128)(2,1)S(1)}, u32[]{:S(2)}, u32[]{:S(2)}) collective-permute-start(bf16[16,64,256]{2,1,0:T(8,128)(2,1)S(1)} %all-to-all-done.own_ref), channel_id=1, source_target_pairs={{0,1},{1,0},{2,3},{3,2},{4,5},{5,4},{6,7},{7,6},{8,9},{9,8},{10,11... | collective-permute-start | bytes 1572872 | tf_op jit(solution)/shard_map/gather_features/ppermute | solution.py:251
  39.0 0.1 pad_maximum_fusion
  39.1 0.1 and_select_fusion.mark_ref
  39.2 1.7 %collective-permute-done.other_ref = bf16[16,64,256]{2,1,0:T(8,128)(2,1)S(1)} collective-permute-done((bf16[16,64,256]{2,1,0:T(8,128)(2,1)S(1)}, bf16[16,64,256]{2,1,0:T(8,128)(2,1)S(1)}, u32[]{:S(2)}, u32[]{:S(2)}) %collective-permute-start) | collective-permute-done | bytes 524320 | tf_op jit(solution)/shard_map/gather_features/ppermute | solution.py:251
  40.9 0.9 keys_values.3
  41.8 1.9 %collective-permute-start.1 = (bf16[128,128]{1,0:T(8,128)(2,1)S(1)}, bf16[128,128]{1,0:T(8,128)(2,1)S(1)}, u32[]{:S(2)}, u32[]{:S(2)}) collective-permute-start(bf16[128,128]{1,0:T(8,128)(2,1)S(1)} %get-tuple-element.15), channel_id=1, source_target_pairs={{0,0},{1,2},{2,4},{3,6},{4,8},{5,10},{6,12},{7,14},{8,1},{9,3},{10... | collective-permute-start | bytes 98312 | tf_op jit(solution)/shard_map/keys_values/ppermute | solution.py:286
  43.7 0.0 copy-start.3
  43.7 0.6 queries.1
  44.3 6.8 %collective-permute-done.1 = bf16[128,128]{1,0:T(8,128)(2,1)S(1)} collective-permute-done((bf16[128,128]{1,0:T(8,128)(2,1)S(1)}, bf16[128,128]{1,0:T(8,128)(2,1)S(1)}, u32[]{:S(2)}, u32[]{:S(2)}) %collective-permute-start.1) | collective-permute-done | bytes 32800 | tf_op jit(solution)/shard_map/keys_values/ppermute | solution.py:286
  51.1 0.9 broadcast_in_dim.27
  52.0 9.7 %all-to-all-start.1 = ((bf16[16,128,128]{2,1,0:T(8,128)(2,1)}), bf16[16,128,128]{2,1,0:T(8,128)(2,1)S(1)}, u32[]{:S(2)}, u32[]{:S(2)}) async-start(bf16[16,128,128]{2,1,0:T(8,128)(2,1)} %broadcast_in_dim.27), calls=%async_computation.1 | async-start | bytes 1048576 | tf_op jit(solution)/shard_map/spread_keys_values/all_to_all | solution.py:300
  61.6 1.9 %collective-permute-start.4 = (bf16[256,4096]{1,0:T(8,128)(2,1)S(1)}, bf16[256,4096]{1,0:T(8,128)(2,1)}, u32[]{:S(2)}, u32[]{:S(2)}) collective-permute-start(bf16[256,4096]{1,0:T(8,128)(2,1)S(1)} %copy-done.3), channel_id=1, source_target_pairs={{0,1},{1,0},{2,3},{3,2},{4,5},{5,4},{6,7},{7,6},{8,9},{9,8},{10,11... | collective-permute-start | bytes 6291464 | tf_op jit(solution)/shard_map/ppermute | solution.py:306
  63.6 2.4 %collective-permute-start.2 = (bf16[128,128]{1,0:T(8,128)(2,1)S(1)}, bf16[128,128]{1,0:T(8,128)(2,1)S(1)}, u32[]{:S(2)}, u32[]{:S(2)}) collective-permute-start(bf16[128,128]{1,0:T(8,128)(2,1)S(1)} %get-tuple-element.22), channel_id=1, source_target_pairs={{0,1},{1,0},{2,3},{3,2},{4,5},{5,4},{6,7},{7,6},{8,9},{9,8},{10,11... | collective-permute-start | bytes 98312 | tf_op jit(solution)/shard_map/share_queries/ppermute | solution.py:302
  66.0 1.8 %collective-permute-done.2 = bf16[128,128]{1,0:T(8,128)(2,1)S(1)} collective-permute-done((bf16[128,128]{1,0:T(8,128)(2,1)S(1)}, bf16[128,128]{1,0:T(8,128)(2,1)S(1)}, u32[]{:S(2)}, u32[]{:S(2)}) %collective-permute-start.2) | collective-permute-done | bytes 32800 | tf_op jit(solution)/shard_map/share_queries/ppermute | solution.py:302
  67.8 10.0 %all_gather.3.query_ref = bf16[1024,128]{1,0:T(8,128)(2,1)S(1)} all-gather(bf16[256,128]{1,0:T(8,128)(2,1)S(1)} %pad_maximum_fusion.2), channel_id=1, replica_groups=mesh['z'=16,'x'=4,'y'=8,'c'=2] {'x'}, dimensions={0}, use_global_device_ids=true | all-gather | bytes 327680 | tf_op jit(solution)/shard_map/share_queries/all_gather | solution.py:303
  77.8 5.3 %all-to-all-done.1.own_ref = bf16[16,128,128]{2,1,0:T(8,128)(2,1)S(1)} async-done(((bf16[16,128,128]{2,1,0:T(8,128)(2,1)}), bf16[16,128,128]{2,1,0:T(8,128)(2,1)S(1)}, u32[]{:S(2)}, u32[]{:S(2)}) %all-to-all-start.1) | async-done | bytes 524320 | tf_op jit(solution)/shard_map/spread_keys_values/all_to_all | solution.py:300
  83.0 1.9 %collective-permute-start.3 = (bf16[16,128,128]{2,1,0:T(8,128)(2,1)S(1)}, bf16[16,128,128]{2,1,0:T(8,128)(2,1)S(1)}, u32[]{:S(2)}, u32[]{:S(2)}) collective-permute-start(bf16[16,128,128]{2,1,0:T(8,128)(2,1)S(1)} %all-to-all-done.1.own_ref), channel_id=1, source_target_pairs={{0,1},{1,0},{2,3},{3,2},{4,5},{5,4},{6,7},{7,6},{8,9},{9,8},{10,11... | collective-permute-start | bytes 1572872 | tf_op jit(solution)/shard_map/share_queries/ppermute | solution.py:305
  85.0 0.1 pad_add_fusion.place_ref
  85.0 1.8 %collective-permute-done.3.other_ref = bf16[16,128,128]{2,1,0:T(8,128)(2,1)S(1)} collective-permute-done((bf16[16,128,128]{2,1,0:T(8,128)(2,1)S(1)}, bf16[16,128,128]{2,1,0:T(8,128)(2,1)S(1)}, u32[]{:S(2)}, u32[]{:S(2)}) %collective-permute-start.3) | collective-permute-done | bytes 524320 | tf_op jit(solution)/shard_map/share_queries/ppermute | solution.py:305
  86.8 2.2 %attend.1 = bf16[4,144,256]{2,1,0:T(8,128)(2,1)} custom-call(s32[3]{0:T(128)S(1)} %pad_add_fusion.place_ref, bf16[1024,128]{1,0:T(8,128)(2,1)S(1)} %all_gather.3.query_ref, bf16[16,128,128]{2,1,0:T(8,128)(2,1)S(1)} %all-to-all-done.1.own_ref, bf16[16,128,128]{2,1,0:T(8,128)(2,1)S(1)} %collective-permute-done.3.other_ref), custom_call_target="tpu_custom_call" | custom-call | flops 1073741824 | bytes 2097152 | tf_op jit(solution)/shard_map/attend/pallas_call | solution.py:309
  89.0 4.0 %all-to-all-start.2 = ((bf16[4,144,256]{2,1,0:T(8,128)(2,1)}), bf16[4,144,256]{2,1,0:T(8,128)(2,1)S(1)}, u32[]{:S(2)}, u32[]{:S(2)}) async-start(bf16[4,144,256]{2,1,0:T(8,128)(2,1)} %attend.1), calls=%async_computation.2 | async-start | bytes 589824 | tf_op jit(solution)/shard_map/attend/all_to_all | solution.py:322
  93.0 0.0 collective-permute-done.4.other_ref
  93.0 6.4 %all-to-all-done.2.parts_ref = bf16[4,144,256]{2,1,0:T(8,128)(2,1)S(1)} async-done(((bf16[4,144,256]{2,1,0:T(8,128)(2,1)}), bf16[4,144,256]{2,1,0:T(8,128)(2,1)S(1)}, u32[]{:S(2)}, u32[]{:S(2)}) %all-to-all-start.2) | async-done | bytes 294944 | tf_op jit(solution)/shard_map/attend/all_to_all | solution.py:322
  99.4 2.7 %project.1 = bf16[16,64,256]{2,1,0:T(8,128)(2,1)S(1)} custom-call(bf16[4,144,256]{2,1,0:T(8,128)(2,1)S(1)} %all-to-all-done.2.parts_ref, bf16[256,4096]{1,0:T(8,128)(2,1)} %collective-permute-done.4.other_ref, bf16[256,4096]{1,0:T(8,128)(2,1)S(1)} %copy-done.3), custom_call_target="tpu_custom_call" | custom-call | flops 268435456 | bytes 5242880 | tf_op jit(solution)/shard_map/project/pallas_call | solution.py:324
  102.2 26.1 %all_to_all.20.parts_ref = bf16[16,64,256]{2,1,0:T(8,128)(2,1)S(1)} all-to-all(bf16[16,64,256]{2,1,0:T(8,128)(2,1)S(1)} %project.1), channel_id=1, replica_groups=mesh['z'=16,'x'=4,'y'=8,'c'=2] {'y','c'}, dimensions={0} | all-to-all | bytes 1048576 | tf_op jit(solution)/shard_map/project/all_to_all | solution.py:336
  128.2 1.0 mix.1
  (17 shorter events, 0.1 us)
Async XLA Ops:
  0.0 21.4 %copy-start.5 = (s32[128]{0:T(128)S(1)}, s32[128]{0:T(128)}, u32[]{:S(2)}) copy-start(s32[128]{0:T(128)} %param.15) | copy-start | bytes 1540
  0.0 20.3 %copy-start.1 = (bf16[4096,128]{1,0:T(8,128)(2,1)S(1)}, bf16[4096,128]{1,0:T(8,128)(2,1)}, u32[]{:S(2)}) copy-start(bf16[4096,128]{1,0:T(8,128)(2,1)} %weight_ref.4) | copy-start | bytes 3145732
  2.1 34.9 %all-to-all-start = ((bf16[16,64,256]{2,1,0:T(8,128)(2,1)}), bf16[16,64,256]{2,1,0:T(8,128)(2,1)S(1)}, u32[]{:S(2)}, u32[]{:S(2)}) async-start(bf16[16,64,256]{2,1,0:T(8,128)(2,1)} %pick.1.after_ref), calls=%async_computation | async-start | bytes 1048576 | tf_op jit(solution)/shard_map/gather_features/all_to_all | solution.py:250
  20.3 1.0 copy-start
  37.0 6.7 %copy-start.2 = (bf16[4096,256]{1,0:T(8,128)(2,1)S(1)}, bf16[4096,256]{1,0:T(8,128)(2,1)}, u32[]{:S(2)}) copy-start(bf16[4096,256]{1,0:T(8,128)(2,1)} %weight_ref.5) | copy-start | bytes 6291460
  37.0 3.9 %collective-permute-start = (bf16[16,64,256]{2,1,0:T(8,128)(2,1)S(1)}, bf16[16,64,256]{2,1,0:T(8,128)(2,1)S(1)}, u32[]{:S(2)}, u32[]{:S(2)}) collective-permute-start(bf16[16,64,256]{2,1,0:T(8,128)(2,1)S(1)} %all-to-all-done.own_ref), channel_id=1, source_target_pairs={{0,1},{1,0},{2,3},{3,2},{4,5},{5,4},{6,7},{7,6},{8,9},{9,8},{10,11... | collective-permute-start | bytes 1572872 | tf_op jit(solution)/shard_map/gather_features/ppermute | solution.py:251
  41.8 9.3 %collective-permute-start.1 = (bf16[128,128]{1,0:T(8,128)(2,1)S(1)}, bf16[128,128]{1,0:T(8,128)(2,1)S(1)}, u32[]{:S(2)}, u32[]{:S(2)}) collective-permute-start(bf16[128,128]{1,0:T(8,128)(2,1)S(1)} %get-tuple-element.15), channel_id=1, source_target_pairs={{0,0},{1,2},{2,4},{3,6},{4,8},{5,10},{6,12},{7,14},{8,1},{9,3},{10... | collective-permute-start | bytes 98312 | tf_op jit(solution)/shard_map/keys_values/ppermute | solution.py:286
  43.7 18.0 %copy-start.3 = (bf16[256,4096]{1,0:T(8,128)(2,1)S(1)}, bf16[256,4096]{1,0:T(8,128)(2,1)}, u32[]{:S(2)}) copy-start(bf16[256,4096]{1,0:T(8,128)(2,1)} %own_ref.1) | copy-start | bytes 6291460
  52.0 31.1 %all-to-all-start.1 = ((bf16[16,128,128]{2,1,0:T(8,128)(2,1)}), bf16[16,128,128]{2,1,0:T(8,128)(2,1)S(1)}, u32[]{:S(2)}, u32[]{:S(2)}) async-start(bf16[16,128,128]{2,1,0:T(8,128)(2,1)} %broadcast_in_dim.27), calls=%async_computation.1 | async-start | bytes 1048576 | tf_op jit(solution)/shard_map/spread_keys_values/all_to_all | solution.py:300
  61.6 31.4 %collective-permute-start.4 = (bf16[256,4096]{1,0:T(8,128)(2,1)S(1)}, bf16[256,4096]{1,0:T(8,128)(2,1)}, u32[]{:S(2)}, u32[]{:S(2)}) collective-permute-start(bf16[256,4096]{1,0:T(8,128)(2,1)S(1)} %copy-done.3), channel_id=1, source_target_pairs={{0,1},{1,0},{2,3},{3,2},{4,5},{5,4},{6,7},{7,6},{8,9},{9,8},{10,11... | collective-permute-start | bytes 6291464 | tf_op jit(solution)/shard_map/ppermute | solution.py:306
  63.6 4.2 %collective-permute-start.2 = (bf16[128,128]{1,0:T(8,128)(2,1)S(1)}, bf16[128,128]{1,0:T(8,128)(2,1)S(1)}, u32[]{:S(2)}, u32[]{:S(2)}) collective-permute-start(bf16[128,128]{1,0:T(8,128)(2,1)S(1)} %get-tuple-element.22), channel_id=1, source_target_pairs={{0,1},{1,0},{2,3},{3,2},{4,5},{5,4},{6,7},{7,6},{8,9},{9,8},{10,11... | collective-permute-start | bytes 98312 | tf_op jit(solution)/shard_map/share_queries/ppermute | solution.py:302
  83.0 3.8 %collective-permute-start.3 = (bf16[16,128,128]{2,1,0:T(8,128)(2,1)S(1)}, bf16[16,128,128]{2,1,0:T(8,128)(2,1)S(1)}, u32[]{:S(2)}, u32[]{:S(2)}) collective-permute-start(bf16[16,128,128]{2,1,0:T(8,128)(2,1)S(1)} %all-to-all-done.1.own_ref), channel_id=1, source_target_pairs={{0,1},{1,0},{2,3},{3,2},{4,5},{5,4},{6,7},{7,6},{8,9},{9,8},{10,11... | collective-permute-start | bytes 1572872 | tf_op jit(solution)/shard_map/share_queries/ppermute | solution.py:305
  89.0 10.4 %all-to-all-start.2 = ((bf16[4,144,256]{2,1,0:T(8,128)(2,1)}), bf16[4,144,256]{2,1,0:T(8,128)(2,1)S(1)}, u32[]{:S(2)}, u32[]{:S(2)}) async-start(bf16[4,144,256]{2,1,0:T(8,128)(2,1)} %attend.1), calls=%async_computation.2 | async-start | bytes 589824 | tf_op jit(solution)/shard_map/attend/all_to_all | solution.py:322
  93.0 35.2 %copy-start.4 = (bf16[512,256]{1,0:T(8,128)(2,1)S(1)}, bf16[512,256]{1,0:T(8,128)(2,1)}, u32[]{:S(2)}) copy-start(bf16[512,256]{1,0:T(8,128)(2,1)} %hidden_ref.3) | copy-start | bytes 786436
  93.0 35.2 %copy-start.6 = (f32[512]{0:T(512)S(1)}, f32[512]{0:T(512)}, u32[]{:S(2)}) copy-start(f32[512]{0:T(512)} %param.10) | copy-start | bytes 6148

commit v3 on v2

--- a/solution.py
+++ b/solution.py
@@ -14,9 +14,11 @@
 ROPE_BASE = 500000.0
 EPS = 1e-05
 
-Z, X, Y, C = 16, 4, 8, 2
-AXES = ("z", "x", "y", "c")
-SEQ, MP = ("z", "x"), ("y", "c")
+ZH, ZP, X, Y, C = 8, 2, 4, 8, 2
+AXES = ("zh", "zp", "x", "y", "c")
+SEQ, MP = ("zh", "zp", "x"), ("y", "c")
+NEAR = ("zp", "x")
+GROUP = ZP * X
 N_MP = Y * C
 CAP = 128
 HALF = CAP // C
@@ -26,7 +28,8 @@
 ROWS = C * HEADS * HALF
 STATS = 16
 UNUSED = 1e30
-CHAINS = 2
+PIECES = 4
+CHAINS = 1
 LOW, LOWER = -1e30, -2e30
 VMEM = 48 * 1024 * 1024
 WHOLE = 62 * 1024 * 1024
@@ -63,7 +66,7 @@
 
 def touch_kernel(weight_ref, after_ref, out_ref):
     del after_ref
-    out_ref[...] = weight_ref[:16, :]
+    out_ref[...] = weight_ref[:16, :HEAD_DIM]
 
 
 def norm_kv_kernel(
@@ -109,14 +112,16 @@
 
 
 def attend_kernel(place_ref, query_ref, own_ref, other_ref, out_ref, high_ref, sum_ref, acc_ref):
-    z, x, c = place_ref[0], place_ref[1], place_ref[2]
-    columns = X * ROWS
+    zh, zp, x, c = place_ref[0], place_ref[1], place_ref[2], place_ref[3]
+    columns = GROUP * ROWS
     scale = math.log2(math.e) / math.sqrt(HEAD_DIM)
     high_ref[...] = jnp.full(high_ref.shape, LOW, jnp.float32)
     sum_ref[...] = jnp.zeros(sum_ref.shape, jnp.float32)
     acc_ref[...] = jnp.zeros(acc_ref.shape, jnp.float32)
     column = lax.broadcasted_iota(jnp.int32, (1, columns), 1)
-    query_shard = z * X + column // ROWS
+    swapped = column // ROWS % ZP
+    query_zp = zp + swapped - 2 * zp * swapped
+    query_shard = (zh * ZP + query_zp) * X + column // (ZP * ROWS)
     query_order = query_shard * CAP + c * HALF + column % HALF
 
     def step(pair, carry):
@@ -125,7 +130,7 @@
         keys = jnp.where(c == 0, own, other)
         values_t = jnp.where(c == 0, other, own).T
         row = lax.broadcasted_iota(jnp.int32, (2 * CAP, 1), 0)
-        shard = (2 * pair + row // CAP) * X + x
+        shard = ((2 * pair + row // CAP) * ZP + zp) * X + x
         key_order = shard * CAP + row % CAP
         unused = keys[:, 0:1].astype(jnp.float32) > 0.1 * UNUSED
         key_order = jnp.where(unused, 1 << 30, key_order)
@@ -144,7 +149,7 @@
             )
         return carry
 
-    lax.fori_loop(0, z // 2 + 1, step, 0)
+    lax.fori_loop(0, zh // 2 + 1, step, 0)
     total = sum_ref[...]
     safe = jnp.maximum(total, 1e-30)
     attended = (acc_ref[...] / safe).astype(jnp.bfloat16)
@@ -156,35 +161,48 @@
         stats = jnp.where(stat_row == k, piece, stats)
         left = left - piece
     stats = stats.astype(jnp.bfloat16)
-    for home in range(X):
-        span = slice(home * ROWS, (home + 1) * ROWS)
-        out_ref[home, :HEAD_DIM, :] = attended[:, span]
-        out_ref[home, HEAD_DIM:, :] = stats[:, span]
-
-
-def project_kernel(parts_ref, other_ref, own_ref, out_ref, own_buf, arrived):
-    copy = pltpu.make_async_copy(own_ref, own_buf, arrived)
-    copy.start()
+    for to_x in range(X):
+        for swap in range(ZP):
+            first = (to_x * ZP + swap) * ROWS
+            home = (zp + swap - 2 * zp * swap) * X + to_x
+            out_ref[home, :HEAD_DIM, :] = attended[:, first : first + ROWS]
+            out_ref[home, HEAD_DIM:, :] = stats[:, first : first + ROWS]
+
+
+def project_kernel(parts_ref, own_ref, *refs):
+    other_refs, (out_ref, other_buf, total_ref, arrived) = refs[:PIECES], refs[PIECES:]
+    copies = [
+        pltpu.make_async_copy(ref, other_buf.at[i], arrived.at[i])
+        for i, ref in enumerate(other_refs)
+    ]
+    for copy in copies:
+        copy.start()
     logs = []
-    for t in range(X):
+    for t in range(GROUP):
         stats = parts_ref[t, HEAD_DIM:, :].astype(jnp.float32)
         logs.append(stats[0:1] + stats[1:2] + stats[2:3])
     high = functools.reduce(jnp.maximum, logs)
     shares = [jnp.exp2(v - high) for v in logs]
     total = functools.reduce(jnp.add, shares)
     merged = jnp.zeros((HEAD_DIM, ROWS), jnp.float32)
-    for t in range(X):
+    for t in range(GROUP):
         part = parts_ref[t, :HEAD_DIM, :].astype(jnp.float32)
         merged += part * (shares[t] / total)
     merged = merged.T.astype(jnp.bfloat16)
     attended = jnp.concatenate(
         [merged[j * HALF : (j + 1) * HALF] for j in range(C * HEADS)], axis=1
     )
-    copy.wait()
     for m in range(N_MP):
         columns = slice(m * WIDTH, (m + 1) * WIDTH)
-        block = dot(attended[:, :WIDTH], own_buf[:, columns], ((1,), (0,)))
-        block += dot(attended[:, WIDTH:], other_ref[:, columns], ((1,), (0,)))
+        total_ref[m] = dot(attended[:, :WIDTH], own_ref[:, columns], ((1,), (0,)))
+    for copy in copies:
+        copy.wait()
+    for m in range(N_MP):
+        columns = slice(m * WIDTH, (m + 1) * WIDTH)
+        block = total_ref[m]
+        for i in range(PIECES):
+            rows = slice(WIDTH + i * WIDTH // PIECES, WIDTH + (i + 1) * WIDTH // PIECES)
+            block += dot(attended[:, rows], other_buf[i, :, columns], ((1,), (0,)))
         out_ref[m] = block.astype(jnp.bfloat16)
 
 
@@ -236,10 +254,10 @@
     dest_shard,
     dest_slot,
 ):
-    z, x = lax.axis_index("z"), lax.axis_index("x")
+    zh, zp, x = lax.axis_index("zh"), lax.axis_index("zp"), lax.axis_index("x")
     y, core = lax.axis_index("y"), lax.axis_index("c")
     is_key = y < Y // 2
-    place = jnp.stack([z, x, core]).astype(jnp.int32)
+    place = jnp.stack([zh, zp, x, core]).astype(jnp.int32)
     core_at = core.astype(jnp.int32)[None]
     sel = sel_rows.reshape(1, CAP)
     swap = [(0, 1), (1, 0)]
@@ -248,10 +266,17 @@
         picked = call(pick_kernel, shape((N_MP, HALF, WIDTH)), 2, vmem=WHOLE)(sel, hidden_state)
     with jax.named_scope("gather_features"):
         own_rows = lax.all_to_all(picked, MP, 0, 0, tiled=True)
+        deep = WIDTH // PIECES
+        out_other = [
+            lax.ppermute(out_weight[i * deep : (i + 1) * deep], "c", swap) for i in range(PIECES)
+        ]
+        own_rows, *out_other = lax.optimization_barrier((own_rows, *out_other))
         other_rows = lax.ppermute(own_rows, "c", swap)
 
+    with jax.named_scope("touch"):
+        touched = call(touch_kernel, shape((16, HEAD_DIM)), 2, loose=1)(kv_weight, picked)
     with jax.named_scope("rotation"):
-        positions = (z * X + x) * TOK + jnp.maximum(sel_rows, 0)
+        positions = ((zh * ZP + zp) * X + x) * TOK + jnp.maximum(sel_rows, 0)
         freqs = ROPE_BASE ** (-(jnp.arange(HALF_DIM, dtype=jnp.float32) * 2.0 / HEAD_DIM))
         angles = positions.astype(jnp.float32)[:, None] * freqs[None, :]
         cosine, sine = jnp.cos(angles), jnp.sin(angles)
@@ -263,25 +288,14 @@
         mark = jnp.where(is_key & (sel_rows < 0)[:, None] & (lane == 0), UNUSED, 0.0)
 
     with jax.named_scope("keys_values"):
-        touched = call(touch_kernel, shape((16, HEAD_DIM)), 2, loose=1)(kv_weight, picked)
         normed, kv = call(
             norm_kv_kernel,
             [shape((CAP, N_MP * WIDTH)), shape((CAP, HEAD_DIM))],
             9,
             smem_first=True,
-            flops=2 * CAP * N_MP * WIDTH * HEAD_DIM,
+            flops=2 * CAP * 4096 * HEAD_DIM,
             nbytes=3 << 20,
-        )(
-            core_at,
-            own_rows,
-            other_rows,
-            norm_gain.reshape(N_MP, WIDTH),
-            cos_kv,
-            sin_kv,
-            mark,
-            kv_weight,
-            touched,
-        )
+        )(core_at, own_rows, other_rows, norm_gain.reshape(N_MP, WIDTH), cos_kv, sin_kv, mark, kv_weight, touched)
         to_heads = [(m, 2 * m if m < Y else 2 * (m - Y) + 1) for m in range(N_MP)]
         kv = lax.ppermute(kv, MP, to_heads)
     with jax.named_scope("queries"):
@@ -293,22 +307,25 @@
             flops=2 * CAP * N_MP * WIDTH * WIDTH,
             nbytes=3 << 20,
         )(core_at, normed, cos_q, sin_q, query_weight)
-        kv, mine = lax.optimization_barrier((kv, mine))
+        both = jnp.concatenate([mine, theirs], axis=0)
+        swapped = lax.ppermute(both, "zp", swap)
+        kv, swapped = lax.optimization_barrier((kv, swapped))
     with jax.named_scope("spread_keys_values"):
-        kv = jnp.broadcast_to(kv[None], (Z, CAP, HEAD_DIM))
-        kv, theirs = lax.optimization_barrier((kv, theirs))
-        own = lax.all_to_all(kv, "z", 0, 0, tiled=True)
+        kv = jnp.broadcast_to(kv[None], (ZH, CAP, HEAD_DIM))
+        kv, both, swapped = lax.optimization_barrier((kv, both, swapped))
+        own = lax.all_to_all(kv, "zh", 0, 0, tiled=True)
     with jax.named_scope("share_queries"):
-        queries = jnp.concatenate([mine, lax.ppermute(theirs, "c", swap)], axis=0)
+        half = HEADS * HALF
+        away = lax.ppermute(jnp.concatenate([both[half:], swapped[half:]], axis=0), "c", swap)
+        queries = jnp.concatenate([both[:half], away[:half], swapped[:half], away[half:]], axis=0)
         queries = lax.all_gather(queries, "x", axis=0, tiled=True)
         own, queries = lax.optimization_barrier((own, queries))
         other = lax.ppermute(own, "c", swap)
-    out_other = lax.ppermute(out_weight, "c", swap)
     with jax.named_scope("attend"):
-        columns = X * ROWS
+        columns = GROUP * ROWS
         parts = call(
             attend_kernel,
-            shape((X, HEAD_DIM + STATS, ROWS)),
+            shape((GROUP, HEAD_DIM + STATS, ROWS)),
             4,
             scratch=(
                 pltpu.VMEM((1, columns), jnp.float32),
@@ -316,23 +333,24 @@
                 pltpu.VMEM((HEAD_DIM, columns), jnp.float32),
             ),
             smem_first=True,
-            flops=4 * columns * HEAD_DIM * Z * CAP,
+            flops=4 * columns * HEAD_DIM * ZH * CAP,
             nbytes=2 << 20,
         )(place, queries, own, other)
-        parts = lax.all_to_all(parts, "x", 0, 0, tiled=True)
+        parts = lax.all_to_all(parts, NEAR, 0, 0, tiled=True)
     with jax.named_scope("project"):
         partial = call(
             project_kernel,
             shape((N_MP, HALF, WIDTH)),
-            3,
-            loose=1,
+            2 + PIECES,
+            loose=PIECES,
             scratch=(
-                pltpu.VMEM((WIDTH, N_MP * WIDTH), jnp.bfloat16),
-                pltpu.SemaphoreType.DMA,
+                pltpu.VMEM((PIECES, WIDTH // PIECES, N_MP * WIDTH), jnp.bfloat16),
+                pltpu.VMEM((N_MP, HALF, WIDTH), jnp.float32),
+                pltpu.SemaphoreType.DMA((PIECES,)),
             ),
             flops=2 * CAP * WIDTH * N_MP * WIDTH,
             nbytes=5 << 20,
-        )(parts, out_other, out_weight)
+        )(parts, out_weight, *out_other)
         partial = lax.all_to_all(partial, MP, 0, 0, tiled=True)
     with jax.named_scope("mix"):
         return call(mix_kernel, shape((TOK, WIDTH)), 4, nbytes=2 << 20)(
@@ -341,7 +359,7 @@
 
 
 def solution(mesh):
-    fine = Mesh(mesh.devices.reshape(Z, X, Y, C), AXES)
+    fine = Mesh(mesh.devices.reshape(ZH, ZP, X, Y, C), AXES)
     in_specs = (
         P(SEQ, MP),
         P(SEQ),

time: 130 us -> 129 us (level)
  waiting for transfers between devices: 38.9 us -> 19.8 us
  blocking collectives: 36.1 us -> 48.2 us
  starting transfers between devices: 41.4 us -> 46.7 us
    all_to_all x0 -> x1, blocking collectives: none -> 14.2 us  [local(): parts = lax.all_to_all(parts, NEAR, 0, 0, tiled=True)]
    all_to_all x1, waiting for transfers between devices: 15.2 us -> 3.7 us  [local(): own_rows = lax.all_to_all(picked, MP, 0, 0, tiled=True)]
    all_to_all x2 -> x1, waiting for transfers between devices: 11.7 us -> 2.96 us  [local(): own = lax.all_to_all(kv, 'zh', 0, 0, tiled=True)]
    ppermute x2 -> x6, starting transfers between devices: 4.33 us -> 12.5 us  [the longest x4 8.64 us: local(): lax.ppermute(out_weight[i * deep:(i + 1) * deep], 'c', swap)]
    slice x0 -> x4, local copies, waits for them, and re-layouts: none -> 3.01 us  [the longest x1 2.99 us: local(): out_weight[i * deep:(i + 1) * deep]]
    all_to_all x1, blocking collectives: 26.1 us -> 23.1 us  [local(): partial = lax.all_to_all(partial, MP, 0, 0, tiled=True)]
    all_to_all x2 -> x1, starting transfers between devices: 13.7 us -> 10.9 us  [local(): own = lax.all_to_all(kv, 'zh', 0, 0, tiled=True)]
    ppermute x2 -> x6, waiting for transfers between devices: 1.76 us -> 2.62 us  [the longest x4 1.4 us: local(): lax.ppermute(out_weight[i * deep:(i + 1) * deep], 'c', swap)]
  transfers between devices with their start and end apart: 8 -> 11, of which waited for: 7 -> 7; matrix products, arithmetic and copies ran while one was open for 1% -> 3% of each run, Pallas kernels for 2% -> 0%
where the time goes in v3:
time: 129 us; the launch traced here: 128 us
  blocking collectives  48.2 us (37%)
  starting transfers between devices  46.7 us (36%)
  waiting for transfers between devices  19.8 us (15%)
  Pallas kernels  8.36 us (6%)
  local copies, waits for them, and re-layouts  3.8 us (3%)
    all_to_all x1, blocking collectives, local(): partial = lax.all_to_all(partial, MP, 0, 0, tiled=True)  23.1 us
    all_to_all x1, starting transfers between devices, local(): own_rows = lax.all_to_all(picked, MP, 0, 0, tiled=True)  17.5 us
    all_to_all x1, blocking collectives, local(): parts = lax.all_to_all(parts, NEAR, 0, 0, tiled=True)  14.2 us
    all_gather x1, blocking collectives, local(): queries = lax.all_gather(queries, 'x', axis=0, tiled=True)  11 us
    all_to_all x1, starting transfers between devices, local(): own = lax.all_to_all(kv, 'zh', 0, 0, tiled=True)  10.9 us
    ppermute x4, starting transfers between devices, local(): lax.ppermute(out_weight[i * deep:(i + 1) * deep], 'c', swap)  8.64 us
    ppermute x1, waiting for transfers between devices, local(): kv = lax.ppermute(kv, MP, to_heads)  7.41 us
    all_to_all x1, waiting for transfers between devices, local(): own_rows = lax.all_to_all(picked, MP, 0, 0, tiled=True)  3.7 us
  transfers between devices with their start and end apart: 11, of which 7 were waited for; matrix products, arithmetic and copies ran while one was open for 3% of the time, Pallas kernels for 0%

profile of v3, /device:TPU:1, one launch (start us, length us, event | category | flops | bytes accessed | tf_op | source)
XLA Modules:
  0.0 127.9 jit_solution(8007124501319552661)
XLA Ops:
  0.0 2.0 %pick.1.after_ref = bf16[16,64,256]{2,1,0:T(8,128)(2,1)} custom-call(s32[1,128]{1,0:T(1,128)} %bitcast.6, bf16[512,256]{1,0:T(8,128)(2,1)} %hidden_ref.3), custom_call_target="tpu_custom_call" | custom-call | tf_op jit(solution)/shard_map/pick/pallas_call | solution.py:266
  2.0 17.5 %all-to-all-start = ((bf16[16,64,256]{2,1,0:T(8,128)(2,1)}), bf16[16,64,256]{2,1,0:T(8,128)(2,1)S(1)}, u32[]{:S(2)}, u32[]{:S(2)}) async-start(bf16[16,64,256]{2,1,0:T(8,128)(2,1)} %pick.1.after_ref), calls=%async_computation | async-start | bytes 1048576 | tf_op jit(solution)/shard_map/gather_features/all_to_all | solution.py:268
  19.6 3.0 %fusion.1 = (bf16[64,4096]{1,0:T(8,128)(2,1)}, bf16[64,4096]{1,0:T(8,128)(2,1)}, bf16[64,4096]{1,0:T(8,128)(2,1)}, bf16[64,4096]{1,0:T(8,128)(2,1)}) fusion(bf16[256,4096]{1,0:T(8,128)(2,1)} %own_ref.1), kind=kLoop, calls=%fused_computation.17 | loop fusion | bytes 4194304 | tf_op jit(solution)/shard_map/gather_features/slice | solution.py:271
  22.6 2.1 %collective-permute-start.3 = (bf16[64,4096]{1,0:T(8,128)(2,1)}, bf16[64,4096]{1,0:T(8,128)(2,1)S(1)}, u32[]{:S(2)}, u32[]{:S(2)}) collective-permute-start(bf16[64,4096]{1,0:T(8,128)(2,1)} %get-tuple-element.39), channel_id=1, source_target_pairs={{0,1},{1,0},{2,3},{3,2},{4,5},{5,4},{6,7},{7,6},{8,9},{9,8},{10,11... | collective-permute-start | bytes 1572872 | tf_op jit(solution)/shard_map/gather_features/ppermute | solution.py:271
  24.7 2.2 %collective-permute-start.2 = (bf16[64,4096]{1,0:T(8,128)(2,1)}, bf16[64,4096]{1,0:T(8,128)(2,1)S(1)}, u32[]{:S(2)}, u32[]{:S(2)}) collective-permute-start(bf16[64,4096]{1,0:T(8,128)(2,1)} %get-tuple-element.40), channel_id=1, source_target_pairs={{0,1},{1,0},{2,3},{3,2},{4,5},{5,4},{6,7},{7,6},{8,9},{9,8},{10,11... | collective-permute-start | bytes 1572872 | tf_op jit(solution)/shard_map/gather_features/ppermute | solution.py:271
  26.9 2.1 %collective-permute-start.1 = (bf16[64,4096]{1,0:T(8,128)(2,1)}, bf16[64,4096]{1,0:T(8,128)(2,1)}, u32[]{:S(2)}, u32[]{:S(2)}) collective-permute-start(bf16[64,4096]{1,0:T(8,128)(2,1)} %get-tuple-element.41), channel_id=1, source_target_pairs={{0,1},{1,0},{2,3},{3,2},{4,5},{5,4},{6,7},{7,6},{8,9},{9,8},{10,11... | collective-permute-start | bytes 1572872 | tf_op jit(solution)/shard_map/gather_features/ppermute | solution.py:271
  29.0 2.2 %collective-permute-start = (bf16[64,4096]{1,0:T(8,128)(2,1)}, bf16[64,4096]{1,0:T(8,128)(2,1)}, u32[]{:S(2)}, u32[]{:S(2)}) collective-permute-start(bf16[64,4096]{1,0:T(8,128)(2,1)} %get-tuple-element.42), channel_id=1, source_target_pairs={{0,1},{1,0},{2,3},{3,2},{4,5},{5,4},{6,7},{7,6},{8,9},{9,8},{10,11... | collective-permute-start | bytes 1572872 | tf_op jit(solution)/shard_map/gather_features/ppermute | solution.py:271
  31.4 0.3 fusion
  31.7 0.1 pad_maximum_fusion.1
  31.8 1.4 %collective-permute-done.refs_0_ = bf16[64,4096]{1,0:T(8,128)(2,1)} collective-permute-done((bf16[64,4096]{1,0:T(8,128)(2,1)}, bf16[64,4096]{1,0:T(8,128)(2,1)}, u32[]{:S(2)}, u32[]{:S(2)}) %collective-permute-start) | collective-permute-done | bytes 524320 | tf_op jit(solution)/shard_map/gather_features/ppermute | solution.py:271
  33.2 3.7 %all-to-all-done.own_ref = bf16[16,64,256]{2,1,0:T(8,128)(2,1)S(1)} async-done(((bf16[16,64,256]{2,1,0:T(8,128)(2,1)}), bf16[16,64,256]{2,1,0:T(8,128)(2,1)S(1)}, u32[]{:S(2)}, u32[]{:S(2)}) %all-to-all-start) | async-done | bytes 524320 | tf_op jit(solution)/shard_map/gather_features/all_to_all | solution.py:268
  36.9 2.0 %collective-permute-start.4 = (bf16[16,64,256]{2,1,0:T(8,128)(2,1)S(1)}, bf16[16,64,256]{2,1,0:T(8,128)(2,1)S(1)}, u32[]{:S(2)}, u32[]{:S(2)}) collective-permute-start(bf16[16,64,256]{2,1,0:T(8,128)(2,1)S(1)} %all-to-all-done.own_ref), channel_id=1, source_target_pairs={{0,1},{1,0},{2,3},{3,2},{4,5},{5,4},{6,7},{7,6},{8,9},{9,8},{10,11... | collective-permute-start | bytes 1572872 | tf_op jit(solution)/shard_map/gather_features/ppermute | solution.py:274
  38.9 0.1 broadcast_select_fusion
  39.1 1.7 %collective-permute-done.4.other_ref = bf16[16,64,256]{2,1,0:T(8,128)(2,1)S(1)} collective-permute-done((bf16[16,64,256]{2,1,0:T(8,128)(2,1)S(1)}, bf16[16,64,256]{2,1,0:T(8,128)(2,1)S(1)}, u32[]{:S(2)}, u32[]{:S(2)}) %collective-permute-start.4) | collective-permute-done | bytes 524320 | tf_op jit(solution)/shard_map/gather_features/ppermute | solution.py:274
  40.8 0.9 keys_values.1
  41.7 0.6 queries.1
  42.3 1.9 %collective-permute-start.6 = (bf16[256,128]{1,0:T(8,128)(2,1)S(1)}, bf16[256,128]{1,0:T(8,128)(2,1)S(1)}, u32[]{:S(2)}, u32[]{:S(2)}) collective-permute-start(bf16[256,128]{1,0:T(8,128)(2,1)S(1)} %constant_dynamic-update-slice_fusion), channel_id=1, source_target_pairs={{0,64},{64,0},{1,65},{65,1},{2,66},{66,2},{3,67},{67,3},{4,68},{68... | collective-permute-start | bytes 196616 | tf_op jit(solution)/shard_map/queries/ppermute | solution.py:311
  44.2 1.9 %collective-permute-start.5 = (bf16[128,128]{1,0:T(8,128)(2,1)S(1)}, bf16[128,128]{1,0:T(8,128)(2,1)S(1)}, u32[]{:S(2)}, u32[]{:S(2)}) collective-permute-start(bf16[128,128]{1,0:T(8,128)(2,1)S(1)} %get-tuple-element.22), channel_id=1, source_target_pairs={{0,0},{1,2},{2,4},{3,6},{4,8},{5,10},{6,12},{7,14},{8,1},{9,3},{10... | collective-permute-start | bytes 98312 | tf_op jit(solution)/shard_map/keys_values/ppermute | solution.py:300
  46.1 7.4 %collective-permute-done.5 = bf16[128,128]{1,0:T(8,128)(2,1)S(1)} collective-permute-done((bf16[128,128]{1,0:T(8,128)(2,1)S(1)}, bf16[128,128]{1,0:T(8,128)(2,1)S(1)}, u32[]{:S(2)}, u32[]{:S(2)}) %collective-permute-start.5) | collective-permute-done | bytes 32800 | tf_op jit(solution)/shard_map/keys_values/ppermute | solution.py:300
  53.6 0.7 broadcast_in_dim.27
  54.3 10.9 %all-to-all-start.1 = ((bf16[8,128,128]{2,1,0:T(8,128)(2,1)}), bf16[8,128,128]{2,1,0:T(8,128)(2,1)S(1)}, u32[]{:S(2)}, u32[]{:S(2)}) async-start(bf16[8,128,128]{2,1,0:T(8,128)(2,1)} %broadcast_in_dim.27), calls=%async_computation.1 | async-start | bytes 524288 | tf_op jit(solution)/shard_map/spread_keys_values/all_to_all | solution.py:316
  65.2 1.9 %collective-permute-start.7 = (bf16[256,128]{1,0:T(8,128)(2,1)S(1)}, bf16[256,128]{1,0:T(8,128)(2,1)S(1)}, u32[]{:S(2)}, u32[]{:S(2)}) collective-permute-start(bf16[256,128]{1,0:T(8,128)(2,1)S(1)} %pad_maximum_fusion.3), channel_id=1, source_target_pairs={{0,1},{1,0},{2,3},{3,2},{4,5},{5,4},{6,7},{7,6},{8,9},{9,8},{10,11... | collective-permute-start | bytes 196616 | tf_op jit(solution)/shard_map/share_queries/ppermute | solution.py:319
  67.1 1.2 collective-permute-done.7
  68.4 11.0 %all_gather.3.query_ref = bf16[2048,128]{1,0:T(8,128)(2,1)S(1)} all-gather(bf16[512,128]{1,0:T(8,128)(2,1)S(1)} %pad_maximum_fusion), channel_id=1, replica_groups=mesh['zh'=8,'zp'=2,'x'=4,'y'=8,'c'=2] {'x'}, dimensions={0}, use_global_device_ids=true | all-gather | bytes 655360 | tf_op jit(solution)/shard_map/share_queries/all_gather | solution.py:321
  79.3 3.0 %all-to-all-done.1.own_ref = bf16[8,128,128]{2,1,0:T(8,128)(2,1)S(1)} async-done(((bf16[8,128,128]{2,1,0:T(8,128)(2,1)}), bf16[8,128,128]{2,1,0:T(8,128)(2,1)S(1)}, u32[]{:S(2)}, u32[]{:S(2)}) %all-to-all-start.1) | async-done | bytes 262176 | tf_op jit(solution)/shard_map/spread_keys_values/all_to_all | solution.py:316
  82.3 1.9 %collective-permute-start.8 = (bf16[8,128,128]{2,1,0:T(8,128)(2,1)S(1)}, bf16[8,128,128]{2,1,0:T(8,128)(2,1)S(1)}, u32[]{:S(2)}, u32[]{:S(2)}) collective-permute-start(bf16[8,128,128]{2,1,0:T(8,128)(2,1)S(1)} %all-to-all-done.1.own_ref), channel_id=1, source_target_pairs={{0,1},{1,0},{2,3},{3,2},{4,5},{5,4},{6,7},{7,6},{8,9},{9,8},{10,11... | collective-permute-start | bytes 786440 | tf_op jit(solution)/shard_map/share_queries/ppermute | solution.py:323
  84.3 1.4 %collective-permute-done.8.other_ref = bf16[8,128,128]{2,1,0:T(8,128)(2,1)S(1)} collective-permute-done((bf16[8,128,128]{2,1,0:T(8,128)(2,1)S(1)}, bf16[8,128,128]{2,1,0:T(8,128)(2,1)S(1)}, u32[]{:S(2)}, u32[]{:S(2)}) %collective-permute-start.8) | collective-permute-done | bytes 262176 | tf_op jit(solution)/shard_map/share_queries/ppermute | solution.py:323
  85.7 1.9 %attend.1 = bf16[8,144,256]{2,1,0:T(8,128)(2,1)S(1)} custom-call(s32[4]{0:T(128)S(1)} %pad_add_fusion.place_ref, bf16[2048,128]{1,0:T(8,128)(2,1)S(1)} %all_gather.3.query_ref, bf16[8,128,128]{2,1,0:T(8,128)(2,1)S(1)} %all-to-all-done.1.own_ref, bf16[8,128,128]{2,1,0:T(8,128)(2,1)S(1)} %collective-permute-done.8.other_ref), custom_call_target="tpu_custom_call" | custom-call | flops 1073741824 | bytes 2097152 | tf_op jit(solution)/shard_map/attend/pallas_call | solution.py:326
  87.6 14.2 %all_to_all.20.parts_ref = bf16[8,144,256]{2,1,0:T(8,128)(2,1)S(1)} all-to-all(bf16[8,144,256]{2,1,0:T(8,128)(2,1)S(1)} %attend.1), channel_id=1, replica_groups=mesh['zh'=8,'zp'=2,'x'=4,'y'=8,'c'=2] {'zp','x'}, dimensions={0} | all-to-all | bytes 1179648 | tf_op jit(solution)/shard_map/attend/all_to_all | solution.py:339
  101.8 2.0 %project.1 = bf16[16,64,256]{2,1,0:T(8,128)(2,1)S(1)} custom-call(bf16[8,144,256]{2,1,0:T(8,128)(2,1)S(1)} %all_to_all.20.parts_ref, bf16[256,4096]{1,0:T(8,128)(2,1)S(1)} %copy-done, bf16[64,4096]{1,0:T(8,128)(2,1)} %collective-permute-done.refs_0_, bf16[64,4096]{1,0:T(8,128)(2,1)} %collective-permute-done.1.refs_1_, ...), custom_call_target="tpu_custom_call" | custom-call | flops 268435456 | bytes 5242880 | tf_op jit(solution)/shard_map/project/pallas_call | solution.py:341
  103.8 23.1 %all_to_all.21.parts_ref = bf16[16,64,256]{2,1,0:T(8,128)(2,1)S(1)} all-to-all(bf16[16,64,256]{2,1,0:T(8,128)(2,1)S(1)} %project.1), channel_id=1, replica_groups=mesh['zh'=8,'zp'=2,'x'=4,'y'=8,'c'=2] {'y','c'}, dimensions={0} | all-to-all | bytes 1048576 | tf_op jit(solution)/shard_map/project/all_to_all | solution.py:354
  126.9 1.0 mix.1
  (34 shorter events, 0.3 us)
Async XLA Ops:
  2.0 34.9 %all-to-all-start = ((bf16[16,64,256]{2,1,0:T(8,128)(2,1)}), bf16[16,64,256]{2,1,0:T(8,128)(2,1)S(1)}, u32[]{:S(2)}, u32[]{:S(2)}) async-start(bf16[16,64,256]{2,1,0:T(8,128)(2,1)} %pick.1.after_ref), calls=%async_computation | async-start | bytes 1048576 | tf_op jit(solution)/shard_map/gather_features/all_to_all | solution.py:268
  19.5 11.7 %copy-start.7 = (f32[4096]{0:T(1024)S(1)}, f32[4096]{0:T(1024)}, u32[]{:S(2)}) copy-start(f32[4096]{0:T(1024)} %param.11) | copy-start | bytes 49156
  19.5 11.7 %copy-start.1 = (bf16[16,64,256]{2,1,0:T(8,128)(2,1)S(1)}, bf16[16,64,256]{2,1,0:T(8,128)(2,1)}, u32[]{:S(2)}) copy-start(bf16[16,64,256]{2,1,0:T(8,128)(2,1)} %pick.1.after_ref) | copy-start | bytes 1572868
  19.6 11.7 %copy-start.2 = (bf16[4096,128]{1,0:T(8,128)(2,1)S(1)}, bf16[4096,128]{1,0:T(8,128)(2,1)}, u32[]{:S(2)}) copy-start(bf16[4096,128]{1,0:T(8,128)(2,1)} %weight_ref.4) | copy-start | bytes 3145732
  19.6 11.8 %copy-start.5 = (s32[128]{0:T(128)S(1)}, s32[128]{0:T(128)}, u32[]{:S(2)}) copy-start(s32[128]{0:T(128)} %param.15) | copy-start | bytes 1540
  22.6 9.2 %collective-permute-start.3 = (bf16[64,4096]{1,0:T(8,128)(2,1)}, bf16[64,4096]{1,0:T(8,128)(2,1)S(1)}, u32[]{:S(2)}, u32[]{:S(2)}) collective-permute-start(bf16[64,4096]{1,0:T(8,128)(2,1)} %get-tuple-element.39), channel_id=1, source_target_pairs={{0,1},{1,0},{2,3},{3,2},{4,5},{5,4},{6,7},{7,6},{8,9},{9,8},{10,11... | collective-permute-start | bytes 1572872 | tf_op jit(solution)/shard_map/gather_features/ppermute | solution.py:271
  24.7 7.1 %collective-permute-start.2 = (bf16[64,4096]{1,0:T(8,128)(2,1)}, bf16[64,4096]{1,0:T(8,128)(2,1)S(1)}, u32[]{:S(2)}, u32[]{:S(2)}) collective-permute-start(bf16[64,4096]{1,0:T(8,128)(2,1)} %get-tuple-element.40), channel_id=1, source_target_pairs={{0,1},{1,0},{2,3},{3,2},{4,5},{5,4},{6,7},{7,6},{8,9},{9,8},{10,11... | collective-permute-start | bytes 1572872 | tf_op jit(solution)/shard_map/gather_features/ppermute | solution.py:271
  26.9 4.9 %collective-permute-start.1 = (bf16[64,4096]{1,0:T(8,128)(2,1)}, bf16[64,4096]{1,0:T(8,128)(2,1)}, u32[]{:S(2)}, u32[]{:S(2)}) collective-permute-start(bf16[64,4096]{1,0:T(8,128)(2,1)} %get-tuple-element.41), channel_id=1, source_target_pairs={{0,1},{1,0},{2,3},{3,2},{4,5},{5,4},{6,7},{7,6},{8,9},{9,8},{10,11... | collective-permute-start | bytes 1572872 | tf_op jit(solution)/shard_map/gather_features/ppermute | solution.py:271
  29.0 4.1 %collective-permute-start = (bf16[64,4096]{1,0:T(8,128)(2,1)}, bf16[64,4096]{1,0:T(8,128)(2,1)}, u32[]{:S(2)}, u32[]{:S(2)}) collective-permute-start(bf16[64,4096]{1,0:T(8,128)(2,1)} %get-tuple-element.42), channel_id=1, source_target_pairs={{0,1},{1,0},{2,3},{3,2},{4,5},{5,4},{6,7},{7,6},{8,9},{9,8},{10,11... | collective-permute-start | bytes 1572872 | tf_op jit(solution)/shard_map/gather_features/ppermute | solution.py:271
  36.9 4.8 %copy-start.3 = (bf16[4096,256]{1,0:T(8,128)(2,1)S(1)}, bf16[4096,256]{1,0:T(8,128)(2,1)}, u32[]{:S(2)}) copy-start(bf16[4096,256]{1,0:T(8,128)(2,1)} %weight_ref.5) | copy-start | bytes 6291460
  36.9 3.9 %collective-permute-start.4 = (bf16[16,64,256]{2,1,0:T(8,128)(2,1)S(1)}, bf16[16,64,256]{2,1,0:T(8,128)(2,1)S(1)}, u32[]{:S(2)}, u32[]{:S(2)}) collective-permute-start(bf16[16,64,256]{2,1,0:T(8,128)(2,1)S(1)} %all-to-all-done.own_ref), channel_id=1, source_target_pairs={{0,1},{1,0},{2,3},{3,2},{4,5},{5,4},{6,7},{7,6},{8,9},{9,8},{10,11... | collective-permute-start | bytes 1572872 | tf_op jit(solution)/shard_map/gather_features/ppermute | solution.py:274
  42.3 11.3 %collective-permute-start.6 = (bf16[256,128]{1,0:T(8,128)(2,1)S(1)}, bf16[256,128]{1,0:T(8,128)(2,1)S(1)}, u32[]{:S(2)}, u32[]{:S(2)}) collective-permute-start(bf16[256,128]{1,0:T(8,128)(2,1)S(1)} %constant_dynamic-update-slice_fusion), channel_id=1, source_target_pairs={{0,64},{64,0},{1,65},{65,1},{2,66},{66,2},{3,67},{67,3},{4,68},{68... | collective-permute-start | bytes 196616 | tf_op jit(solution)/shard_map/queries/ppermute | solution.py:311
  44.2 9.3 %collective-permute-start.5 = (bf16[128,128]{1,0:T(8,128)(2,1)S(1)}, bf16[128,128]{1,0:T(8,128)(2,1)S(1)}, u32[]{:S(2)}, u32[]{:S(2)}) collective-permute-start(bf16[128,128]{1,0:T(8,128)(2,1)S(1)} %get-tuple-element.22), channel_id=1, source_target_pairs={{0,0},{1,2},{2,4},{3,6},{4,8},{5,10},{6,12},{7,14},{8,1},{9,3},{10... | collective-permute-start | bytes 98312 | tf_op jit(solution)/shard_map/keys_values/ppermute | solution.py:300
  54.3 28.0 %all-to-all-start.1 = ((bf16[8,128,128]{2,1,0:T(8,128)(2,1)}), bf16[8,128,128]{2,1,0:T(8,128)(2,1)S(1)}, u32[]{:S(2)}, u32[]{:S(2)}) async-start(bf16[8,128,128]{2,1,0:T(8,128)(2,1)} %broadcast_in_dim.27), calls=%async_computation.1 | async-start | bytes 524288 | tf_op jit(solution)/shard_map/spread_keys_values/all_to_all | solution.py:316
  65.2 3.1 %collective-permute-start.7 = (bf16[256,128]{1,0:T(8,128)(2,1)S(1)}, bf16[256,128]{1,0:T(8,128)(2,1)S(1)}, u32[]{:S(2)}, u32[]{:S(2)}) collective-permute-start(bf16[256,128]{1,0:T(8,128)(2,1)S(1)} %pad_maximum_fusion.3), channel_id=1, source_target_pairs={{0,1},{1,0},{2,3},{3,2},{4,5},{5,4},{6,7},{7,6},{8,9},{9,8},{10,11... | collective-permute-start | bytes 196616 | tf_op jit(solution)/shard_map/share_queries/ppermute | solution.py:319
  82.3 3.4 %collective-permute-start.8 = (bf16[8,128,128]{2,1,0:T(8,128)(2,1)S(1)}, bf16[8,128,128]{2,1,0:T(8,128)(2,1)S(1)}, u32[]{:S(2)}, u32[]{:S(2)}) collective-permute-start(bf16[8,128,128]{2,1,0:T(8,128)(2,1)S(1)} %all-to-all-done.1.own_ref), channel_id=1, source_target_pairs={{0,1},{1,0},{2,3},{3,2},{4,5},{5,4},{6,7},{7,6},{8,9},{9,8},{10,11... | collective-permute-start | bytes 786440 | tf_op jit(solution)/shard_map/share_queries/ppermute | solution.py:323
  84.3 17.5 %copy-start = (bf16[256,4096]{1,0:T(8,128)(2,1)S(1)}, bf16[256,4096]{1,0:T(8,128)(2,1)}, u32[]{:S(2)}) copy-start(bf16[256,4096]{1,0:T(8,128)(2,1)} %own_ref.1) | copy-start | bytes 6291460
  101.8 25.1 %copy-start.4 = (bf16[512,256]{1,0:T(8,128)(2,1)S(1)}, bf16[512,256]{1,0:T(8,128)(2,1)}, u32[]{:S(2)}) copy-start(bf16[512,256]{1,0:T(8,128)(2,1)} %hidden_ref.3) | copy-start | bytes 786436
  101.8 25.1 %copy-start.6 = (f32[512]{0:T(512)S(1)}, f32[512]{0:T(512)}, u32[]{:S(2)}) copy-start(f32[512]{0:T(512)} %param.10) | copy-start | bytes 6148

commit v4 on v3

--- a/solution.py
+++ b/solution.py
@@ -99,6 +99,11 @@
     kv_ref[...] = (turn(total, cos_ref[...], sin_ref[...]) + mark_ref[...]).astype(jnp.bfloat16)
 
 
+def lay_kernel(kv_ref, out_ref):
+    for t in range(ZH):
+        out_ref[t] = kv_ref[...]
+
+
 def query_kernel(core_ref, normed_ref, cos_ref, sin_ref, weight_ref, mine_ref, theirs_ref):
     core = core_ref[0]
     total = dot(normed_ref[...], weight_ref[...], ((1,), (0,)))
@@ -298,6 +303,7 @@
         )(core_at, own_rows, other_rows, norm_gain.reshape(N_MP, WIDTH), cos_kv, sin_kv, mark, kv_weight, touched)
         to_heads = [(m, 2 * m if m < Y else 2 * (m - Y) + 1) for m in range(N_MP)]
         kv = lax.ppermute(kv, MP, to_heads)
+        kv = call(lay_kernel, shape((ZH, CAP, HEAD_DIM)), 1, flops=1 << 35, nbytes=64 << 20)(kv)
     with jax.named_scope("queries"):
         mine, theirs = call(
             query_kernel,
@@ -309,10 +315,8 @@
         )(core_at, normed, cos_q, sin_q, query_weight)
         both = jnp.concatenate([mine, theirs], axis=0)
         swapped = lax.ppermute(both, "zp", swap)
-        kv, swapped = lax.optimization_barrier((kv, swapped))
+        kv, both = lax.optimization_barrier((kv, both))
     with jax.named_scope("spread_keys_values"):
-        kv = jnp.broadcast_to(kv[None], (ZH, CAP, HEAD_DIM))
-        kv, both, swapped = lax.optimization_barrier((kv, both, swapped))
         own = lax.all_to_all(kv, "zh", 0, 0, tiled=True)
     with jax.named_scope("share_queries"):
         half = HEADS * HALF

time: 129 us -> 126 us (0.977)
  waiting for transfers between devices: 19.8 us -> 16.5 us
  blocking collectives: 48.2 us -> 50.3 us
    ppermute x1, waiting for transfers between devices: 7.41 us -> 5.46 us  [local(): kv = lax.ppermute(kv, MP, to_heads)]
    all_to_all x1, blocking collectives: 14.2 us -> 15.6 us  [local(): parts = lax.all_to_all(parts, NEAR, 0, 0, tiled=True)]
    all_to_all x1, starting transfers between devices: 10.9 us -> 9.53 us  [local(): own = lax.all_to_all(kv, 'zh', 0, 0, tiled=True)]
  transfers between devices with their start and end apart: 11 -> 11, of which waited for: 7 -> 7; matrix products, arithmetic and copies ran while one was open for 3% -> 3% of each run, Pallas kernels for 0% -> 1%
where the time goes in v4:
time: 126 us
  blocking collectives  50.3 us (40%)
  starting transfers between devices  45.8 us (36%)
  waiting for transfers between devices  16.5 us (13%)
  Pallas kernels  9.11 us (7%)
  local copies, waits for them, and re-layouts  3.06 us (2%)
    all_to_all x1, blocking collectives, local(): partial = lax.all_to_all(partial, MP, 0, 0, tiled=True)  23.7 us
    all_to_all x1, starting transfers between devices, local(): own_rows = lax.all_to_all(picked, MP, 0, 0, tiled=True)  17.5 us
    all_to_all x1, blocking collectives, local(): parts = lax.all_to_all(parts, NEAR, 0, 0, tiled=True)  15.6 us
    all_gather x1, blocking collectives, local(): queries = lax.all_gather(queries, 'x', axis=0, tiled=True)  11 us
    all_to_all x1, starting transfers between devices, local(): own = lax.all_to_all(kv, 'zh', 0, 0, tiled=True)  9.53 us
    ppermute x4, starting transfers between devices, local(): lax.ppermute(out_weight[i * deep:(i + 1) * deep], 'c', swap)  8.64 us
    ppermute x1, waiting for transfers between devices, local(): kv = lax.ppermute(kv, MP, to_heads)  5.46 us
    all_to_all x1, waiting for transfers between devices, local(): own_rows = lax.all_to_all(picked, MP, 0, 0, tiled=True)  3.7 us
  transfers between devices with their start and end apart: 11, of which 7 were waited for; matrix products, arithmetic and copies ran while one was open for 3% of the time, Pallas kernels for 1%

profile of v4, /device:TPU:1, one launch (start us, length us, event | category | flops | bytes accessed | tf_op | source)
XLA Modules:
  0.0 125.8 jit_solution(3504777506844857974)
XLA Ops:
  0.0 2.0 %pick.1.after_ref = bf16[16,64,256]{2,1,0:T(8,128)(2,1)} custom-call(s32[1,128]{1,0:T(1,128)} %bitcast.6, bf16[512,256]{1,0:T(8,128)(2,1)} %hidden_ref.3), custom_call_target="tpu_custom_call" | custom-call | tf_op jit(solution)/shard_map/pick/pallas_call | solution.py:271
  2.0 17.5 %all-to-all-start = ((bf16[16,64,256]{2,1,0:T(8,128)(2,1)}), bf16[16,64,256]{2,1,0:T(8,128)(2,1)S(1)}, u32[]{:S(2)}, u32[]{:S(2)}) async-start(bf16[16,64,256]{2,1,0:T(8,128)(2,1)} %pick.1.after_ref), calls=%async_computation | async-start | bytes 1048576 | tf_op jit(solution)/shard_map/gather_features/all_to_all | solution.py:273
  19.6 3.0 %fusion.1 = (bf16[64,4096]{1,0:T(8,128)(2,1)}, bf16[64,4096]{1,0:T(8,128)(2,1)}, bf16[64,4096]{1,0:T(8,128)(2,1)}, bf16[64,4096]{1,0:T(8,128)(2,1)}) fusion(bf16[256,4096]{1,0:T(8,128)(2,1)} %own_ref.1), kind=kLoop, calls=%fused_computation.17 | loop fusion | bytes 4194304 | tf_op jit(solution)/shard_map/gather_features/slice | solution.py:276
  22.6 2.1 %collective-permute-start.3 = (bf16[64,4096]{1,0:T(8,128)(2,1)}, bf16[64,4096]{1,0:T(8,128)(2,1)S(1)}, u32[]{:S(2)}, u32[]{:S(2)}) collective-permute-start(bf16[64,4096]{1,0:T(8,128)(2,1)} %get-tuple-element.33), channel_id=1, source_target_pairs={{0,1},{1,0},{2,3},{3,2},{4,5},{5,4},{6,7},{7,6},{8,9},{9,8},{10,11... | collective-permute-start | bytes 1572872 | tf_op jit(solution)/shard_map/gather_features/ppermute | solution.py:276
  24.7 2.2 %collective-permute-start.2 = (bf16[64,4096]{1,0:T(8,128)(2,1)}, bf16[64,4096]{1,0:T(8,128)(2,1)S(1)}, u32[]{:S(2)}, u32[]{:S(2)}) collective-permute-start(bf16[64,4096]{1,0:T(8,128)(2,1)} %get-tuple-element.34), channel_id=1, source_target_pairs={{0,1},{1,0},{2,3},{3,2},{4,5},{5,4},{6,7},{7,6},{8,9},{9,8},{10,11... | collective-permute-start | bytes 1572872 | tf_op jit(solution)/shard_map/gather_features/ppermute | solution.py:276
  26.9 2.1 %collective-permute-start.1 = (bf16[64,4096]{1,0:T(8,128)(2,1)}, bf16[64,4096]{1,0:T(8,128)(2,1)}, u32[]{:S(2)}, u32[]{:S(2)}) collective-permute-start(bf16[64,4096]{1,0:T(8,128)(2,1)} %get-tuple-element.35), channel_id=1, source_target_pairs={{0,1},{1,0},{2,3},{3,2},{4,5},{5,4},{6,7},{7,6},{8,9},{9,8},{10,11... | collective-permute-start | bytes 1572872 | tf_op jit(solution)/shard_map/gather_features/ppermute | solution.py:276
  29.0 2.2 %collective-permute-start = (bf16[64,4096]{1,0:T(8,128)(2,1)}, bf16[64,4096]{1,0:T(8,128)(2,1)}, u32[]{:S(2)}, u32[]{:S(2)}) collective-permute-start(bf16[64,4096]{1,0:T(8,128)(2,1)} %get-tuple-element.36), channel_id=1, source_target_pairs={{0,1},{1,0},{2,3},{3,2},{4,5},{5,4},{6,7},{7,6},{8,9},{9,8},{10,11... | collective-permute-start | bytes 1572872 | tf_op jit(solution)/shard_map/gather_features/ppermute | solution.py:276
  31.4 0.3 fusion
  31.7 0.1 pad_maximum_fusion.1
  31.8 1.4 %collective-permute-done.refs_0_ = bf16[64,4096]{1,0:T(8,128)(2,1)} collective-permute-done((bf16[64,4096]{1,0:T(8,128)(2,1)}, bf16[64,4096]{1,0:T(8,128)(2,1)}, u32[]{:S(2)}, u32[]{:S(2)}) %collective-permute-start) | collective-permute-done | bytes 524320 | tf_op jit(solution)/shard_map/gather_features/ppermute | solution.py:276
  33.2 3.7 %all-to-all-done.own_ref = bf16[16,64,256]{2,1,0:T(8,128)(2,1)S(1)} async-done(((bf16[16,64,256]{2,1,0:T(8,128)(2,1)}), bf16[16,64,256]{2,1,0:T(8,128)(2,1)S(1)}, u32[]{:S(2)}, u32[]{:S(2)}) %all-to-all-start) | async-done | bytes 524320 | tf_op jit(solution)/shard_map/gather_features/all_to_all | solution.py:273
  36.9 2.0 %collective-permute-start.4 = (bf16[16,64,256]{2,1,0:T(8,128)(2,1)S(1)}, bf16[16,64,256]{2,1,0:T(8,128)(2,1)S(1)}, u32[]{:S(2)}, u32[]{:S(2)}) collective-permute-start(bf16[16,64,256]{2,1,0:T(8,128)(2,1)S(1)} %all-to-all-done.own_ref), channel_id=1, source_target_pairs={{0,1},{1,0},{2,3},{3,2},{4,5},{5,4},{6,7},{7,6},{8,9},{9,8},{10,11... | collective-permute-start | bytes 1572872 | tf_op jit(solution)/shard_map/gather_features/ppermute | solution.py:279
  38.9 0.1 broadcast_select_fusion
  39.1 1.7 %collective-permute-done.4.other_ref = bf16[16,64,256]{2,1,0:T(8,128)(2,1)S(1)} collective-permute-done((bf16[16,64,256]{2,1,0:T(8,128)(2,1)S(1)}, bf16[16,64,256]{2,1,0:T(8,128)(2,1)S(1)}, u32[]{:S(2)}, u32[]{:S(2)}) %collective-permute-start.4) | collective-permute-done | bytes 524320 | tf_op jit(solution)/shard_map/gather_features/ppermute | solution.py:279
  40.8 0.9 keys_values.2
  41.7 0.6 queries.1
  42.3 1.9 %collective-permute-start.5 = (bf16[128,128]{1,0:T(8,128)(2,1)S(1)}, bf16[128,128]{1,0:T(8,128)(2,1)S(1)}, u32[]{:S(2)}, u32[]{:S(2)}) collective-permute-start(bf16[128,128]{1,0:T(8,128)(2,1)S(1)} %get-tuple-element.19), channel_id=1, source_target_pairs={{0,0},{1,2},{2,4},{3,6},{4,8},{5,10},{6,12},{7,14},{8,1},{9,3},{10... | collective-permute-start | bytes 98312 | tf_op jit(solution)/shard_map/keys_values/ppermute | solution.py:305
  44.2 1.9 %collective-permute-start.6 = (bf16[256,128]{1,0:T(8,128)(2,1)S(1)}, bf16[256,128]{1,0:T(8,128)(2,1)S(1)}, u32[]{:S(2)}, u32[]{:S(2)}) collective-permute-start(bf16[256,128]{1,0:T(8,128)(2,1)S(1)} %constant_dynamic-update-slice_fusion), channel_id=1, source_target_pairs={{0,64},{64,0},{1,65},{65,1},{2,66},{66,2},{3,67},{67,3},{4,68},{68... | collective-permute-start | bytes 196616 | tf_op jit(solution)/shard_map/queries/ppermute | solution.py:317
  46.1 5.5 %collective-permute-done.5.kv_ref = bf16[128,128]{1,0:T(8,128)(2,1)S(1)} collective-permute-done((bf16[128,128]{1,0:T(8,128)(2,1)S(1)}, bf16[128,128]{1,0:T(8,128)(2,1)S(1)}, u32[]{:S(2)}, u32[]{:S(2)}) %collective-permute-start.5) | collective-permute-done | bytes 32800 | tf_op jit(solution)/shard_map/keys_values/ppermute | solution.py:305
  51.6 0.7 keys_values.3
  52.3 9.5 %all-to-all-start.1 = ((bf16[8,128,128]{2,1,0:T(8,128)(2,1)}), bf16[8,128,128]{2,1,0:T(8,128)(2,1)S(1)}, u32[]{:S(2)}, u32[]{:S(2)}) async-start(bf16[8,128,128]{2,1,0:T(8,128)(2,1)} %keys_values.3), calls=%async_computation.1 | async-start | bytes 524288 | tf_op jit(solution)/shard_map/spread_keys_values/all_to_all | solution.py:320
  61.9 1.9 %collective-permute-start.7 = (bf16[256,128]{1,0:T(8,128)(2,1)S(1)}, bf16[256,128]{1,0:T(8,128)(2,1)S(1)}, u32[]{:S(2)}, u32[]{:S(2)}) collective-permute-start(bf16[256,128]{1,0:T(8,128)(2,1)S(1)} %pad_maximum_fusion.3), channel_id=1, source_target_pairs={{0,1},{1,0},{2,3},{3,2},{4,5},{5,4},{6,7},{7,6},{8,9},{9,8},{10,11... | collective-permute-start | bytes 196616 | tf_op jit(solution)/shard_map/share_queries/ppermute | solution.py:323
  63.9 1.2 collective-permute-done.7
  65.1 11.0 %all_gather.3.query_ref = bf16[2048,128]{1,0:T(8,128)(2,1)S(1)} all-gather(bf16[512,128]{1,0:T(8,128)(2,1)S(1)} %pad_maximum_fusion), channel_id=1, replica_groups=mesh['zh'=8,'zp'=2,'x'=4,'y'=8,'c'=2] {'x'}, dimensions={0}, use_global_device_ids=true | all-gather | bytes 655360 | tf_op jit(solution)/shard_map/share_queries/all_gather | solution.py:325
  76.1 2.0 %all-to-all-done.1.own_ref = bf16[8,128,128]{2,1,0:T(8,128)(2,1)S(1)} async-done(((bf16[8,128,128]{2,1,0:T(8,128)(2,1)}), bf16[8,128,128]{2,1,0:T(8,128)(2,1)S(1)}, u32[]{:S(2)}, u32[]{:S(2)}) %all-to-all-start.1) | async-done | bytes 262176 | tf_op jit(solution)/shard_map/spread_keys_values/all_to_all | solution.py:320
  78.0 2.4 %collective-permute-start.8 = (bf16[8,128,128]{2,1,0:T(8,128)(2,1)S(1)}, bf16[8,128,128]{2,1,0:T(8,128)(2,1)S(1)}, u32[]{:S(2)}, u32[]{:S(2)}) collective-permute-start(bf16[8,128,128]{2,1,0:T(8,128)(2,1)S(1)} %all-to-all-done.1.own_ref), channel_id=1, source_target_pairs={{0,1},{1,0},{2,3},{3,2},{4,5},{5,4},{6,7},{7,6},{8,9},{9,8},{10,11... | collective-permute-start | bytes 786440 | tf_op jit(solution)/shard_map/share_queries/ppermute | solution.py:327
  80.5 1.1 collective-permute-done.8.other_ref
  81.5 1.9 %attend.1 = bf16[8,144,256]{2,1,0:T(8,128)(2,1)S(1)} custom-call(s32[4]{0:T(128)S(1)} %pad_add_fusion.place_ref, bf16[2048,128]{1,0:T(8,128)(2,1)S(1)} %all_gather.3.query_ref, bf16[8,128,128]{2,1,0:T(8,128)(2,1)S(1)} %all-to-all-done.1.own_ref, bf16[8,128,128]{2,1,0:T(8,128)(2,1)S(1)} %collective-permute-done.8.other_ref), custom_call_target="tpu_custom_call" | custom-call | flops 1073741824 | bytes 2097152 | tf_op jit(solution)/shard_map/attend/pallas_call | solution.py:330
  83.4 15.6 %all_to_all.20.parts_ref = bf16[8,144,256]{2,1,0:T(8,128)(2,1)S(1)} all-to-all(bf16[8,144,256]{2,1,0:T(8,128)(2,1)S(1)} %attend.1), channel_id=1, replica_groups=mesh['zh'=8,'zp'=2,'x'=4,'y'=8,'c'=2] {'zp','x'}, dimensions={0} | all-to-all | bytes 1179648 | tf_op jit(solution)/shard_map/attend/all_to_all | solution.py:343
  99.0 2.0 %project.1 = bf16[16,64,256]{2,1,0:T(8,128)(2,1)S(1)} custom-call(bf16[8,144,256]{2,1,0:T(8,128)(2,1)S(1)} %all_to_all.20.parts_ref, bf16[256,4096]{1,0:T(8,128)(2,1)S(1)} %copy-done, bf16[64,4096]{1,0:T(8,128)(2,1)} %collective-permute-done.refs_0_, bf16[64,4096]{1,0:T(8,128)(2,1)} %collective-permute-done.1.refs_1_, ...), custom_call_target="tpu_custom_call" | custom-call | flops 268435456 | bytes 5242880 | tf_op jit(solution)/shard_map/project/pallas_call | solution.py:345
  101.0 23.7 %all_to_all.21.parts_ref = bf16[16,64,256]{2,1,0:T(8,128)(2,1)S(1)} all-to-all(bf16[16,64,256]{2,1,0:T(8,128)(2,1)S(1)} %project.1), channel_id=1, replica_groups=mesh['zh'=8,'zp'=2,'x'=4,'y'=8,'c'=2] {'y','c'}, dimensions={0} | all-to-all | bytes 1048576 | tf_op jit(solution)/shard_map/project/all_to_all | solution.py:358
  124.7 1.0 mix.1
  (34 shorter events, 0.3 us)
Async XLA Ops:
  2.0 34.9 %all-to-all-start = ((bf16[16,64,256]{2,1,0:T(8,128)(2,1)}), bf16[16,64,256]{2,1,0:T(8,128)(2,1)S(1)}, u32[]{:S(2)}, u32[]{:S(2)}) async-start(bf16[16,64,256]{2,1,0:T(8,128)(2,1)} %pick.1.after_ref), calls=%async_computation | async-start | bytes 1048576 | tf_op jit(solution)/shard_map/gather_features/all_to_all | solution.py:273
  19.5 11.7 %copy-start.7 = (f32[4096]{0:T(1024)S(1)}, f32[4096]{0:T(1024)}, u32[]{:S(2)}) copy-start(f32[4096]{0:T(1024)} %param.11) | copy-start | bytes 49156
  19.5 11.7 %copy-start.1 = (bf16[16,64,256]{2,1,0:T(8,128)(2,1)S(1)}, bf16[16,64,256]{2,1,0:T(8,128)(2,1)}, u32[]{:S(2)}) copy-start(bf16[16,64,256]{2,1,0:T(8,128)(2,1)} %pick.1.after_ref) | copy-start | bytes 1572868
  19.6 11.7 %copy-start.2 = (bf16[4096,128]{1,0:T(8,128)(2,1)S(1)}, bf16[4096,128]{1,0:T(8,128)(2,1)}, u32[]{:S(2)}) copy-start(bf16[4096,128]{1,0:T(8,128)(2,1)} %weight_ref.4) | copy-start | bytes 3145732
  19.6 11.8 %copy-start.5 = (s32[128]{0:T(128)S(1)}, s32[128]{0:T(128)}, u32[]{:S(2)}) copy-start(s32[128]{0:T(128)} %param.15) | copy-start | bytes 1540
  22.6 9.2 %collective-permute-start.3 = (bf16[64,4096]{1,0:T(8,128)(2,1)}, bf16[64,4096]{1,0:T(8,128)(2,1)S(1)}, u32[]{:S(2)}, u32[]{:S(2)}) collective-permute-start(bf16[64,4096]{1,0:T(8,128)(2,1)} %get-tuple-element.33), channel_id=1, source_target_pairs={{0,1},{1,0},{2,3},{3,2},{4,5},{5,4},{6,7},{7,6},{8,9},{9,8},{10,11... | collective-permute-start | bytes 1572872 | tf_op jit(solution)/shard_map/gather_features/ppermute | solution.py:276
  24.7 7.1 %collective-permute-start.2 = (bf16[64,4096]{1,0:T(8,128)(2,1)}, bf16[64,4096]{1,0:T(8,128)(2,1)S(1)}, u32[]{:S(2)}, u32[]{:S(2)}) collective-permute-start(bf16[64,4096]{1,0:T(8,128)(2,1)} %get-tuple-element.34), channel_id=1, source_target_pairs={{0,1},{1,0},{2,3},{3,2},{4,5},{5,4},{6,7},{7,6},{8,9},{9,8},{10,11... | collective-permute-start | bytes 1572872 | tf_op jit(solution)/shard_map/gather_features/ppermute | solution.py:276
  26.9 4.9 %collective-permute-start.1 = (bf16[64,4096]{1,0:T(8,128)(2,1)}, bf16[64,4096]{1,0:T(8,128)(2,1)}, u32[]{:S(2)}, u32[]{:S(2)}) collective-permute-start(bf16[64,4096]{1,0:T(8,128)(2,1)} %get-tuple-element.35), channel_id=1, source_target_pairs={{0,1},{1,0},{2,3},{3,2},{4,5},{5,4},{6,7},{7,6},{8,9},{9,8},{10,11... | collective-permute-start | bytes 1572872 | tf_op jit(solution)/shard_map/gather_features/ppermute | solution.py:276
  29.0 4.1 %collective-permute-start = (bf16[64,4096]{1,0:T(8,128)(2,1)}, bf16[64,4096]{1,0:T(8,128)(2,1)}, u32[]{:S(2)}, u32[]{:S(2)}) collective-permute-start(bf16[64,4096]{1,0:T(8,128)(2,1)} %get-tuple-element.36), channel_id=1, source_target_pairs={{0,1},{1,0},{2,3},{3,2},{4,5},{5,4},{6,7},{7,6},{8,9},{9,8},{10,11... | collective-permute-start | bytes 1572872 | tf_op jit(solution)/shard_map/gather_features/ppermute | solution.py:276
  36.9 4.8 %copy-start.3 = (bf16[4096,256]{1,0:T(8,128)(2,1)S(1)}, bf16[4096,256]{1,0:T(8,128)(2,1)}, u32[]{:S(2)}) copy-start(bf16[4096,256]{1,0:T(8,128)(2,1)} %weight_ref.5) | copy-start | bytes 6291460
  36.9 3.9 %collective-permute-start.4 = (bf16[16,64,256]{2,1,0:T(8,128)(2,1)S(1)}, bf16[16,64,256]{2,1,0:T(8,128)(2,1)S(1)}, u32[]{:S(2)}, u32[]{:S(2)}) collective-permute-start(bf16[16,64,256]{2,1,0:T(8,128)(2,1)S(1)} %all-to-all-done.own_ref), channel_id=1, source_target_pairs={{0,1},{1,0},{2,3},{3,2},{4,5},{5,4},{6,7},{7,6},{8,9},{9,8},{10,11... | collective-permute-start | bytes 1572872 | tf_op jit(solution)/shard_map/gather_features/ppermute | solution.py:279
  42.3 9.3 %collective-permute-start.5 = (bf16[128,128]{1,0:T(8,128)(2,1)S(1)}, bf16[128,128]{1,0:T(8,128)(2,1)S(1)}, u32[]{:S(2)}, u32[]{:S(2)}) collective-permute-start(bf16[128,128]{1,0:T(8,128)(2,1)S(1)} %get-tuple-element.19), channel_id=1, source_target_pairs={{0,0},{1,2},{2,4},{3,6},{4,8},{5,10},{6,12},{7,14},{8,1},{9,3},{10... | collective-permute-start | bytes 98312 | tf_op jit(solution)/shard_map/keys_values/ppermute | solution.py:305
  44.2 17.7 %collective-permute-start.6 = (bf16[256,128]{1,0:T(8,128)(2,1)S(1)}, bf16[256,128]{1,0:T(8,128)(2,1)S(1)}, u32[]{:S(2)}, u32[]{:S(2)}) collective-permute-start(bf16[256,128]{1,0:T(8,128)(2,1)S(1)} %constant_dynamic-update-slice_fusion), channel_id=1, source_target_pairs={{0,64},{64,0},{1,65},{65,1},{2,66},{66,2},{3,67},{67,3},{4,68},{68... | collective-permute-start | bytes 196616 | tf_op jit(solution)/shard_map/queries/ppermute | solution.py:317
  52.3 25.7 %all-to-all-start.1 = ((bf16[8,128,128]{2,1,0:T(8,128)(2,1)}), bf16[8,128,128]{2,1,0:T(8,128)(2,1)S(1)}, u32[]{:S(2)}, u32[]{:S(2)}) async-start(bf16[8,128,128]{2,1,0:T(8,128)(2,1)} %keys_values.3), calls=%async_computation.1 | async-start | bytes 524288 | tf_op jit(solution)/shard_map/spread_keys_values/all_to_all | solution.py:320
  61.9 3.1 %collective-permute-start.7 = (bf16[256,128]{1,0:T(8,128)(2,1)S(1)}, bf16[256,128]{1,0:T(8,128)(2,1)S(1)}, u32[]{:S(2)}, u32[]{:S(2)}) collective-permute-start(bf16[256,128]{1,0:T(8,128)(2,1)S(1)} %pad_maximum_fusion.3), channel_id=1, source_target_pairs={{0,1},{1,0},{2,3},{3,2},{4,5},{5,4},{6,7},{7,6},{8,9},{9,8},{10,11... | collective-permute-start | bytes 196616 | tf_op jit(solution)/shard_map/share_queries/ppermute | solution.py:323
  78.0 3.5 %collective-permute-start.8 = (bf16[8,128,128]{2,1,0:T(8,128)(2,1)S(1)}, bf16[8,128,128]{2,1,0:T(8,128)(2,1)S(1)}, u32[]{:S(2)}, u32[]{:S(2)}) collective-permute-start(bf16[8,128,128]{2,1,0:T(8,128)(2,1)S(1)} %all-to-all-done.1.own_ref), channel_id=1, source_target_pairs={{0,1},{1,0},{2,3},{3,2},{4,5},{5,4},{6,7},{7,6},{8,9},{9,8},{10,11... | collective-permute-start | bytes 786440 | tf_op jit(solution)/shard_map/share_queries/ppermute | solution.py:327
  80.5 18.5 %copy-start = (bf16[256,4096]{1,0:T(8,128)(2,1)S(1)}, bf16[256,4096]{1,0:T(8,128)(2,1)}, u32[]{:S(2)}) copy-start(bf16[256,4096]{1,0:T(8,128)(2,1)} %own_ref.1) | copy-start | bytes 6291460
  99.0 25.7 %copy-start.4 = (bf16[512,256]{1,0:T(8,128)(2,1)S(1)}, bf16[512,256]{1,0:T(8,128)(2,1)}, u32[]{:S(2)}) copy-start(bf16[512,256]{1,0:T(8,128)(2,1)} %hidden_ref.3) | copy-start | bytes 786436
  99.0 25.7 %copy-start.6 = (f32[512]{0:T(512)S(1)}, f32[512]{0:T(512)}, u32[]{:S(2)}) copy-start(f32[512]{0:T(512)} %param.10) | copy-start | bytes 6148

commit v5 on v4

--- a/solution.py
+++ b/solution.py
@@ -315,7 +315,6 @@
         )(core_at, normed, cos_q, sin_q, query_weight)
         both = jnp.concatenate([mine, theirs], axis=0)
         swapped = lax.ppermute(both, "zp", swap)
-        kv, both = lax.optimization_barrier((kv, both))
     with jax.named_scope("spread_keys_values"):
         own = lax.all_to_all(kv, "zh", 0, 0, tiled=True)
     with jax.named_scope("share_queries"):

time: 126 us -> 126 us (level)
    all_to_all x1, waiting for transfers between devices: 1.95 us -> 3.33 us  [local(): own = lax.all_to_all(kv, 'zh', 0, 0, tiled=True)]
    all_to_all x1, blocking collectives: 15.6 us -> 14.3 us  [local(): parts = lax.all_to_all(parts, NEAR, 0, 0, tiled=True)]
where the time goes in v5:
time: 126 us; the launch traced here: 125 us
  blocking collectives  49.2 us (39%)
  starting transfers between devices  45.4 us (36%)
  waiting for transfers between devices  17.6 us (14%)
  Pallas kernels  9.09 us (7%)
  local copies, waits for them, and re-layouts  3.05 us (2%)
    all_to_all x1, blocking collectives, local(): partial = lax.all_to_all(partial, MP, 0, 0, tiled=True)  24 us
    all_to_all x1, starting transfers between devices, local(): own_rows = lax.all_to_all(picked, MP, 0, 0, tiled=True)  17.5 us
    all_to_all x1, blocking collectives, local(): parts = lax.all_to_all(parts, NEAR, 0, 0, tiled=True)  14.3 us
    all_gather x1, blocking collectives, local(): queries = lax.all_gather(queries, 'x', axis=0, tiled=True)  11 us
    all_to_all x1, starting transfers between devices, local(): own = lax.all_to_all(kv, 'zh', 0, 0, tiled=True)  9.55 us
    ppermute x4, starting transfers between devices, local(): lax.ppermute(out_weight[i * deep:(i + 1) * deep], 'c', swap)  8.64 us
    ppermute x1, waiting for transfers between devices, local(): kv = lax.ppermute(kv, MP, to_heads)  4.89 us
    all_to_all x1, waiting for transfers between devices, local(): own_rows = lax.all_to_all(picked, MP, 0, 0, tiled=True)  3.69 us
  transfers between devices with their start and end apart: 11, of which 7 were waited for; matrix products, arithmetic and copies ran while one was open for 3% of the time, Pallas kernels for 1%

profile of v5, /device:TPU:1, one launch (start us, length us, event | category | flops | bytes accessed | tf_op | source)
XLA Modules:
  0.0 125.4 jit_solution(16381043160223410035)
XLA Ops:
  0.0 2.0 %pick.1.after_ref = bf16[16,64,256]{2,1,0:T(8,128)(2,1)} custom-call(s32[1,128]{1,0:T(1,128)} %bitcast.6, bf16[512,256]{1,0:T(8,128)(2,1)} %hidden_ref.3), custom_call_target="tpu_custom_call" | custom-call | tf_op jit(solution)/shard_map/pick/pallas_call | solution.py:271
  2.0 17.5 %all-to-all-start = ((bf16[16,64,256]{2,1,0:T(8,128)(2,1)}), bf16[16,64,256]{2,1,0:T(8,128)(2,1)S(1)}, u32[]{:S(2)}, u32[]{:S(2)}) async-start(bf16[16,64,256]{2,1,0:T(8,128)(2,1)} %pick.1.after_ref), calls=%async_computation | async-start | bytes 1048576 | tf_op jit(solution)/shard_map/gather_features/all_to_all | solution.py:273
  19.6 3.0 %fusion.1 = (bf16[64,4096]{1,0:T(8,128)(2,1)}, bf16[64,4096]{1,0:T(8,128)(2,1)}, bf16[64,4096]{1,0:T(8,128)(2,1)}, bf16[64,4096]{1,0:T(8,128)(2,1)}) fusion(bf16[256,4096]{1,0:T(8,128)(2,1)} %own_ref.1), kind=kLoop, calls=%fused_computation.16 | loop fusion | bytes 4194304 | tf_op jit(solution)/shard_map/gather_features/slice | solution.py:276
  22.6 2.1 %collective-permute-start.3 = (bf16[64,4096]{1,0:T(8,128)(2,1)}, bf16[64,4096]{1,0:T(8,128)(2,1)S(1)}, u32[]{:S(2)}, u32[]{:S(2)}) collective-permute-start(bf16[64,4096]{1,0:T(8,128)(2,1)} %get-tuple-element.29), channel_id=1, source_target_pairs={{0,1},{1,0},{2,3},{3,2},{4,5},{5,4},{6,7},{7,6},{8,9},{9,8},{10,11... | collective-permute-start | bytes 1572872 | tf_op jit(solution)/shard_map/gather_features/ppermute | solution.py:276
  24.7 2.2 %collective-permute-start.2 = (bf16[64,4096]{1,0:T(8,128)(2,1)}, bf16[64,4096]{1,0:T(8,128)(2,1)S(1)}, u32[]{:S(2)}, u32[]{:S(2)}) collective-permute-start(bf16[64,4096]{1,0:T(8,128)(2,1)} %get-tuple-element.30), channel_id=1, source_target_pairs={{0,1},{1,0},{2,3},{3,2},{4,5},{5,4},{6,7},{7,6},{8,9},{9,8},{10,11... | collective-permute-start | bytes 1572872 | tf_op jit(solution)/shard_map/gather_features/ppermute | solution.py:276
  26.9 2.1 %collective-permute-start.1 = (bf16[64,4096]{1,0:T(8,128)(2,1)}, bf16[64,4096]{1,0:T(8,128)(2,1)}, u32[]{:S(2)}, u32[]{:S(2)}) collective-permute-start(bf16[64,4096]{1,0:T(8,128)(2,1)} %get-tuple-element.31), channel_id=1, source_target_pairs={{0,1},{1,0},{2,3},{3,2},{4,5},{5,4},{6,7},{7,6},{8,9},{9,8},{10,11... | collective-permute-start | bytes 1572872 | tf_op jit(solution)/shard_map/gather_features/ppermute | solution.py:276
  29.0 2.2 %collective-permute-start = (bf16[64,4096]{1,0:T(8,128)(2,1)}, bf16[64,4096]{1,0:T(8,128)(2,1)}, u32[]{:S(2)}, u32[]{:S(2)}) collective-permute-start(bf16[64,4096]{1,0:T(8,128)(2,1)} %get-tuple-element.32), channel_id=1, source_target_pairs={{0,1},{1,0},{2,3},{3,2},{4,5},{5,4},{6,7},{7,6},{8,9},{9,8},{10,11... | collective-permute-start | bytes 1572872 | tf_op jit(solution)/shard_map/gather_features/ppermute | solution.py:276
  31.4 0.3 fusion
  31.7 0.1 pad_maximum_fusion.1
  31.8 1.4 %collective-permute-done.refs_0_ = bf16[64,4096]{1,0:T(8,128)(2,1)} collective-permute-done((bf16[64,4096]{1,0:T(8,128)(2,1)}, bf16[64,4096]{1,0:T(8,128)(2,1)}, u32[]{:S(2)}, u32[]{:S(2)}) %collective-permute-start) | collective-permute-done | bytes 524320 | tf_op jit(solution)/shard_map/gather_features/ppermute | solution.py:276
  33.2 3.7 %all-to-all-done.own_ref = bf16[16,64,256]{2,1,0:T(8,128)(2,1)S(1)} async-done(((bf16[16,64,256]{2,1,0:T(8,128)(2,1)}), bf16[16,64,256]{2,1,0:T(8,128)(2,1)S(1)}, u32[]{:S(2)}, u32[]{:S(2)}) %all-to-all-start) | async-done | bytes 524320 | tf_op jit(solution)/shard_map/gather_features/all_to_all | solution.py:273
  36.9 2.0 %collective-permute-start.4 = (bf16[16,64,256]{2,1,0:T(8,128)(2,1)S(1)}, bf16[16,64,256]{2,1,0:T(8,128)(2,1)S(1)}, u32[]{:S(2)}, u32[]{:S(2)}) collective-permute-start(bf16[16,64,256]{2,1,0:T(8,128)(2,1)S(1)} %all-to-all-done.own_ref), channel_id=1, source_target_pairs={{0,1},{1,0},{2,3},{3,2},{4,5},{5,4},{6,7},{7,6},{8,9},{9,8},{10,11... | collective-permute-start | bytes 1572872 | tf_op jit(solution)/shard_map/gather_features/ppermute | solution.py:279
  38.9 0.1 broadcast_select_fusion
  39.1 1.7 %collective-permute-done.4.other_ref = bf16[16,64,256]{2,1,0:T(8,128)(2,1)S(1)} collective-permute-done((bf16[16,64,256]{2,1,0:T(8,128)(2,1)S(1)}, bf16[16,64,256]{2,1,0:T(8,128)(2,1)S(1)}, u32[]{:S(2)}, u32[]{:S(2)}) %collective-permute-start.4) | collective-permute-done | bytes 524320 | tf_op jit(solution)/shard_map/gather_features/ppermute | solution.py:279
  40.8 0.9 keys_values.2
  41.7 1.9 %collective-permute-start.5 = (bf16[128,128]{1,0:T(8,128)(2,1)S(1)}, bf16[128,128]{1,0:T(8,128)(2,1)S(1)}, u32[]{:S(2)}, u32[]{:S(2)}) collective-permute-start(bf16[128,128]{1,0:T(8,128)(2,1)S(1)} %get-tuple-element.17), channel_id=1, source_target_pairs={{0,0},{1,2},{2,4},{3,6},{4,8},{5,10},{6,12},{7,14},{8,1},{9,3},{10... | collective-permute-start | bytes 98312 | tf_op jit(solution)/shard_map/keys_values/ppermute | solution.py:305
  43.6 0.6 queries.1
  44.2 1.9 %collective-permute-start.6 = (bf16[256,128]{1,0:T(8,128)(2,1)S(1)}, bf16[256,128]{1,0:T(8,128)(2,1)S(1)}, u32[]{:S(2)}, u32[]{:S(2)}) collective-permute-start(bf16[256,128]{1,0:T(8,128)(2,1)S(1)} %pad_maximum_fusion.3), channel_id=1, source_target_pairs={{0,64},{64,0},{1,65},{65,1},{2,66},{66,2},{3,67},{67,3},{4,68},{68... | collective-permute-start | bytes 196616 | tf_op jit(solution)/shard_map/queries/ppermute | solution.py:317
  46.1 4.9 %collective-permute-done.5.kv_ref = bf16[128,128]{1,0:T(8,128)(2,1)S(1)} collective-permute-done((bf16[128,128]{1,0:T(8,128)(2,1)S(1)}, bf16[128,128]{1,0:T(8,128)(2,1)S(1)}, u32[]{:S(2)}, u32[]{:S(2)}) %collective-permute-start.5) | collective-permute-done | bytes 32800 | tf_op jit(solution)/shard_map/keys_values/ppermute | solution.py:305
  51.0 0.7 keys_values.3
  51.7 9.5 %all-to-all-start.1 = ((bf16[8,128,128]{2,1,0:T(8,128)(2,1)}), bf16[8,128,128]{2,1,0:T(8,128)(2,1)S(1)}, u32[]{:S(2)}, u32[]{:S(2)}) async-start(bf16[8,128,128]{2,1,0:T(8,128)(2,1)} %keys_values.3), calls=%async_computation.1 | async-start | bytes 524288 | tf_op jit(solution)/shard_map/spread_keys_values/all_to_all | solution.py:319
  61.3 1.9 %collective-permute-start.7 = (bf16[256,128]{1,0:T(8,128)(2,1)S(1)}, bf16[256,128]{1,0:T(8,128)(2,1)S(1)}, u32[]{:S(2)}, u32[]{:S(2)}) collective-permute-start(bf16[256,128]{1,0:T(8,128)(2,1)S(1)} %pad_maximum_fusion.4), channel_id=1, source_target_pairs={{0,1},{1,0},{2,3},{3,2},{4,5},{5,4},{6,7},{7,6},{8,9},{9,8},{10,11... | collective-permute-start | bytes 196616 | tf_op jit(solution)/shard_map/share_queries/ppermute | solution.py:322
  63.2 1.2 collective-permute-done.7
  64.5 11.0 %all_gather.3.query_ref = bf16[2048,128]{1,0:T(8,128)(2,1)S(1)} all-gather(bf16[512,128]{1,0:T(8,128)(2,1)S(1)} %pad_maximum_fusion), channel_id=1, replica_groups=mesh['zh'=8,'zp'=2,'x'=4,'y'=8,'c'=2] {'x'}, dimensions={0}, use_global_device_ids=true | all-gather | bytes 655360 | tf_op jit(solution)/shard_map/share_queries/all_gather | solution.py:324
  75.5 3.3 %all-to-all-done.1.own_ref = bf16[8,128,128]{2,1,0:T(8,128)(2,1)S(1)} async-done(((bf16[8,128,128]{2,1,0:T(8,128)(2,1)}), bf16[8,128,128]{2,1,0:T(8,128)(2,1)S(1)}, u32[]{:S(2)}, u32[]{:S(2)}) %all-to-all-start.1) | async-done | bytes 262176 | tf_op jit(solution)/shard_map/spread_keys_values/all_to_all | solution.py:319
  78.8 1.9 %collective-permute-start.8 = (bf16[8,128,128]{2,1,0:T(8,128)(2,1)S(1)}, bf16[8,128,128]{2,1,0:T(8,128)(2,1)S(1)}, u32[]{:S(2)}, u32[]{:S(2)}) collective-permute-start(bf16[8,128,128]{2,1,0:T(8,128)(2,1)S(1)} %all-to-all-done.1.own_ref), channel_id=1, source_target_pairs={{0,1},{1,0},{2,3},{3,2},{4,5},{5,4},{6,7},{7,6},{8,9},{9,8},{10,11... | collective-permute-start | bytes 786440 | tf_op jit(solution)/shard_map/share_queries/ppermute | solution.py:326
  80.8 1.4 %collective-permute-done.8.other_ref = bf16[8,128,128]{2,1,0:T(8,128)(2,1)S(1)} collective-permute-done((bf16[8,128,128]{2,1,0:T(8,128)(2,1)S(1)}, bf16[8,128,128]{2,1,0:T(8,128)(2,1)S(1)}, u32[]{:S(2)}, u32[]{:S(2)}) %collective-permute-start.8) | collective-permute-done | bytes 262176 | tf_op jit(solution)/shard_map/share_queries/ppermute | solution.py:326
  82.2 1.9 %attend.1 = bf16[8,144,256]{2,1,0:T(8,128)(2,1)S(1)} custom-call(s32[4]{0:T(128)S(1)} %pad_add_fusion.place_ref, bf16[2048,128]{1,0:T(8,128)(2,1)S(1)} %all_gather.3.query_ref, bf16[8,128,128]{2,1,0:T(8,128)(2,1)S(1)} %all-to-all-done.1.own_ref, bf16[8,128,128]{2,1,0:T(8,128)(2,1)S(1)} %collective-permute-done.8.other_ref), custom_call_target="tpu_custom_call" | custom-call | flops 1073741824 | bytes 2097152 | tf_op jit(solution)/shard_map/attend/pallas_call | solution.py:329
  84.1 14.3 %all_to_all.20.parts_ref = bf16[8,144,256]{2,1,0:T(8,128)(2,1)S(1)} all-to-all(bf16[8,144,256]{2,1,0:T(8,128)(2,1)S(1)} %attend.1), channel_id=1, replica_groups=mesh['zh'=8,'zp'=2,'x'=4,'y'=8,'c'=2] {'zp','x'}, dimensions={0} | all-to-all | bytes 1179648 | tf_op jit(solution)/shard_map/attend/all_to_all | solution.py:342
  98.4 2.0 %project.1 = bf16[16,64,256]{2,1,0:T(8,128)(2,1)S(1)} custom-call(bf16[8,144,256]{2,1,0:T(8,128)(2,1)S(1)} %all_to_all.20.parts_ref, bf16[256,4096]{1,0:T(8,128)(2,1)S(1)} %copy-done, bf16[64,4096]{1,0:T(8,128)(2,1)} %collective-permute-done.refs_0_, bf16[64,4096]{1,0:T(8,128)(2,1)} %collective-permute-done.1.refs_1_, ...), custom_call_target="tpu_custom_call" | custom-call | flops 268435456 | bytes 5242880 | tf_op jit(solution)/shard_map/project/pallas_call | solution.py:344
  100.4 24.0 %all_to_all.21.parts_ref = bf16[16,64,256]{2,1,0:T(8,128)(2,1)S(1)} all-to-all(bf16[16,64,256]{2,1,0:T(8,128)(2,1)S(1)} %project.1), channel_id=1, replica_groups=mesh['zh'=8,'zp'=2,'x'=4,'y'=8,'c'=2] {'y','c'}, dimensions={0} | all-to-all | bytes 1048576 | tf_op jit(solution)/shard_map/project/all_to_all | solution.py:357
  124.4 1.0 mix.1
  (32 shorter events, 0.3 us)
Async XLA Ops:
  2.0 34.9 %all-to-all-start = ((bf16[16,64,256]{2,1,0:T(8,128)(2,1)}), bf16[16,64,256]{2,1,0:T(8,128)(2,1)S(1)}, u32[]{:S(2)}, u32[]{:S(2)}) async-start(bf16[16,64,256]{2,1,0:T(8,128)(2,1)} %pick.1.after_ref), calls=%async_computation | async-start | bytes 1048576 | tf_op jit(solution)/shard_map/gather_features/all_to_all | solution.py:273
  19.5 11.7 %copy-start.7 = (f32[4096]{0:T(1024)S(1)}, f32[4096]{0:T(1024)}, u32[]{:S(2)}) copy-start(f32[4096]{0:T(1024)} %param.11) | copy-start | bytes 49156
  19.5 11.7 %copy-start.1 = (bf16[16,64,256]{2,1,0:T(8,128)(2,1)S(1)}, bf16[16,64,256]{2,1,0:T(8,128)(2,1)}, u32[]{:S(2)}) copy-start(bf16[16,64,256]{2,1,0:T(8,128)(2,1)} %pick.1.after_ref) | copy-start | bytes 1572868
  19.5 11.7 %copy-start.2 = (bf16[4096,128]{1,0:T(8,128)(2,1)S(1)}, bf16[4096,128]{1,0:T(8,128)(2,1)}, u32[]{:S(2)}) copy-start(bf16[4096,128]{1,0:T(8,128)(2,1)} %weight_ref.4) | copy-start | bytes 3145732
  19.6 11.8 %copy-start.5 = (s32[128]{0:T(128)S(1)}, s32[128]{0:T(128)}, u32[]{:S(2)}) copy-start(s32[128]{0:T(128)} %param.15) | copy-start | bytes 1540
  22.6 9.2 %collective-permute-start.3 = (bf16[64,4096]{1,0:T(8,128)(2,1)}, bf16[64,4096]{1,0:T(8,128)(2,1)S(1)}, u32[]{:S(2)}, u32[]{:S(2)}) collective-permute-start(bf16[64,4096]{1,0:T(8,128)(2,1)} %get-tuple-element.29), channel_id=1, source_target_pairs={{0,1},{1,0},{2,3},{3,2},{4,5},{5,4},{6,7},{7,6},{8,9},{9,8},{10,11... | collective-permute-start | bytes 1572872 | tf_op jit(solution)/shard_map/gather_features/ppermute | solution.py:276
  24.7 7.1 %collective-permute-start.2 = (bf16[64,4096]{1,0:T(8,128)(2,1)}, bf16[64,4096]{1,0:T(8,128)(2,1)S(1)}, u32[]{:S(2)}, u32[]{:S(2)}) collective-permute-start(bf16[64,4096]{1,0:T(8,128)(2,1)} %get-tuple-element.30), channel_id=1, source_target_pairs={{0,1},{1,0},{2,3},{3,2},{4,5},{5,4},{6,7},{7,6},{8,9},{9,8},{10,11... | collective-permute-start | bytes 1572872 | tf_op jit(solution)/shard_map/gather_features/ppermute | solution.py:276
  26.9 4.9 %collective-permute-start.1 = (bf16[64,4096]{1,0:T(8,128)(2,1)}, bf16[64,4096]{1,0:T(8,128)(2,1)}, u32[]{:S(2)}, u32[]{:S(2)}) collective-permute-start(bf16[64,4096]{1,0:T(8,128)(2,1)} %get-tuple-element.31), channel_id=1, source_target_pairs={{0,1},{1,0},{2,3},{3,2},{4,5},{5,4},{6,7},{7,6},{8,9},{9,8},{10,11... | collective-permute-start | bytes 1572872 | tf_op jit(solution)/shard_map/gather_features/ppermute | solution.py:276
  29.0 4.1 %collective-permute-start = (bf16[64,4096]{1,0:T(8,128)(2,1)}, bf16[64,4096]{1,0:T(8,128)(2,1)}, u32[]{:S(2)}, u32[]{:S(2)}) collective-permute-start(bf16[64,4096]{1,0:T(8,128)(2,1)} %get-tuple-element.32), channel_id=1, source_target_pairs={{0,1},{1,0},{2,3},{3,2},{4,5},{5,4},{6,7},{7,6},{8,9},{9,8},{10,11... | collective-permute-start | bytes 1572872 | tf_op jit(solution)/shard_map/gather_features/ppermute | solution.py:276
  36.9 6.7 %copy-start.3 = (bf16[4096,256]{1,0:T(8,128)(2,1)S(1)}, bf16[4096,256]{1,0:T(8,128)(2,1)}, u32[]{:S(2)}) copy-start(bf16[4096,256]{1,0:T(8,128)(2,1)} %weight_ref.5) | copy-start | bytes 6291460
  36.9 3.9 %collective-permute-start.4 = (bf16[16,64,256]{2,1,0:T(8,128)(2,1)S(1)}, bf16[16,64,256]{2,1,0:T(8,128)(2,1)S(1)}, u32[]{:S(2)}, u32[]{:S(2)}) collective-permute-start(bf16[16,64,256]{2,1,0:T(8,128)(2,1)S(1)} %all-to-all-done.own_ref), channel_id=1, source_target_pairs={{0,1},{1,0},{2,3},{3,2},{4,5},{5,4},{6,7},{7,6},{8,9},{9,8},{10,11... | collective-permute-start | bytes 1572872 | tf_op jit(solution)/shard_map/gather_features/ppermute | solution.py:279
  41.7 9.3 %collective-permute-start.5 = (bf16[128,128]{1,0:T(8,128)(2,1)S(1)}, bf16[128,128]{1,0:T(8,128)(2,1)S(1)}, u32[]{:S(2)}, u32[]{:S(2)}) collective-permute-start(bf16[128,128]{1,0:T(8,128)(2,1)S(1)} %get-tuple-element.17), channel_id=1, source_target_pairs={{0,0},{1,2},{2,4},{3,6},{4,8},{5,10},{6,12},{7,14},{8,1},{9,3},{10... | collective-permute-start | bytes 98312 | tf_op jit(solution)/shard_map/keys_values/ppermute | solution.py:305
  44.2 17.1 %collective-permute-start.6 = (bf16[256,128]{1,0:T(8,128)(2,1)S(1)}, bf16[256,128]{1,0:T(8,128)(2,1)S(1)}, u32[]{:S(2)}, u32[]{:S(2)}) collective-permute-start(bf16[256,128]{1,0:T(8,128)(2,1)S(1)} %pad_maximum_fusion.3), channel_id=1, source_target_pairs={{0,64},{64,0},{1,65},{65,1},{2,66},{66,2},{3,67},{67,3},{4,68},{68... | collective-permute-start | bytes 196616 | tf_op jit(solution)/shard_map/queries/ppermute | solution.py:317
  51.7 27.0 %all-to-all-start.1 = ((bf16[8,128,128]{2,1,0:T(8,128)(2,1)}), bf16[8,128,128]{2,1,0:T(8,128)(2,1)S(1)}, u32[]{:S(2)}, u32[]{:S(2)}) async-start(bf16[8,128,128]{2,1,0:T(8,128)(2,1)} %keys_values.3), calls=%async_computation.1 | async-start | bytes 524288 | tf_op jit(solution)/shard_map/spread_keys_values/all_to_all | solution.py:319
  61.3 3.1 %collective-permute-start.7 = (bf16[256,128]{1,0:T(8,128)(2,1)S(1)}, bf16[256,128]{1,0:T(8,128)(2,1)S(1)}, u32[]{:S(2)}, u32[]{:S(2)}) collective-permute-start(bf16[256,128]{1,0:T(8,128)(2,1)S(1)} %pad_maximum_fusion.4), channel_id=1, source_target_pairs={{0,1},{1,0},{2,3},{3,2},{4,5},{5,4},{6,7},{7,6},{8,9},{9,8},{10,11... | collective-permute-start | bytes 196616 | tf_op jit(solution)/shard_map/share_queries/ppermute | solution.py:322
  78.8 3.4 %collective-permute-start.8 = (bf16[8,128,128]{2,1,0:T(8,128)(2,1)S(1)}, bf16[8,128,128]{2,1,0:T(8,128)(2,1)S(1)}, u32[]{:S(2)}, u32[]{:S(2)}) collective-permute-start(bf16[8,128,128]{2,1,0:T(8,128)(2,1)S(1)} %all-to-all-done.1.own_ref), channel_id=1, source_target_pairs={{0,1},{1,0},{2,3},{3,2},{4,5},{5,4},{6,7},{7,6},{8,9},{9,8},{10,11... | collective-permute-start | bytes 786440 | tf_op jit(solution)/shard_map/share_queries/ppermute | solution.py:326
  80.8 17.6 %copy-start = (bf16[256,4096]{1,0:T(8,128)(2,1)S(1)}, bf16[256,4096]{1,0:T(8,128)(2,1)}, u32[]{:S(2)}) copy-start(bf16[256,4096]{1,0:T(8,128)(2,1)} %own_ref.1) | copy-start | bytes 6291460
  98.4 26.0 %copy-start.4 = (bf16[512,256]{1,0:T(8,128)(2,1)S(1)}, bf16[512,256]{1,0:T(8,128)(2,1)}, u32[]{:S(2)}) copy-start(bf16[512,256]{1,0:T(8,128)(2,1)} %hidden_ref.3) | copy-start | bytes 786436
  98.4 26.0 %copy-start.6 = (f32[512]{0:T(512)S(1)}, f32[512]{0:T(512)}, u32[]{:S(2)}) copy-start(f32[512]{0:T(512)} %param.10) | copy-start | bytes 6148

commit v6 on v5

--- a/solution.py
+++ b/solution.py
@@ -129,14 +129,12 @@
     query_shard = (zh * ZP + query_zp) * X + column // (ZP * ROWS)
     query_order = query_shard * CAP + c * HALF + column % HALF
 
-    def step(pair, carry):
-        own = own_ref[pl.ds(2 * pair, 2)].reshape(2 * CAP, HEAD_DIM)
-        other = other_ref[pl.ds(2 * pair, 2)].reshape(2 * CAP, HEAD_DIM)
+    def step(far, carry):
+        own, other = own_ref[far], other_ref[far]
         keys = jnp.where(c == 0, own, other)
         values_t = jnp.where(c == 0, other, own).T
-        row = lax.broadcasted_iota(jnp.int32, (2 * CAP, 1), 0)
-        shard = ((2 * pair + row // CAP) * ZP + zp) * X + x
-        key_order = shard * CAP + row % CAP
+        entry = lax.broadcasted_iota(jnp.int32, (CAP, 1), 0)
+        key_order = ((far * ZP + zp) * X + x) * CAP + entry
         unused = keys[:, 0:1].astype(jnp.float32) > 0.1 * UNUSED
         key_order = jnp.where(unused, 1 << 30, key_order)
         for part in range(CHAINS):
@@ -154,7 +152,7 @@
             )
         return carry
 
-    lax.fori_loop(0, zh // 2 + 1, step, 0)
+    lax.fori_loop(0, zh + 1, step, 0)
     total = sum_ref[...]
     safe = jnp.maximum(total, 1e-30)
     attended = (acc_ref[...] / safe).astype(jnp.bfloat16)

time: 126 us -> 126 us (level)
  no operation moved by 1% of the time
where the time goes in v6:
time: 126 us; the launch traced here: 125 us
  blocking collectives  49.3 us (39%)
  starting transfers between devices  45.4 us (36%)
  waiting for transfers between devices  17.6 us (14%)
  Pallas kernels  8.66 us (7%)
  local copies, waits for them, and re-layouts  3.05 us (2%)
    all_to_all x1, blocking collectives, local(): partial = lax.all_to_all(partial, MP, 0, 0, tiled=True)  24 us
    all_to_all x1, starting transfers between devices, local(): own_rows = lax.all_to_all(picked, MP, 0, 0, tiled=True)  17.5 us
    all_to_all x1, blocking collectives, local(): parts = lax.all_to_all(parts, NEAR, 0, 0, tiled=True)  14.3 us
    all_gather x1, blocking collectives, local(): queries = lax.all_gather(queries, 'x', axis=0, tiled=True)  11 us
    all_to_all x1, starting transfers between devices, local(): own = lax.all_to_all(kv, 'zh', 0, 0, tiled=True)  9.55 us
    ppermute x4, starting transfers between devices, local(): lax.ppermute(out_weight[i * deep:(i + 1) * deep], 'c', swap)  8.64 us
    ppermute x1, waiting for transfers between devices, local(): kv = lax.ppermute(kv, MP, to_heads)  4.89 us
    all_to_all x1, waiting for transfers between devices, local(): own_rows = lax.all_to_all(picked, MP, 0, 0, tiled=True)  3.69 us
  transfers between devices with their start and end apart: 11, of which 7 were waited for; matrix products, arithmetic and copies ran while one was open for 3% of the time, Pallas kernels for 1%

profile of v6, /device:TPU:1, one launch (start us, length us, event | category | flops | bytes accessed | tf_op | source)
XLA Modules:
  0.0 125.0 jit_solution(14302819209524426801)
XLA Ops:
  0.0 2.0 %pick.1.after_ref = bf16[16,64,256]{2,1,0:T(8,128)(2,1)} custom-call(s32[1,128]{1,0:T(1,128)} %bitcast.6, bf16[512,256]{1,0:T(8,128)(2,1)} %hidden_ref.3), custom_call_target="tpu_custom_call" | custom-call | tf_op jit(solution)/shard_map/pick/pallas_call | solution.py:269
  2.0 17.5 %all-to-all-start = ((bf16[16,64,256]{2,1,0:T(8,128)(2,1)}), bf16[16,64,256]{2,1,0:T(8,128)(2,1)S(1)}, u32[]{:S(2)}, u32[]{:S(2)}) async-start(bf16[16,64,256]{2,1,0:T(8,128)(2,1)} %pick.1.after_ref), calls=%async_computation | async-start | bytes 1048576 | tf_op jit(solution)/shard_map/gather_features/all_to_all | solution.py:271
  19.6 3.0 %fusion.1 = (bf16[64,4096]{1,0:T(8,128)(2,1)}, bf16[64,4096]{1,0:T(8,128)(2,1)}, bf16[64,4096]{1,0:T(8,128)(2,1)}, bf16[64,4096]{1,0:T(8,128)(2,1)}) fusion(bf16[256,4096]{1,0:T(8,128)(2,1)} %own_ref.1), kind=kLoop, calls=%fused_computation.16 | loop fusion | bytes 4194304 | tf_op jit(solution)/shard_map/gather_features/slice | solution.py:274
  22.6 2.1 %collective-permute-start.3 = (bf16[64,4096]{1,0:T(8,128)(2,1)}, bf16[64,4096]{1,0:T(8,128)(2,1)S(1)}, u32[]{:S(2)}, u32[]{:S(2)}) collective-permute-start(bf16[64,4096]{1,0:T(8,128)(2,1)} %get-tuple-element.29), channel_id=1, source_target_pairs={{0,1},{1,0},{2,3},{3,2},{4,5},{5,4},{6,7},{7,6},{8,9},{9,8},{10,11... | collective-permute-start | bytes 1572872 | tf_op jit(solution)/shard_map/gather_features/ppermute | solution.py:274
  24.7 2.2 %collective-permute-start.2 = (bf16[64,4096]{1,0:T(8,128)(2,1)}, bf16[64,4096]{1,0:T(8,128)(2,1)S(1)}, u32[]{:S(2)}, u32[]{:S(2)}) collective-permute-start(bf16[64,4096]{1,0:T(8,128)(2,1)} %get-tuple-element.30), channel_id=1, source_target_pairs={{0,1},{1,0},{2,3},{3,2},{4,5},{5,4},{6,7},{7,6},{8,9},{9,8},{10,11... | collective-permute-start | bytes 1572872 | tf_op jit(solution)/shard_map/gather_features/ppermute | solution.py:274
  26.9 2.1 %collective-permute-start.1 = (bf16[64,4096]{1,0:T(8,128)(2,1)}, bf16[64,4096]{1,0:T(8,128)(2,1)}, u32[]{:S(2)}, u32[]{:S(2)}) collective-permute-start(bf16[64,4096]{1,0:T(8,128)(2,1)} %get-tuple-element.31), channel_id=1, source_target_pairs={{0,1},{1,0},{2,3},{3,2},{4,5},{5,4},{6,7},{7,6},{8,9},{9,8},{10,11... | collective-permute-start | bytes 1572872 | tf_op jit(solution)/shard_map/gather_features/ppermute | solution.py:274
  29.0 2.2 %collective-permute-start = (bf16[64,4096]{1,0:T(8,128)(2,1)}, bf16[64,4096]{1,0:T(8,128)(2,1)}, u32[]{:S(2)}, u32[]{:S(2)}) collective-permute-start(bf16[64,4096]{1,0:T(8,128)(2,1)} %get-tuple-element.32), channel_id=1, source_target_pairs={{0,1},{1,0},{2,3},{3,2},{4,5},{5,4},{6,7},{7,6},{8,9},{9,8},{10,11... | collective-permute-start | bytes 1572872 | tf_op jit(solution)/shard_map/gather_features/ppermute | solution.py:274
  31.4 0.3 fusion
  31.7 0.1 pad_maximum_fusion.1
  31.8 1.4 %collective-permute-done.refs_0_ = bf16[64,4096]{1,0:T(8,128)(2,1)} collective-permute-done((bf16[64,4096]{1,0:T(8,128)(2,1)}, bf16[64,4096]{1,0:T(8,128)(2,1)}, u32[]{:S(2)}, u32[]{:S(2)}) %collective-permute-start) | collective-permute-done | bytes 524320 | tf_op jit(solution)/shard_map/gather_features/ppermute | solution.py:274
  33.2 3.7 %all-to-all-done.own_ref = bf16[16,64,256]{2,1,0:T(8,128)(2,1)S(1)} async-done(((bf16[16,64,256]{2,1,0:T(8,128)(2,1)}), bf16[16,64,256]{2,1,0:T(8,128)(2,1)S(1)}, u32[]{:S(2)}, u32[]{:S(2)}) %all-to-all-start) | async-done | bytes 524320 | tf_op jit(solution)/shard_map/gather_features/all_to_all | solution.py:271
  36.9 2.0 %collective-permute-start.4 = (bf16[16,64,256]{2,1,0:T(8,128)(2,1)S(1)}, bf16[16,64,256]{2,1,0:T(8,128)(2,1)S(1)}, u32[]{:S(2)}, u32[]{:S(2)}) collective-permute-start(bf16[16,64,256]{2,1,0:T(8,128)(2,1)S(1)} %all-to-all-done.own_ref), channel_id=1, source_target_pairs={{0,1},{1,0},{2,3},{3,2},{4,5},{5,4},{6,7},{7,6},{8,9},{9,8},{10,11... | collective-permute-start | bytes 1572872 | tf_op jit(solution)/shard_map/gather_features/ppermute | solution.py:277
  38.9 0.1 broadcast_select_fusion
  39.1 1.7 %collective-permute-done.4.other_ref = bf16[16,64,256]{2,1,0:T(8,128)(2,1)S(1)} collective-permute-done((bf16[16,64,256]{2,1,0:T(8,128)(2,1)S(1)}, bf16[16,64,256]{2,1,0:T(8,128)(2,1)S(1)}, u32[]{:S(2)}, u32[]{:S(2)}) %collective-permute-start.4) | collective-permute-done | bytes 524320 | tf_op jit(solution)/shard_map/gather_features/ppermute | solution.py:277
  40.8 0.9 keys_values.2
  41.7 1.9 %collective-permute-start.5 = (bf16[128,128]{1,0:T(8,128)(2,1)S(1)}, bf16[128,128]{1,0:T(8,128)(2,1)S(1)}, u32[]{:S(2)}, u32[]{:S(2)}) collective-permute-start(bf16[128,128]{1,0:T(8,128)(2,1)S(1)} %get-tuple-element.17), channel_id=1, source_target_pairs={{0,0},{1,2},{2,4},{3,6},{4,8},{5,10},{6,12},{7,14},{8,1},{9,3},{10... | collective-permute-start | bytes 98312 | tf_op jit(solution)/shard_map/keys_values/ppermute | solution.py:303
  43.6 0.6 queries.1
  44.2 1.9 %collective-permute-start.6 = (bf16[256,128]{1,0:T(8,128)(2,1)S(1)}, bf16[256,128]{1,0:T(8,128)(2,1)S(1)}, u32[]{:S(2)}, u32[]{:S(2)}) collective-permute-start(bf16[256,128]{1,0:T(8,128)(2,1)S(1)} %pad_maximum_fusion.3), channel_id=1, source_target_pairs={{0,64},{64,0},{1,65},{65,1},{2,66},{66,2},{3,67},{67,3},{4,68},{68... | collective-permute-start | bytes 196616 | tf_op jit(solution)/shard_map/queries/ppermute | solution.py:315
  46.1 4.9 %collective-permute-done.5.kv_ref = bf16[128,128]{1,0:T(8,128)(2,1)S(1)} collective-permute-done((bf16[128,128]{1,0:T(8,128)(2,1)S(1)}, bf16[128,128]{1,0:T(8,128)(2,1)S(1)}, u32[]{:S(2)}, u32[]{:S(2)}) %collective-permute-start.5) | collective-permute-done | bytes 32800 | tf_op jit(solution)/shard_map/keys_values/ppermute | solution.py:303
  51.0 0.7 keys_values.3
  51.7 9.5 %all-to-all-start.1 = ((bf16[8,128,128]{2,1,0:T(8,128)(2,1)}), bf16[8,128,128]{2,1,0:T(8,128)(2,1)S(1)}, u32[]{:S(2)}, u32[]{:S(2)}) async-start(bf16[8,128,128]{2,1,0:T(8,128)(2,1)} %keys_values.3), calls=%async_computation.1 | async-start | bytes 524288 | tf_op jit(solution)/shard_map/spread_keys_values/all_to_all | solution.py:317
  61.3 1.9 %collective-permute-start.7 = (bf16[256,128]{1,0:T(8,128)(2,1)S(1)}, bf16[256,128]{1,0:T(8,128)(2,1)S(1)}, u32[]{:S(2)}, u32[]{:S(2)}) collective-permute-start(bf16[256,128]{1,0:T(8,128)(2,1)S(1)} %pad_maximum_fusion.4), channel_id=1, source_target_pairs={{0,1},{1,0},{2,3},{3,2},{4,5},{5,4},{6,7},{7,6},{8,9},{9,8},{10,11... | collective-permute-start | bytes 196616 | tf_op jit(solution)/shard_map/share_queries/ppermute | solution.py:320
  63.2 1.2 collective-permute-done.7
  64.5 11.0 %all_gather.3.query_ref = bf16[2048,128]{1,0:T(8,128)(2,1)S(1)} all-gather(bf16[512,128]{1,0:T(8,128)(2,1)S(1)} %pad_maximum_fusion), channel_id=1, replica_groups=mesh['zh'=8,'zp'=2,'x'=4,'y'=8,'c'=2] {'x'}, dimensions={0}, use_global_device_ids=true | all-gather | bytes 655360 | tf_op jit(solution)/shard_map/share_queries/all_gather | solution.py:322
  75.5 3.3 %all-to-all-done.1.own_ref = bf16[8,128,128]{2,1,0:T(8,128)(2,1)S(1)} async-done(((bf16[8,128,128]{2,1,0:T(8,128)(2,1)}), bf16[8,128,128]{2,1,0:T(8,128)(2,1)S(1)}, u32[]{:S(2)}, u32[]{:S(2)}) %all-to-all-start.1) | async-done | bytes 262176 | tf_op jit(solution)/shard_map/spread_keys_values/all_to_all | solution.py:317
  78.8 1.9 %collective-permute-start.8 = (bf16[8,128,128]{2,1,0:T(8,128)(2,1)S(1)}, bf16[8,128,128]{2,1,0:T(8,128)(2,1)S(1)}, u32[]{:S(2)}, u32[]{:S(2)}) collective-permute-start(bf16[8,128,128]{2,1,0:T(8,128)(2,1)S(1)} %all-to-all-done.1.own_ref), channel_id=1, source_target_pairs={{0,1},{1,0},{2,3},{3,2},{4,5},{5,4},{6,7},{7,6},{8,9},{9,8},{10,11... | collective-permute-start | bytes 786440 | tf_op jit(solution)/shard_map/share_queries/ppermute | solution.py:324
  80.8 1.4 %collective-permute-done.8.other_ref = bf16[8,128,128]{2,1,0:T(8,128)(2,1)S(1)} collective-permute-done((bf16[8,128,128]{2,1,0:T(8,128)(2,1)S(1)}, bf16[8,128,128]{2,1,0:T(8,128)(2,1)S(1)}, u32[]{:S(2)}, u32[]{:S(2)}) %collective-permute-start.8) | collective-permute-done | bytes 262176 | tf_op jit(solution)/shard_map/share_queries/ppermute | solution.py:324
  82.2 1.5 %attend.1 = bf16[8,144,256]{2,1,0:T(8,128)(2,1)S(1)} custom-call(s32[4]{0:T(128)S(1)} %pad_add_fusion.place_ref, bf16[2048,128]{1,0:T(8,128)(2,1)S(1)} %all_gather.3.query_ref, bf16[8,128,128]{2,1,0:T(8,128)(2,1)S(1)} %all-to-all-done.1.own_ref, bf16[8,128,128]{2,1,0:T(8,128)(2,1)S(1)} %collective-permute-done.8.other_ref), custom_call_target="tpu_custom_call" | custom-call | flops 1073741824 | bytes 2097152 | tf_op jit(solution)/shard_map/attend/pallas_call | solution.py:327
  83.7 14.3 %all_to_all.20.parts_ref = bf16[8,144,256]{2,1,0:T(8,128)(2,1)S(1)} all-to-all(bf16[8,144,256]{2,1,0:T(8,128)(2,1)S(1)} %attend.1), channel_id=1, replica_groups=mesh['zh'=8,'zp'=2,'x'=4,'y'=8,'c'=2] {'zp','x'}, dimensions={0} | all-to-all | bytes 1179648 | tf_op jit(solution)/shard_map/attend/all_to_all | solution.py:340
  98.0 2.0 %project.1 = bf16[16,64,256]{2,1,0:T(8,128)(2,1)S(1)} custom-call(bf16[8,144,256]{2,1,0:T(8,128)(2,1)S(1)} %all_to_all.20.parts_ref, bf16[256,4096]{1,0:T(8,128)(2,1)S(1)} %copy-done, bf16[64,4096]{1,0:T(8,128)(2,1)} %collective-permute-done.refs_0_, bf16[64,4096]{1,0:T(8,128)(2,1)} %collective-permute-done.1.refs_1_, ...), custom_call_target="tpu_custom_call" | custom-call | flops 268435456 | bytes 5242880 | tf_op jit(solution)/shard_map/project/pallas_call | solution.py:342
  100.0 24.0 %all_to_all.21.parts_ref = bf16[16,64,256]{2,1,0:T(8,128)(2,1)S(1)} all-to-all(bf16[16,64,256]{2,1,0:T(8,128)(2,1)S(1)} %project.1), channel_id=1, replica_groups=mesh['zh'=8,'zp'=2,'x'=4,'y'=8,'c'=2] {'y','c'}, dimensions={0} | all-to-all | bytes 1048576 | tf_op jit(solution)/shard_map/project/all_to_all | solution.py:355
  124.0 1.0 mix.1
  (32 shorter events, 0.3 us)
Async XLA Ops:
  2.0 34.9 %all-to-all-start = ((bf16[16,64,256]{2,1,0:T(8,128)(2,1)}), bf16[16,64,256]{2,1,0:T(8,128)(2,1)S(1)}, u32[]{:S(2)}, u32[]{:S(2)}) async-start(bf16[16,64,256]{2,1,0:T(8,128)(2,1)} %pick.1.after_ref), calls=%async_computation | async-start | bytes 1048576 | tf_op jit(solution)/shard_map/gather_features/all_to_all | solution.py:271
  19.5 11.7 %copy-start.7 = (f32[4096]{0:T(1024)S(1)}, f32[4096]{0:T(1024)}, u32[]{:S(2)}) copy-start(f32[4096]{0:T(1024)} %param.11) | copy-start | bytes 49156
  19.5 11.7 %copy-start.1 = (bf16[16,64,256]{2,1,0:T(8,128)(2,1)S(1)}, bf16[16,64,256]{2,1,0:T(8,128)(2,1)}, u32[]{:S(2)}) copy-start(bf16[16,64,256]{2,1,0:T(8,128)(2,1)} %pick.1.after_ref) | copy-start | bytes 1572868
  19.5 11.7 %copy-start.2 = (bf16[4096,128]{1,0:T(8,128)(2,1)S(1)}, bf16[4096,128]{1,0:T(8,128)(2,1)}, u32[]{:S(2)}) copy-start(bf16[4096,128]{1,0:T(8,128)(2,1)} %weight_ref.4) | copy-start | bytes 3145732
  19.6 11.8 %copy-start.5 = (s32[128]{0:T(128)S(1)}, s32[128]{0:T(128)}, u32[]{:S(2)}) copy-start(s32[128]{0:T(128)} %param.15) | copy-start | bytes 1540
  22.6 9.2 %collective-permute-start.3 = (bf16[64,4096]{1,0:T(8,128)(2,1)}, bf16[64,4096]{1,0:T(8,128)(2,1)S(1)}, u32[]{:S(2)}, u32[]{:S(2)}) collective-permute-start(bf16[64,4096]{1,0:T(8,128)(2,1)} %get-tuple-element.29), channel_id=1, source_target_pairs={{0,1},{1,0},{2,3},{3,2},{4,5},{5,4},{6,7},{7,6},{8,9},{9,8},{10,11... | collective-permute-start | bytes 1572872 | tf_op jit(solution)/shard_map/gather_features/ppermute | solution.py:274
  24.7 7.1 %collective-permute-start.2 = (bf16[64,4096]{1,0:T(8,128)(2,1)}, bf16[64,4096]{1,0:T(8,128)(2,1)S(1)}, u32[]{:S(2)}, u32[]{:S(2)}) collective-permute-start(bf16[64,4096]{1,0:T(8,128)(2,1)} %get-tuple-element.30), channel_id=1, source_target_pairs={{0,1},{1,0},{2,3},{3,2},{4,5},{5,4},{6,7},{7,6},{8,9},{9,8},{10,11... | collective-permute-start | bytes 1572872 | tf_op jit(solution)/shard_map/gather_features/ppermute | solution.py:274
  26.9 4.9 %collective-permute-start.1 = (bf16[64,4096]{1,0:T(8,128)(2,1)}, bf16[64,4096]{1,0:T(8,128)(2,1)}, u32[]{:S(2)}, u32[]{:S(2)}) collective-permute-start(bf16[64,4096]{1,0:T(8,128)(2,1)} %get-tuple-element.31), channel_id=1, source_target_pairs={{0,1},{1,0},{2,3},{3,2},{4,5},{5,4},{6,7},{7,6},{8,9},{9,8},{10,11... | collective-permute-start | bytes 1572872 | tf_op jit(solution)/shard_map/gather_features/ppermute | solution.py:274
  29.0 4.1 %collective-permute-start = (bf16[64,4096]{1,0:T(8,128)(2,1)}, bf16[64,4096]{1,0:T(8,128)(2,1)}, u32[]{:S(2)}, u32[]{:S(2)}) collective-permute-start(bf16[64,4096]{1,0:T(8,128)(2,1)} %get-tuple-element.32), channel_id=1, source_target_pairs={{0,1},{1,0},{2,3},{3,2},{4,5},{5,4},{6,7},{7,6},{8,9},{9,8},{10,11... | collective-permute-start | bytes 1572872 | tf_op jit(solution)/shard_map/gather_features/ppermute | solution.py:274
  36.9 6.7 %copy-start.3 = (bf16[4096,256]{1,0:T(8,128)(2,1)S(1)}, bf16[4096,256]{1,0:T(8,128)(2,1)}, u32[]{:S(2)}) copy-start(bf16[4096,256]{1,0:T(8,128)(2,1)} %weight_ref.5) | copy-start | bytes 6291460
  36.9 3.9 %collective-permute-start.4 = (bf16[16,64,256]{2,1,0:T(8,128)(2,1)S(1)}, bf16[16,64,256]{2,1,0:T(8,128)(2,1)S(1)}, u32[]{:S(2)}, u32[]{:S(2)}) collective-permute-start(bf16[16,64,256]{2,1,0:T(8,128)(2,1)S(1)} %all-to-all-done.own_ref), channel_id=1, source_target_pairs={{0,1},{1,0},{2,3},{3,2},{4,5},{5,4},{6,7},{7,6},{8,9},{9,8},{10,11... | collective-permute-start | bytes 1572872 | tf_op jit(solution)/shard_map/gather_features/ppermute | solution.py:277
  41.7 9.3 %collective-permute-start.5 = (bf16[128,128]{1,0:T(8,128)(2,1)S(1)}, bf16[128,128]{1,0:T(8,128)(2,1)S(1)}, u32[]{:S(2)}, u32[]{:S(2)}) collective-permute-start(bf16[128,128]{1,0:T(8,128)(2,1)S(1)} %get-tuple-element.17), channel_id=1, source_target_pairs={{0,0},{1,2},{2,4},{3,6},{4,8},{5,10},{6,12},{7,14},{8,1},{9,3},{10... | collective-permute-start | bytes 98312 | tf_op jit(solution)/shard_map/keys_values/ppermute | solution.py:303
  44.2 17.1 %collective-permute-start.6 = (bf16[256,128]{1,0:T(8,128)(2,1)S(1)}, bf16[256,128]{1,0:T(8,128)(2,1)S(1)}, u32[]{:S(2)}, u32[]{:S(2)}) collective-permute-start(bf16[256,128]{1,0:T(8,128)(2,1)S(1)} %pad_maximum_fusion.3), channel_id=1, source_target_pairs={{0,64},{64,0},{1,65},{65,1},{2,66},{66,2},{3,67},{67,3},{4,68},{68... | collective-permute-start | bytes 196616 | tf_op jit(solution)/shard_map/queries/ppermute | solution.py:315
  51.7 27.0 %all-to-all-start.1 = ((bf16[8,128,128]{2,1,0:T(8,128)(2,1)}), bf16[8,128,128]{2,1,0:T(8,128)(2,1)S(1)}, u32[]{:S(2)}, u32[]{:S(2)}) async-start(bf16[8,128,128]{2,1,0:T(8,128)(2,1)} %keys_values.3), calls=%async_computation.1 | async-start | bytes 524288 | tf_op jit(solution)/shard_map/spread_keys_values/all_to_all | solution.py:317
  61.3 3.1 %collective-permute-start.7 = (bf16[256,128]{1,0:T(8,128)(2,1)S(1)}, bf16[256,128]{1,0:T(8,128)(2,1)S(1)}, u32[]{:S(2)}, u32[]{:S(2)}) collective-permute-start(bf16[256,128]{1,0:T(8,128)(2,1)S(1)} %pad_maximum_fusion.4), channel_id=1, source_target_pairs={{0,1},{1,0},{2,3},{3,2},{4,5},{5,4},{6,7},{7,6},{8,9},{9,8},{10,11... | collective-permute-start | bytes 196616 | tf_op jit(solution)/shard_map/share_queries/ppermute | solution.py:320
  78.8 3.4 %collective-permute-start.8 = (bf16[8,128,128]{2,1,0:T(8,128)(2,1)S(1)}, bf16[8,128,128]{2,1,0:T(8,128)(2,1)S(1)}, u32[]{:S(2)}, u32[]{:S(2)}) collective-permute-start(bf16[8,128,128]{2,1,0:T(8,128)(2,1)S(1)} %all-to-all-done.1.own_ref), channel_id=1, source_target_pairs={{0,1},{1,0},{2,3},{3,2},{4,5},{5,4},{6,7},{7,6},{8,9},{9,8},{10,11... | collective-permute-start | bytes 786440 | tf_op jit(solution)/shard_map/share_queries/ppermute | solution.py:324
  80.8 17.2 %copy-start = (bf16[256,4096]{1,0:T(8,128)(2,1)S(1)}, bf16[256,4096]{1,0:T(8,128)(2,1)}, u32[]{:S(2)}) copy-start(bf16[256,4096]{1,0:T(8,128)(2,1)} %own_ref.1) | copy-start | bytes 6291460
  98.0 26.0 %copy-start.4 = (bf16[512,256]{1,0:T(8,128)(2,1)S(1)}, bf16[512,256]{1,0:T(8,128)(2,1)}, u32[]{:S(2)}) copy-start(bf16[512,256]{1,0:T(8,128)(2,1)} %hidden_ref.3) | copy-start | bytes 786436
  98.0 26.0 %copy-start.6 = (f32[512]{0:T(512)S(1)}, f32[512]{0:T(512)}, u32[]{:S(2)}) copy-start(f32[512]{0:T(512)} %param.10) | copy-start | bytes 6148

commit v7 on v6

--- a/solution.py
+++ b/solution.py
@@ -28,6 +28,7 @@
 ROWS = C * HEADS * HALF
 STATS = 16
 UNUSED = 1e30
+STRIPS = 4
 PIECES = 4
 CHAINS = 1
 LOW, LOWER = -1e30, -2e30
@@ -174,10 +175,16 @@
 
 def project_kernel(parts_ref, own_ref, *refs):
     other_refs, (out_ref, other_buf, total_ref, arrived) = refs[:PIECES], refs[PIECES:]
-    copies = [
-        pltpu.make_async_copy(ref, other_buf.at[i], arrived.at[i])
-        for i, ref in enumerate(other_refs)
-    ]
+    strip = N_MP // STRIPS * WIDTH
+    copies = []
+    for k in range(STRIPS):
+        span = pl.ds(k * strip, strip)
+        for i, ref in enumerate(other_refs):
+            copies.append(
+                pltpu.make_async_copy(
+                    ref.at[:, span], other_buf.at[i, :, span], arrived.at[k * PIECES + i]
+                )
+            )
     for copy in copies:
         copy.start()
     logs = []
@@ -198,9 +205,11 @@
     for m in range(N_MP):
         columns = slice(m * WIDTH, (m + 1) * WIDTH)
         total_ref[m] = dot(attended[:, :WIDTH], own_ref[:, columns], ((1,), (0,)))
-    for copy in copies:
-        copy.wait()
     for m in range(N_MP):
+        if m % (N_MP // STRIPS) == 0:
+            first = m // (N_MP // STRIPS) * PIECES
+            for copy in copies[first : first + PIECES]:
+                copy.wait()
         columns = slice(m * WIDTH, (m + 1) * WIDTH)
         block = total_ref[m]
         for i in range(PIECES):
@@ -347,7 +356,7 @@
             scratch=(
                 pltpu.VMEM((PIECES, WIDTH // PIECES, N_MP * WIDTH), jnp.bfloat16),
                 pltpu.VMEM((N_MP, HALF, WIDTH), jnp.float32),
-                pltpu.SemaphoreType.DMA((PIECES,)),
+                pltpu.SemaphoreType.DMA((STRIPS * PIECES,)),
             ),
             flops=2 * CAP * WIDTH * N_MP * WIDTH,
             nbytes=5 << 20,

time: 126 us -> 126 us (level)
  no operation moved by 1% of the time
where the time goes in v7:
time: 126 us; the launch traced here: 125 us
  blocking collectives  49.2 us (39%)
  starting transfers between devices  45.4 us (36%)
  waiting for transfers between devices  17.6 us (14%)
  Pallas kernels  8.98 us (7%)
  local copies, waits for them, and re-layouts  3.05 us (2%)
    all_to_all x1, blocking collectives, local(): partial = lax.all_to_all(partial, MP, 0, 0, tiled=True)  24 us
    all_to_all x1, starting transfers between devices, local(): own_rows = lax.all_to_all(picked, MP, 0, 0, tiled=True)  17.5 us
    all_to_all x1, blocking collectives, local(): parts = lax.all_to_all(parts, NEAR, 0, 0, tiled=True)  14.3 us
    all_gather x1, blocking collectives, local(): queries = lax.all_gather(queries, 'x', axis=0, tiled=True)  11 us
    all_to_all x1, starting transfers between devices, local(): own = lax.all_to_all(kv, 'zh', 0, 0, tiled=True)  9.55 us
    ppermute x4, starting transfers between devices, local(): lax.ppermute(out_weight[i * deep:(i + 1) * deep], 'c', swap)  8.64 us
    ppermute x1, waiting for transfers between devices, local(): kv = lax.ppermute(kv, MP, to_heads)  4.89 us
    all_to_all x1, waiting for transfers between devices, local(): own_rows = lax.all_to_all(picked, MP, 0, 0, tiled=True)  3.69 us
  transfers between devices with their start and end apart: 11, of which 7 were waited for; matrix products, arithmetic and copies ran while one was open for 3% of the time, Pallas kernels for 1%

profile of v7, /device:TPU:1, one launch (start us, length us, event | category | flops | bytes accessed | tf_op | source)
XLA Modules:
  0.0 125.3 jit_solution(16900887466074316087)
XLA Ops:
  0.0 2.0 %pick.1.after_ref = bf16[16,64,256]{2,1,0:T(8,128)(2,1)} custom-call(s32[1,128]{1,0:T(1,128)} %bitcast.6, bf16[512,256]{1,0:T(8,128)(2,1)} %hidden_ref.3), custom_call_target="tpu_custom_call" | custom-call | tf_op jit(solution)/shard_map/pick/pallas_call | solution.py:278
  2.0 17.5 %all-to-all-start = ((bf16[16,64,256]{2,1,0:T(8,128)(2,1)}), bf16[16,64,256]{2,1,0:T(8,128)(2,1)S(1)}, u32[]{:S(2)}, u32[]{:S(2)}) async-start(bf16[16,64,256]{2,1,0:T(8,128)(2,1)} %pick.1.after_ref), calls=%async_computation | async-start | bytes 1048576 | tf_op jit(solution)/shard_map/gather_features/all_to_all | solution.py:280
  19.6 3.0 %fusion.1 = (bf16[64,4096]{1,0:T(8,128)(2,1)}, bf16[64,4096]{1,0:T(8,128)(2,1)}, bf16[64,4096]{1,0:T(8,128)(2,1)}, bf16[64,4096]{1,0:T(8,128)(2,1)}) fusion(bf16[256,4096]{1,0:T(8,128)(2,1)} %own_ref.1), kind=kLoop, calls=%fused_computation.16 | loop fusion | bytes 4194304 | tf_op jit(solution)/shard_map/gather_features/slice | solution.py:283
  22.6 2.1 %collective-permute-start.3 = (bf16[64,4096]{1,0:T(8,128)(2,1)}, bf16[64,4096]{1,0:T(8,128)(2,1)S(1)}, u32[]{:S(2)}, u32[]{:S(2)}) collective-permute-start(bf16[64,4096]{1,0:T(8,128)(2,1)} %get-tuple-element.29), channel_id=1, source_target_pairs={{0,1},{1,0},{2,3},{3,2},{4,5},{5,4},{6,7},{7,6},{8,9},{9,8},{10,11... | collective-permute-start | bytes 1572872 | tf_op jit(solution)/shard_map/gather_features/ppermute | solution.py:283
  24.7 2.2 %collective-permute-start.2 = (bf16[64,4096]{1,0:T(8,128)(2,1)}, bf16[64,4096]{1,0:T(8,128)(2,1)S(1)}, u32[]{:S(2)}, u32[]{:S(2)}) collective-permute-start(bf16[64,4096]{1,0:T(8,128)(2,1)} %get-tuple-element.30), channel_id=1, source_target_pairs={{0,1},{1,0},{2,3},{3,2},{4,5},{5,4},{6,7},{7,6},{8,9},{9,8},{10,11... | collective-permute-start | bytes 1572872 | tf_op jit(solution)/shard_map/gather_features/ppermute | solution.py:283
  26.9 2.1 %collective-permute-start.1 = (bf16[64,4096]{1,0:T(8,128)(2,1)}, bf16[64,4096]{1,0:T(8,128)(2,1)}, u32[]{:S(2)}, u32[]{:S(2)}) collective-permute-start(bf16[64,4096]{1,0:T(8,128)(2,1)} %get-tuple-element.31), channel_id=1, source_target_pairs={{0,1},{1,0},{2,3},{3,2},{4,5},{5,4},{6,7},{7,6},{8,9},{9,8},{10,11... | collective-permute-start | bytes 1572872 | tf_op jit(solution)/shard_map/gather_features/ppermute | solution.py:283
  29.0 2.2 %collective-permute-start = (bf16[64,4096]{1,0:T(8,128)(2,1)}, bf16[64,4096]{1,0:T(8,128)(2,1)}, u32[]{:S(2)}, u32[]{:S(2)}) collective-permute-start(bf16[64,4096]{1,0:T(8,128)(2,1)} %get-tuple-element.32), channel_id=1, source_target_pairs={{0,1},{1,0},{2,3},{3,2},{4,5},{5,4},{6,7},{7,6},{8,9},{9,8},{10,11... | collective-permute-start | bytes 1572872 | tf_op jit(solution)/shard_map/gather_features/ppermute | solution.py:283
  31.4 0.3 fusion
  31.7 0.1 pad_maximum_fusion.1
  31.8 1.4 %collective-permute-done.refs_0_ = bf16[64,4096]{1,0:T(8,128)(2,1)} collective-permute-done((bf16[64,4096]{1,0:T(8,128)(2,1)}, bf16[64,4096]{1,0:T(8,128)(2,1)}, u32[]{:S(2)}, u32[]{:S(2)}) %collective-permute-start) | collective-permute-done | bytes 524320 | tf_op jit(solution)/shard_map/gather_features/ppermute | solution.py:283
  33.2 3.7 %all-to-all-done.own_ref = bf16[16,64,256]{2,1,0:T(8,128)(2,1)S(1)} async-done(((bf16[16,64,256]{2,1,0:T(8,128)(2,1)}), bf16[16,64,256]{2,1,0:T(8,128)(2,1)S(1)}, u32[]{:S(2)}, u32[]{:S(2)}) %all-to-all-start) | async-done | bytes 524320 | tf_op jit(solution)/shard_map/gather_features/all_to_all | solution.py:280
  36.9 2.0 %collective-permute-start.4 = (bf16[16,64,256]{2,1,0:T(8,128)(2,1)S(1)}, bf16[16,64,256]{2,1,0:T(8,128)(2,1)S(1)}, u32[]{:S(2)}, u32[]{:S(2)}) collective-permute-start(bf16[16,64,256]{2,1,0:T(8,128)(2,1)S(1)} %all-to-all-done.own_ref), channel_id=1, source_target_pairs={{0,1},{1,0},{2,3},{3,2},{4,5},{5,4},{6,7},{7,6},{8,9},{9,8},{10,11... | collective-permute-start | bytes 1572872 | tf_op jit(solution)/shard_map/gather_features/ppermute | solution.py:286
  38.9 0.1 broadcast_select_fusion
  39.1 1.7 %collective-permute-done.4.other_ref = bf16[16,64,256]{2,1,0:T(8,128)(2,1)S(1)} collective-permute-done((bf16[16,64,256]{2,1,0:T(8,128)(2,1)S(1)}, bf16[16,64,256]{2,1,0:T(8,128)(2,1)S(1)}, u32[]{:S(2)}, u32[]{:S(2)}) %collective-permute-start.4) | collective-permute-done | bytes 524320 | tf_op jit(solution)/shard_map/gather_features/ppermute | solution.py:286
  40.8 0.9 keys_values.2
  41.7 1.9 %collective-permute-start.5 = (bf16[128,128]{1,0:T(8,128)(2,1)S(1)}, bf16[128,128]{1,0:T(8,128)(2,1)S(1)}, u32[]{:S(2)}, u32[]{:S(2)}) collective-permute-start(bf16[128,128]{1,0:T(8,128)(2,1)S(1)} %get-tuple-element.17), channel_id=1, source_target_pairs={{0,0},{1,2},{2,4},{3,6},{4,8},{5,10},{6,12},{7,14},{8,1},{9,3},{10... | collective-permute-start | bytes 98312 | tf_op jit(solution)/shard_map/keys_values/ppermute | solution.py:312
  43.6 0.6 queries.1
  44.2 1.9 %collective-permute-start.6 = (bf16[256,128]{1,0:T(8,128)(2,1)S(1)}, bf16[256,128]{1,0:T(8,128)(2,1)S(1)}, u32[]{:S(2)}, u32[]{:S(2)}) collective-permute-start(bf16[256,128]{1,0:T(8,128)(2,1)S(1)} %pad_maximum_fusion.3), channel_id=1, source_target_pairs={{0,64},{64,0},{1,65},{65,1},{2,66},{66,2},{3,67},{67,3},{4,68},{68... | collective-permute-start | bytes 196616 | tf_op jit(solution)/shard_map/queries/ppermute | solution.py:324
  46.1 4.9 %collective-permute-done.5.kv_ref = bf16[128,128]{1,0:T(8,128)(2,1)S(1)} collective-permute-done((bf16[128,128]{1,0:T(8,128)(2,1)S(1)}, bf16[128,128]{1,0:T(8,128)(2,1)S(1)}, u32[]{:S(2)}, u32[]{:S(2)}) %collective-permute-start.5) | collective-permute-done | bytes 32800 | tf_op jit(solution)/shard_map/keys_values/ppermute | solution.py:312
  51.0 0.7 keys_values.3
  51.7 9.5 %all-to-all-start.1 = ((bf16[8,128,128]{2,1,0:T(8,128)(2,1)}), bf16[8,128,128]{2,1,0:T(8,128)(2,1)S(1)}, u32[]{:S(2)}, u32[]{:S(2)}) async-start(bf16[8,128,128]{2,1,0:T(8,128)(2,1)} %keys_values.3), calls=%async_computation.1 | async-start | bytes 524288 | tf_op jit(solution)/shard_map/spread_keys_values/all_to_all | solution.py:326
  61.3 1.9 %collective-permute-start.7 = (bf16[256,128]{1,0:T(8,128)(2,1)S(1)}, bf16[256,128]{1,0:T(8,128)(2,1)S(1)}, u32[]{:S(2)}, u32[]{:S(2)}) collective-permute-start(bf16[256,128]{1,0:T(8,128)(2,1)S(1)} %pad_maximum_fusion.4), channel_id=1, source_target_pairs={{0,1},{1,0},{2,3},{3,2},{4,5},{5,4},{6,7},{7,6},{8,9},{9,8},{10,11... | collective-permute-start | bytes 196616 | tf_op jit(solution)/shard_map/share_queries/ppermute | solution.py:329
  63.2 1.2 collective-permute-done.7
  64.5 11.0 %all_gather.3.query_ref = bf16[2048,128]{1,0:T(8,128)(2,1)S(1)} all-gather(bf16[512,128]{1,0:T(8,128)(2,1)S(1)} %pad_maximum_fusion), channel_id=1, replica_groups=mesh['zh'=8,'zp'=2,'x'=4,'y'=8,'c'=2] {'x'}, dimensions={0}, use_global_device_ids=true | all-gather | bytes 655360 | tf_op jit(solution)/shard_map/share_queries/all_gather | solution.py:331
  75.5 3.3 %all-to-all-done.1.own_ref = bf16[8,128,128]{2,1,0:T(8,128)(2,1)S(1)} async-done(((bf16[8,128,128]{2,1,0:T(8,128)(2,1)}), bf16[8,128,128]{2,1,0:T(8,128)(2,1)S(1)}, u32[]{:S(2)}, u32[]{:S(2)}) %all-to-all-start.1) | async-done | bytes 262176 | tf_op jit(solution)/shard_map/spread_keys_values/all_to_all | solution.py:326
  78.8 1.9 %collective-permute-start.8 = (bf16[8,128,128]{2,1,0:T(8,128)(2,1)S(1)}, bf16[8,128,128]{2,1,0:T(8,128)(2,1)S(1)}, u32[]{:S(2)}, u32[]{:S(2)}) collective-permute-start(bf16[8,128,128]{2,1,0:T(8,128)(2,1)S(1)} %all-to-all-done.1.own_ref), channel_id=1, source_target_pairs={{0,1},{1,0},{2,3},{3,2},{4,5},{5,4},{6,7},{7,6},{8,9},{9,8},{10,11... | collective-permute-start | bytes 786440 | tf_op jit(solution)/shard_map/share_queries/ppermute | solution.py:333
  80.8 1.4 %collective-permute-done.8.other_ref = bf16[8,128,128]{2,1,0:T(8,128)(2,1)S(1)} collective-permute-done((bf16[8,128,128]{2,1,0:T(8,128)(2,1)S(1)}, bf16[8,128,128]{2,1,0:T(8,128)(2,1)S(1)}, u32[]{:S(2)}, u32[]{:S(2)}) %collective-permute-start.8) | collective-permute-done | bytes 262176 | tf_op jit(solution)/shard_map/share_queries/ppermute | solution.py:333
  82.2 1.5 %attend.1 = bf16[8,144,256]{2,1,0:T(8,128)(2,1)S(1)} custom-call(s32[4]{0:T(128)S(1)} %pad_add_fusion.place_ref, bf16[2048,128]{1,0:T(8,128)(2,1)S(1)} %all_gather.3.query_ref, bf16[8,128,128]{2,1,0:T(8,128)(2,1)S(1)} %all-to-all-done.1.own_ref, bf16[8,128,128]{2,1,0:T(8,128)(2,1)S(1)} %collective-permute-done.8.other_ref), custom_call_target="tpu_custom_call" | custom-call | flops 1073741824 | bytes 2097152 | tf_op jit(solution)/shard_map/attend/pallas_call | solution.py:336
  83.7 14.3 %all_to_all.20.parts_ref = bf16[8,144,256]{2,1,0:T(8,128)(2,1)S(1)} all-to-all(bf16[8,144,256]{2,1,0:T(8,128)(2,1)S(1)} %attend.1), channel_id=1, replica_groups=mesh['zh'=8,'zp'=2,'x'=4,'y'=8,'c'=2] {'zp','x'}, dimensions={0} | all-to-all | bytes 1179648 | tf_op jit(solution)/shard_map/attend/all_to_all | solution.py:349
  98.0 2.3 %project.1 = bf16[16,64,256]{2,1,0:T(8,128)(2,1)S(1)} custom-call(bf16[8,144,256]{2,1,0:T(8,128)(2,1)S(1)} %all_to_all.20.parts_ref, bf16[256,4096]{1,0:T(8,128)(2,1)S(1)} %copy-done, bf16[64,4096]{1,0:T(8,128)(2,1)} %collective-permute-done.refs_0_, bf16[64,4096]{1,0:T(8,128)(2,1)} %collective-permute-done.1.refs_1_, ...), custom_call_target="tpu_custom_call" | custom-call | flops 268435456 | bytes 5242880 | tf_op jit(solution)/shard_map/project/pallas_call | solution.py:351
  100.3 24.0 %all_to_all.21.parts_ref = bf16[16,64,256]{2,1,0:T(8,128)(2,1)S(1)} all-to-all(bf16[16,64,256]{2,1,0:T(8,128)(2,1)S(1)} %project.1), channel_id=1, replica_groups=mesh['zh'=8,'zp'=2,'x'=4,'y'=8,'c'=2] {'y','c'}, dimensions={0} | all-to-all | bytes 1048576 | tf_op jit(solution)/shard_map/project/all_to_all | solution.py:364
  124.3 1.0 mix.1
  (32 shorter events, 0.3 us)
Async XLA Ops:
  2.0 34.9 %all-to-all-start = ((bf16[16,64,256]{2,1,0:T(8,128)(2,1)}), bf16[16,64,256]{2,1,0:T(8,128)(2,1)S(1)}, u32[]{:S(2)}, u32[]{:S(2)}) async-start(bf16[16,64,256]{2,1,0:T(8,128)(2,1)} %pick.1.after_ref), calls=%async_computation | async-start | bytes 1048576 | tf_op jit(solution)/shard_map/gather_features/all_to_all | solution.py:280
  19.5 11.7 %copy-start.7 = (f32[4096]{0:T(1024)S(1)}, f32[4096]{0:T(1024)}, u32[]{:S(2)}) copy-start(f32[4096]{0:T(1024)} %param.11) | copy-start | bytes 49156
  19.5 11.7 %copy-start.1 = (bf16[16,64,256]{2,1,0:T(8,128)(2,1)S(1)}, bf16[16,64,256]{2,1,0:T(8,128)(2,1)}, u32[]{:S(2)}) copy-start(bf16[16,64,256]{2,1,0:T(8,128)(2,1)} %pick.1.after_ref) | copy-start | bytes 1572868
  19.5 11.7 %copy-start.2 = (bf16[4096,128]{1,0:T(8,128)(2,1)S(1)}, bf16[4096,128]{1,0:T(8,128)(2,1)}, u32[]{:S(2)}) copy-start(bf16[4096,128]{1,0:T(8,128)(2,1)} %weight_ref.4) | copy-start | bytes 3145732
  19.6 11.8 %copy-start.5 = (s32[128]{0:T(128)S(1)}, s32[128]{0:T(128)}, u32[]{:S(2)}) copy-start(s32[128]{0:T(128)} %param.15) | copy-start | bytes 1540
  22.6 9.2 %collective-permute-start.3 = (bf16[64,4096]{1,0:T(8,128)(2,1)}, bf16[64,4096]{1,0:T(8,128)(2,1)S(1)}, u32[]{:S(2)}, u32[]{:S(2)}) collective-permute-start(bf16[64,4096]{1,0:T(8,128)(2,1)} %get-tuple-element.29), channel_id=1, source_target_pairs={{0,1},{1,0},{2,3},{3,2},{4,5},{5,4},{6,7},{7,6},{8,9},{9,8},{10,11... | collective-permute-start | bytes 1572872 | tf_op jit(solution)/shard_map/gather_features/ppermute | solution.py:283
  24.7 7.1 %collective-permute-start.2 = (bf16[64,4096]{1,0:T(8,128)(2,1)}, bf16[64,4096]{1,0:T(8,128)(2,1)S(1)}, u32[]{:S(2)}, u32[]{:S(2)}) collective-permute-start(bf16[64,4096]{1,0:T(8,128)(2,1)} %get-tuple-element.30), channel_id=1, source_target_pairs={{0,1},{1,0},{2,3},{3,2},{4,5},{5,4},{6,7},{7,6},{8,9},{9,8},{10,11... | collective-permute-start | bytes 1572872 | tf_op jit(solution)/shard_map/gather_features/ppermute | solution.py:283
  26.9 4.9 %collective-permute-start.1 = (bf16[64,4096]{1,0:T(8,128)(2,1)}, bf16[64,4096]{1,0:T(8,128)(2,1)}, u32[]{:S(2)}, u32[]{:S(2)}) collective-permute-start(bf16[64,4096]{1,0:T(8,128)(2,1)} %get-tuple-element.31), channel_id=1, source_target_pairs={{0,1},{1,0},{2,3},{3,2},{4,5},{5,4},{6,7},{7,6},{8,9},{9,8},{10,11... | collective-permute-start | bytes 1572872 | tf_op jit(solution)/shard_map/gather_features/ppermute | solution.py:283
  29.0 4.1 %collective-permute-start = (bf16[64,4096]{1,0:T(8,128)(2,1)}, bf16[64,4096]{1,0:T(8,128)(2,1)}, u32[]{:S(2)}, u32[]{:S(2)}) collective-permute-start(bf16[64,4096]{1,0:T(8,128)(2,1)} %get-tuple-element.32), channel_id=1, source_target_pairs={{0,1},{1,0},{2,3},{3,2},{4,5},{5,4},{6,7},{7,6},{8,9},{9,8},{10,11... | collective-permute-start | bytes 1572872 | tf_op jit(solution)/shard_map/gather_features/ppermute | solution.py:283
  36.9 6.7 %copy-start.3 = (bf16[4096,256]{1,0:T(8,128)(2,1)S(1)}, bf16[4096,256]{1,0:T(8,128)(2,1)}, u32[]{:S(2)}) copy-start(bf16[4096,256]{1,0:T(8,128)(2,1)} %weight_ref.5) | copy-start | bytes 6291460
  36.9 3.9 %collective-permute-start.4 = (bf16[16,64,256]{2,1,0:T(8,128)(2,1)S(1)}, bf16[16,64,256]{2,1,0:T(8,128)(2,1)S(1)}, u32[]{:S(2)}, u32[]{:S(2)}) collective-permute-start(bf16[16,64,256]{2,1,0:T(8,128)(2,1)S(1)} %all-to-all-done.own_ref), channel_id=1, source_target_pairs={{0,1},{1,0},{2,3},{3,2},{4,5},{5,4},{6,7},{7,6},{8,9},{9,8},{10,11... | collective-permute-start | bytes 1572872 | tf_op jit(solution)/shard_map/gather_features/ppermute | solution.py:286
  41.7 9.3 %collective-permute-start.5 = (bf16[128,128]{1,0:T(8,128)(2,1)S(1)}, bf16[128,128]{1,0:T(8,128)(2,1)S(1)}, u32[]{:S(2)}, u32[]{:S(2)}) collective-permute-start(bf16[128,128]{1,0:T(8,128)(2,1)S(1)} %get-tuple-element.17), channel_id=1, source_target_pairs={{0,0},{1,2},{2,4},{3,6},{4,8},{5,10},{6,12},{7,14},{8,1},{9,3},{10... | collective-permute-start | bytes 98312 | tf_op jit(solution)/shard_map/keys_values/ppermute | solution.py:312
  44.2 17.1 %collective-permute-start.6 = (bf16[256,128]{1,0:T(8,128)(2,1)S(1)}, bf16[256,128]{1,0:T(8,128)(2,1)S(1)}, u32[]{:S(2)}, u32[]{:S(2)}) collective-permute-start(bf16[256,128]{1,0:T(8,128)(2,1)S(1)} %pad_maximum_fusion.3), channel_id=1, source_target_pairs={{0,64},{64,0},{1,65},{65,1},{2,66},{66,2},{3,67},{67,3},{4,68},{68... | collective-permute-start | bytes 196616 | tf_op jit(solution)/shard_map/queries/ppermute | solution.py:324
  51.7 27.0 %all-to-all-start.1 = ((bf16[8,128,128]{2,1,0:T(8,128)(2,1)}), bf16[8,128,128]{2,1,0:T(8,128)(2,1)S(1)}, u32[]{:S(2)}, u32[]{:S(2)}) async-start(bf16[8,128,128]{2,1,0:T(8,128)(2,1)} %keys_values.3), calls=%async_computation.1 | async-start | bytes 524288 | tf_op jit(solution)/shard_map/spread_keys_values/all_to_all | solution.py:326
  61.3 3.1 %collective-permute-start.7 = (bf16[256,128]{1,0:T(8,128)(2,1)S(1)}, bf16[256,128]{1,0:T(8,128)(2,1)S(1)}, u32[]{:S(2)}, u32[]{:S(2)}) collective-permute-start(bf16[256,128]{1,0:T(8,128)(2,1)S(1)} %pad_maximum_fusion.4), channel_id=1, source_target_pairs={{0,1},{1,0},{2,3},{3,2},{4,5},{5,4},{6,7},{7,6},{8,9},{9,8},{10,11... | collective-permute-start | bytes 196616 | tf_op jit(solution)/shard_map/share_queries/ppermute | solution.py:329
  78.8 3.4 %collective-permute-start.8 = (bf16[8,128,128]{2,1,0:T(8,128)(2,1)S(1)}, bf16[8,128,128]{2,1,0:T(8,128)(2,1)S(1)}, u32[]{:S(2)}, u32[]{:S(2)}) collective-permute-start(bf16[8,128,128]{2,1,0:T(8,128)(2,1)S(1)} %all-to-all-done.1.own_ref), channel_id=1, source_target_pairs={{0,1},{1,0},{2,3},{3,2},{4,5},{5,4},{6,7},{7,6},{8,9},{9,8},{10,11... | collective-permute-start | bytes 786440 | tf_op jit(solution)/shard_map/share_queries/ppermute | solution.py:333
  80.8 17.2 %copy-start = (bf16[256,4096]{1,0:T(8,128)(2,1)S(1)}, bf16[256,4096]{1,0:T(8,128)(2,1)}, u32[]{:S(2)}) copy-start(bf16[256,4096]{1,0:T(8,128)(2,1)} %own_ref.1) | copy-start | bytes 6291460
  98.0 26.3 %copy-start.4 = (bf16[512,256]{1,0:T(8,128)(2,1)S(1)}, bf16[512,256]{1,0:T(8,128)(2,1)}, u32[]{:S(2)}) copy-start(bf16[512,256]{1,0:T(8,128)(2,1)} %hidden_ref.3) | copy-start | bytes 786436
  98.0 26.3 %copy-start.6 = (f32[512]{0:T(512)S(1)}, f32[512]{0:T(512)}, u32[]{:S(2)}) copy-start(f32[512]{0:T(512)} %param.10) | copy-start | bytes 6148
